TPU v7x, 32 devices: a whole 2x2x4 slice. The times are simulated.
32 devices in a mesh: cube: 32 (over z, y, x, core).
Axes of the slice: x: 2, y: 2, z: 4, core: 2. Of those that a mesh axis runs over, the one named last changes fastest.
Arguments:
- vectors: bfloat16 [131072, 768], P('cube'), may hold values from -40 to 40
- child_labels: int32 [2, 131072], P(None, 'cube'), may hold values from 0 to 1, as said below
Outputs:
- held: bfloat16 [229376, 768], P('cube')
- margin_one: float32 [196608], P('cube')
- margin_two: float32 [229376], P('cube')
- centroids: float32 [6, 768], replicated
Inputs may be any that keep to these rules, and one draw needn't show every extreme that they name: `child_labels`: per device, the vectors leaving at the first level number from 1024 to 2048, and 2048 on some device in every draw. `child_labels`: per device, the second-level leavers among its vectors that stay at the first level number at most 512, and among the vectors it sends away at the first level at most 512; in every draw some device holds 512 second-level leavers of each kind (its own stayers and those received at the first level), so its second-level send buffer is full.
All inputs are finite; a program needn't handle non-finite values.
Results may differ from a plain program's by a relative error of at most 0.0011.
Values may be sent and summed in bfloat16 or wider, within the bound.
No kernel may reach another device: no remote copies, remote signals or barrier semaphores. Data moves between devices by JAX's collectives and lax.ppermute only.
A program may use at most 128 MiB of HBM per device.

v0:
```python
import functools
import jax
import jax.numpy as jnp
from jax import lax
from jax.experimental import pallas as pl
from jax.experimental.pallas import tpu as pltpu
from jax.sharding import PartitionSpec as P

BF = jnp.bfloat16
F32 = jnp.float32
I32 = jnp.int32
BLK = 256
HANDS = 8
WIDE = BLK // 2 + 16
SLOTS = 128
VMEM_BYTES = 28 * 1024 * 1024


def swap(x, bits):
    return lax.ppermute(x, "cube", [(i, i ^ bits) for i in range(lax.axis_size("cube"))])


def dot(a, b):
    return lax.dot_general(a, b, (((1,), (0,)), ((), ())), preferred_element_type=F32)


def dot_t(a, b):
    return lax.dot_general(a, b, (((1,), (1,)), ((), ())), preferred_element_type=F32)


def iota(shape, dim):
    return lax.broadcasted_iota(I32, shape, dim)


def as_bf(mask):
    return jnp.where(mask, jnp.float32(1), jnp.float32(0)).astype(BF)


def pack(sums, counts, width):
    high = sums.astype(BF).astype(F32)
    middle = (sums - high).astype(BF).astype(F32)
    low = sums - high - middle
    spare = width - 128 * len(counts)
    counts = jnp.concatenate(counts + ([jnp.zeros((1, spare), I32)] if spare else []), axis=1)
    upper, lower = (counts >> 8).astype(F32), (counts & 255).astype(F32)
    return jnp.concatenate([high, middle, low, upper, lower, jnp.zeros((2, width), F32)], axis=0).astype(BF)


def unpack(extra):
    extra = extra.astype(F32)
    sums = extra[0:4] + extra[4:8] + extra[8:12]
    return sums, extra[12:13] * 256.0 + extra[13:14]


def count_at(extra, k):
    extra = extra[12:14, 128 * k : 128 * k + 1].astype(F32)
    return (extra[0:1] * 256.0 + extra[1:2]).astype(I32)


def spec(memory):
    return pl.BlockSpec(memory_space=memory)


def params():
    return pltpu.CompilerParams(vmem_limit_bytes=VMEM_BYTES)


def plan_kernel(here, labels, pos, off_ref, every, leavers):
    rows = labels.shape[1]
    blocks = rows // BLK
    leave = labels[0:1, :] != here[0]
    miss = labels[1:2, :] != here[1]
    code = jnp.where(leave, jnp.where(miss, 0, 1), jnp.where(miss, 2, 3))
    code = jnp.concatenate(
        [jnp.broadcast_to(code[:, b * BLK : (b + 1) * BLK], (8, BLK)) for b in range(blocks)], axis=0
    )
    tall = 8 * blocks
    kind = iota((tall, BLK), 0) & 7
    mask = (code == kind) | ((kind == 4) & (code <= 1))
    maskb = as_bf(mask)
    upper = as_bf(iota((BLK, BLK), 0) <= iota((BLK, BLK), 1))
    before = dot(maskb, upper)
    total = dot(maskb, jnp.ones((BLK, BLK), BF)).astype(BF)
    r, c = iota((tall, tall), 0), iota((tall, tall), 1)
    same = ((r ^ c) & 7) == 0
    earlier = as_bf((same & (c < r)) | (((r & 7) == 1) & ((c & 7) == 0)))
    off = dot(earlier, total)
    pos[...] = jnp.where(mask, (before + off).astype(I32) - 1, -1)
    off_ref[...] = (off + jnp.where(iota((tall, BLK), 1) < 64, 0.0, total.astype(F32)))[:, :128].astype(I32)
    r8, c8 = iota((8, tall), 0), iota((8, tall), 1)
    count = dot(as_bf(r8 == (c8 & 7)), total)[:, :128].astype(I32)
    every[...] = count
    leavers[...] = jnp.broadcast_to(count[4:5], leavers.shape)


def plan_call(here, labels):
    rows = labels.shape[1]
    tall = 8 * rows // BLK
    return pl.pallas_call(
        plan_kernel,
        out_shape=[
            jax.ShapeDtypeStruct((tall, BLK), I32),
            jax.ShapeDtypeStruct((tall, 128), I32),
            jax.ShapeDtypeStruct((8, 128), I32),
            jax.ShapeDtypeStruct((8, 128), I32),
        ],
        in_specs=[spec(pltpu.SMEM), spec(pltpu.VMEM)],
        out_specs=[spec(pltpu.VMEM)] * 4,
        compiler_params=params(),
        cost_estimate=pl.CostEstimate(flops=2 * 10**10, bytes_accessed=10**7, transcendentals=0),
        name="plan_places",
    )(here, labels)


def sort_kernel(here, labels, pos_ref, off_ref, every, x, first, middle, rest, buf, sums):
    rows = labels.shape[1]
    blocks = rows // BLK
    cap = rows // 2
    buf[...] = jnp.zeros_like(buf)
    group = 2 * labels[0:1, :] + labels[1:2, :]
    slot = iota((WIDE, BLK), 0)
    more_slot = iota((BLK + 16 - WIDE, BLK), 0) + WIDE
    sums[...] = jnp.zeros_like(sums)
    tails = []
    for b in range(blocks):
        vectors = x.at[pl.ds(b * BLK, BLK)]
        hot = [as_bf((iota((16, BLK), 0) & 3) == group[:, b * BLK : (b + 1) * BLK])]
        bases = []
        ends = []
        places = []
        for kind in (0, 1):
            line = slice(8 * b + kind, 8 * b + kind + 1)
            base = pl.multiple_of(jnp.minimum((off_ref[line, 0:1][0, 0] // 16) * 16, cap), 16)
            bases.append(base)
            ends.append(off_ref[line, 64:65][0, 0])
            places.append(pos_ref[line, :] - base)
            hot.append(as_bf(slot == places[kind]))
        got = dot(jnp.concatenate(hot, axis=0), vectors[...])
        sums[...] += got[0:8]
        got = got[16:].astype(BF)
        buf[pl.ds(bases[0], WIDE), :] += got[:WIDE]
        buf[pl.ds(bases[1], 16), :] += got[WIDE : WIDE + 16]
        buf[pl.ds(bases[1] + 16, WIDE - 16), :] = got[WIDE + 16 :]
        for kind in (0, 1):
            tails.append((b, places[kind], bases[kind], ends[kind] - bases[kind]))

    @pl.when(functools.reduce(jnp.maximum, [size for *_, size in tails]) > WIDE)
    def _():
        for b, place, base, size in tails:

            @pl.when(size > WIDE)
            def _():
                more = dot(as_bf(more_slot == place), x[b * BLK : (b + 1) * BLK, :]).astype(BF)
                buf[pl.ds(base + WIDE, BLK + 16 - WIDE), :] += more

    one, two = here[0], here[1]
    kinds = [every[k : k + 1] for k in range(4)]
    counts = []
    for g in range(4):
        away, miss = jnp.int32(g >> 1) != one, jnp.int32(g & 1) != two
        counts.append(jnp.where(away, jnp.where(miss, kinds[0], kinds[1]), jnp.where(miss, kinds[2], kinds[3])))
    part = cap // 4
    first[0:part, :] = buf[0:part, :]
    first[part:, :] = pack(sums[0:4, :], counts + [kinds[0], kinds[2]], x.shape[1])
    middle[...] = buf[part : 2 * part, :]
    rest[...] = buf[2 * part : cap, :]


def sort_call(here, labels, pos, off, every, vectors):
    rows, width = vectors.shape
    part = rows // 8
    return pl.pallas_call(
        sort_kernel,
        out_shape=[
            jax.ShapeDtypeStruct((part + 16, width), BF),
            jax.ShapeDtypeStruct((part, width), BF),
            jax.ShapeDtypeStruct((2 * part, width), BF),
        ],
        in_specs=[spec(pltpu.SMEM)] + [spec(pltpu.VMEM)] * 5,
        out_specs=[spec(pltpu.VMEM)] * 3,
        scratch_shapes=[pltpu.VMEM((rows // 2 + BLK + 16, width), BF), pltpu.VMEM((8, width), F32)],
        compiler_params=params(),
        cost_estimate=pl.CostEstimate(flops=8 * 10**9, bytes_accessed=10 * 10**6, transcendentals=0),
        name="sort_leavers",
    )(here, labels, pos, off, every, vectors)


def deal_kernel(rest, own, near, top, far, *hands):
    rows, width = rest.shape
    turns = rows // 16 // HANDS
    counts = jnp.concatenate([ref[0:1, :] for ref in (own, near, top, far)], axis=1)
    counts = jnp.concatenate([counts, jnp.zeros((1, width - 512), I32)], axis=1)
    upper, lower = (counts >> 8).astype(F32), (counts & 255).astype(F32)
    tail = jnp.concatenate([upper, lower, jnp.zeros((14, width), F32)], axis=0).astype(BF)
    for h, hand in enumerate(hands):
        for turn in range(turns):
            block = 16 * (h + HANDS * turn)
            hand[16 * turn : 16 * turn + 16, :] = rest[block : block + 16, :]
        hand[16 * turns :, :] = tail


def deal_call(rest, *counts):
    rows, width = rest.shape
    turns = rows // 16 // HANDS
    return pl.pallas_call(
        deal_kernel,
        out_shape=[jax.ShapeDtypeStruct((16 * turns + 16, width), BF)] * HANDS,
        in_specs=[spec(pltpu.VMEM)] * 5,
        out_specs=[spec(pltpu.VMEM)] * HANDS,
        compiler_params=params(),
        cost_estimate=pl.CostEstimate(flops=0, bytes_accessed=10**5, transcendentals=0),
        name="deal_rest",
    )(rest, *counts)


def pack_kernel(step, *refs):
    hands, (out, longest, begins) = refs[:HANDS], refs[HANDS:]
    rows = hands[0].shape[0] - 16
    out[...] = jnp.zeros_like(out)
    full = []
    for hand in hands:
        count = hand[rows : rows + 2, 0:512].astype(F32)
        count = (count[0:1] * 256.0 + count[1:2]).astype(I32)
        full.append((jnp.maximum(count - rows * HANDS, 0) + 15) >> 4)
    place = jnp.zeros((1, 512), I32)
    for h, hand in enumerate(hands):
        base = pl.multiple_of(place[0, 0] * 16, 16)
        out[pl.ds(base, rows), :] = hand[0:rows, :]
        begins[h : h + 1, :] = place[:, 256:384] * 16
        place = jnp.minimum(place + ((full[h] + (HANDS - 1 - h)) >> 3), (h + 1) * (rows // 16))
    most = jnp.zeros((1, 512), I32)
    for other in range(HANDS):
        size = jnp.zeros((1, 512), I32)
        for h in range(HANDS):
            size = size + ((full[other ^ h] + (HANDS - 1 - h)) >> 3)
        most = jnp.maximum(most, size)
    most = jnp.max(most.astype(F32), axis=1, keepdims=True).astype(I32)
    per = step // 16
    longest[...] = jnp.broadcast_to(jnp.minimum(most + per - 1, out.shape[0] // 16) // per, longest.shape)


def pack_call(step, hands):
    rows, width = hands[0].shape
    rows -= 16
    return pl.pallas_call(
        functools.partial(pack_kernel, step),
        out_shape=[
            jax.ShapeDtypeStruct((rows * HANDS, width), BF),
            jax.ShapeDtypeStruct((8, 128), I32),
            jax.ShapeDtypeStruct((8, 128), I32),
        ],
        in_specs=[spec(pltpu.VMEM)] * HANDS,
        out_specs=[spec(pltpu.VMEM)] * 3,
        compiler_params=params(),
        cost_estimate=pl.CostEstimate(flops=0, bytes_accessed=10**5, transcendentals=0),
        name="pack_hands",
    )(*hands)


def part_kernel(begins, pack_in, *refs):
    hands, sem = refs[:HANDS], refs[HANDS]
    rows = hands[0].shape[0]
    copies = []
    for h, hand in enumerate(hands):
        base = pl.multiple_of((begins[h, 0] // 16) * 16, 16)
        copies.append(pltpu.make_async_copy(pack_in.at[pl.ds(base, rows)], hand, sem.at[h]))
    for copy in copies:
        copy.start()
    for copy in copies:
        copy.wait()


def part_call(begins, pack_in):
    rows, width = pack_in.shape
    return pl.pallas_call(
        part_kernel,
        out_shape=[jax.ShapeDtypeStruct((rows // HANDS, width), BF)] * HANDS,
        in_specs=[spec(pltpu.SMEM), spec(pl.ANY)],
        out_specs=[spec(pl.ANY)] * HANDS,
        scratch_shapes=[pltpu.SemaphoreType.DMA((HANDS,))],
        compiler_params=params(),
        cost_estimate=pl.CostEstimate(flops=0, bytes_accessed=3 * 10**6, transcendentals=0),
        name="part_pack",
    )(begins, pack_in)


def second_send_kernel(off, pos, first, x, second, buf):
    half = second.shape[0] - 16
    buf[...] = jnp.zeros_like(buf)
    slot = iota((WIDE, BLK), 0)
    more_slot = iota((BLK + 16 - WIDE, BLK), 0) + WIDE
    tails = []
    for b in range(x.shape[0] // BLK):
        line = slice(8 * b + 2, 8 * b + 3)
        base = pl.multiple_of(jnp.minimum((off[line, 0:1][0, 0] // 16) * 16, half), 16)
        place = pos[line, :] - base
        got = dot(as_bf(slot == place), x[b * BLK : (b + 1) * BLK, :]).astype(BF)
        buf[pl.ds(base, 16), :] += got[:16]
        buf[pl.ds(base + 16, WIDE - 16), :] = got[16:]
        tails.append((b, place, base, off[line, 64:65][0, 0] - base))

    @pl.when(functools.reduce(jnp.maximum, [size for *_, size in tails]) > WIDE)
    def _():
        for b, place, base, size in tails:

            @pl.when(size > WIDE)
            def _():
                more = dot(as_bf(more_slot == place), x[b * BLK : (b + 1) * BLK, :]).astype(BF)
                buf[pl.ds(base + WIDE, BLK + 16 - WIDE), :] += more

    second[0:half, :] = buf[0:half, :]
    second[half:, :] = first[half:, :]


def second_send_call(off, pos, first, x):
    rows, width = x.shape
    half = rows // 8
    return pl.pallas_call(
        second_send_kernel,
        out_shape=jax.ShapeDtypeStruct((half + 16, width), BF),
        in_specs=[spec(pltpu.VMEM)] * 4,
        out_specs=spec(pltpu.VMEM),
        scratch_shapes=[pltpu.VMEM((half + BLK + 16, width), BF)],
        compiler_params=params(),
        cost_estimate=pl.CostEstimate(flops=10**8, bytes_accessed=10**6, transcendentals=0),
        name="second_send",
    )(off, pos, first, x)


def rank_kernel(off, pos, meta, ranks):
    ranks[...] = jnp.zeros_like(ranks)
    cap = 8 * meta.shape[1]
    line = iota((16, BLK), 0)
    slot = iota((BLK + 128, BLK), 0)
    for b in range(pos.shape[0] // 8):
        rank = pos[8 * b + 4 : 8 * b + 5, :]
        value = jnp.where(line == 0, rank >> 8, jnp.where(line == 1, rank & 255, 1))
        value = jnp.where(rank >= 0, value, 0).astype(F32).astype(BF)
        for kind in (0, 1):
            row = slice(8 * b + kind, 8 * b + kind + 1)
            base = pl.multiple_of(jnp.minimum((off[row, 0:1][0, 0] // 128) * 128, cap), 128)
            ranks[:, pl.ds(base, BLK + 128)] += dot_t(value, as_bf(slot == pos[row, :] - base))[:8]
    seen = ranks[2:3, :cap] > 0.5
    rank = (ranks[0:1, :cap] * 256.0 + ranks[1:2, :cap]).astype(I32)
    goal = jnp.where(seen, rank, 1 << 20)
    line = cap // 8
    for k in range(8):
        meta[k : k + 1, :] = goal[:, k * line : (k + 1) * line]


def rank_call(off, pos):
    cap = pos.shape[0] // 8 * BLK // 2
    return pl.pallas_call(
        rank_kernel,
        out_shape=jax.ShapeDtypeStruct((8, cap // 8), I32),
        in_specs=[spec(pltpu.VMEM)] * 2,
        out_specs=spec(pltpu.VMEM),
        scratch_shapes=[pltpu.VMEM((8, cap + BLK + 128), F32)],
        compiler_params=params(),
        cost_estimate=pl.CostEstimate(flops=10**8, bytes_accessed=10**6, transcendentals=0),
        name="list_ranks",
    )(off, pos)


def own_kernel(pos, x, held):
    same = iota((BLK, BLK), 0) == iota((BLK, BLK), 1)
    start = pl.program_id(0) * held.shape[0]
    for sub in range(held.shape[0] // BLK):
        keep = as_bf(same & (pos[8 * sub + 3 : 8 * sub + 4, :] >= 0))
        held[sub * BLK : (sub + 1) * BLK, :] = dot(keep, x[pl.ds(start + sub * BLK, BLK), :]).astype(BF)


def own_call(pos, x):
    rows, width = x.shape
    return pl.pallas_call(
        own_kernel,
        grid=(rows // 1024,),
        out_shape=jax.ShapeDtypeStruct((rows + rows // 2 + rows // 4, width), BF),
        in_specs=[pl.BlockSpec((8 * 1024 // BLK, BLK), lambda b: (b, 0)), spec(pltpu.VMEM)],
        out_specs=pl.BlockSpec((1024, width), lambda b: (b, 0)),
        compiler_params=params(),
        cost_estimate=pl.CostEstimate(flops=10**8, bytes_accessed=10**6, transcendentals=0),
        name="own_slots",
    )(pos, x)


def scores(x, turned):
    score = dot(x, turned)
    lane = iota(score.shape, 1)
    high = score.astype(BF).astype(F32)
    middle = (score - high).astype(BF).astype(F32)
    terms = jnp.where(lane < 4, high, jnp.where(lane < 8, middle, score - high - middle)).astype(BF)
    lane = iota((16, 128), 1)
    return dot_t(as_bf(((lane & 3) == iota((16, 128), 0)) & (lane < 12)), terms)


def margins(score, shift, first, width):
    return (score[first + 1 : first + 2] - score[first : first + 1] - shift) / width


def put_lines(ref, start, values):
    for k in range(values.shape[1] // 128):
        ref[start + k : start + k + 1, :] = values[:, 128 * k : 128 * (k + 1)]


def centre_kernel(here, total, labels, x_ref, cents, turned, shifts, one, two):
    width = x_ref.shape[1]
    lines = labels.shape[1]

    @pl.when(pl.program_id(0) == 0)
    def _():
        sums, counts = total[0:4, :], total[4:8, :]
        low = (sums[0:1] + sums[1:2]) / (counts[0:1] + counts[1:2])
        high = (sums[2:3] + sums[3:4]) / (counts[2:3] + counts[3:4])
        groups = sums / counts
        cents[0:1, :] = low
        cents[1:2, :] = high
        cents[2:6, :] = groups
        top = here[0] == 1
        left = jnp.where(top, groups[2:3], groups[0:1])
        right = jnp.where(top, groups[3:4], groups[1:2])
        rows = jnp.concatenate([low, high, left, right] * 3 + [jnp.zeros((116, width), F32)], axis=0)
        turned[...] = rows.T.astype(BF)
        for k, (a, b) in enumerate(((low, high), (left, right))):
            shift = 0.5 * (jnp.sum(b * b, axis=1, keepdims=True) - jnp.sum(a * a, axis=1, keepdims=True))
            shifts[k : k + 1, :] = jnp.broadcast_to(shift, (1, 128))

    score = scores(x_ref[pl.ds(pl.program_id(0) * lines, lines), :], turned[...])
    stay = labels[0:1, :] == here[0]
    keep = stay & (labels[1:2, :] == here[1])
    put_lines(one, 0, jnp.where(stay, margins(score, shifts[0:1, 0:1], 0, width), 0.0))
    put_lines(two, 0, jnp.where(keep, margins(score, shifts[1:2, 0:1], 2, width), 0.0))


def centre_call(here, total, labels, vectors):
    rows, width = vectors.shape
    cap = rows // 2
    return pl.pallas_call(
        centre_kernel,
        grid=(rows // 1024,),
        out_shape=[
            jax.ShapeDtypeStruct((6, width), F32),
            jax.ShapeDtypeStruct((width, 128), BF),
            jax.ShapeDtypeStruct((8, 128), F32),
            jax.ShapeDtypeStruct(((rows + cap) // 128, 128), F32),
            jax.ShapeDtypeStruct(((rows + cap + cap // 2) // 128, 128), F32),
        ],
        in_specs=[
            spec(pltpu.SMEM),
            pl.BlockSpec((8, width), lambda b: (0, 0)),
            pl.BlockSpec((2, 1024), lambda b: (0, b)),
            spec(pltpu.VMEM),
        ],
        out_specs=[
            pl.BlockSpec((6, width), lambda b: (0, 0)),
            pl.BlockSpec((width, 128), lambda b: (0, 0)),
            pl.BlockSpec((8, 128), lambda b: (0, 0)),
            pl.BlockSpec((8, 128), lambda b: (b, 0)),
            pl.BlockSpec((8, 128), lambda b: (b, 0)),
        ],
        compiler_params=params(),
        cost_estimate=pl.CostEstimate(flops=10**8, bytes_accessed=10**5, transcendentals=0),
        name="own_margins",
    )(here, total, labels, vectors)


def second_kernel(turned, shifts, second, relay, first, meta, leavers, held_in, two_in, held, two, again, alone, start, goals):
    del held_in, two_in
    half = second.shape[0] - 16
    slots = held.shape[0]
    cap = 2 * slots
    have = count_at(second[half:, :], 5)
    more = count_at(relay[half:, :], 4)
    both = count_at(first[half:, :], 4)
    lane = iota((1, half), 1)
    goal = jnp.where(lane < more, lane + have, -1)
    moved = dot(as_bf(iota((slots, half), 0) == goal), relay[0:half, :]).astype(BF)
    held[0:half, :] = moved[0:half] + second[0:half, :]
    held[half:, :] = moved[half:]
    score = scores(held[...], turned[...])
    width = held.shape[1]
    live = iota((1, slots), 1) < have + more
    put_lines(two, 0, jnp.where(live, margins(score, shifts[1:2, 0:1], 2, width), 0.0))

    score = scores(first[0:half, :], turned[...])
    value = jnp.where(lane < both, margins(score, shifts[0:1, 0:1], 0, width), 0.0)
    high = value.astype(BF).astype(F32)
    middle = (value - high).astype(BF).astype(F32)
    low = value - high - middle
    value = jnp.concatenate([high, middle, low, jnp.ones((1, half), F32), jnp.zeros((12, half), F32)], axis=0).astype(BF)
    place = jnp.concatenate([meta[k : k + 1, :] for k in range(8)], axis=1)
    goal = jnp.where(lane < both, place[:, :half], -1)
    for k in range(cap // BLK):
        hot = as_bf(iota((BLK, half), 0) + k * BLK == goal)
        got = dot_t(value, hot)
        put_lines(again, k * BLK // 128, got[0:1] + got[1:2] + got[2:3])
        free = (iota((1, BLK), 1) + k * BLK < leavers[0:1, 0:1]) & (got[3:4] < 0.5)
        put_lines(alone, k * BLK // 128, jnp.where(free, 1.0, 0.0))
    lines = cap // SLOTS
    lane = iota((lines, cap), 1)
    earlier = (lane < both) | (place < SLOTS * iota((lines, cap), 0))
    begin = jnp.sum(jnp.where(earlier, 1.0, 0.0), axis=1, keepdims=True).astype(I32)
    begin = jnp.minimum((begin >> 7) << 7, cap - SLOTS - 128)
    start[...] = jnp.broadcast_to(begin, start.shape)
    goals[...] = jnp.broadcast_to(jnp.where(iota((1, cap), 1) < both, -1, place), goals.shape)


def second_call(turned, shifts, second, relay, first, meta, leavers, held, two):
    half, width = second.shape
    half -= 16
    cap = 4 * half
    slots = cap // 2
    return pl.pallas_call(
        second_kernel,
        grid=(1,),
        out_shape=[
            jax.ShapeDtypeStruct(held.shape, BF),
            jax.ShapeDtypeStruct(two.shape, F32),
            jax.ShapeDtypeStruct((cap // 128, 128), F32),
            jax.ShapeDtypeStruct((cap // 128, 128), F32),
            jax.ShapeDtypeStruct((cap // SLOTS, 128), I32),
            jax.ShapeDtypeStruct((8, cap), I32),
        ],
        in_specs=[spec(pltpu.VMEM)] * 7 + [spec(pl.ANY)] * 2,
        out_specs=[
            pl.BlockSpec((slots, width), lambda b: (held.shape[0] // slots - 1, 0)),
            pl.BlockSpec((slots // 128, 128), lambda b: (held.shape[0] // slots - 1, 0)),
            pl.BlockSpec((cap // 128, 128), lambda b: (0, 0)),
            pl.BlockSpec((cap // 128, 128), lambda b: (0, 0)),
            pl.BlockSpec((cap // SLOTS, 128), lambda b: (0, 0)),
            pl.BlockSpec((8, cap), lambda b: (0, 0)),
        ],
        input_output_aliases={7: 0, 8: 1},
        compiler_params=params(),
        cost_estimate=pl.CostEstimate(flops=10**8, bytes_accessed=10**5, transcendentals=0),
        name="second_slots",
    )(turned, shifts, second, relay, first, meta, leavers, held, two)


def column_kernel(own, a, b, c, out):
    sums, counts = unpack(own[...])
    for other in (a, b, c):
        s, n = unpack(other[...])
        sums, counts = sums + s, counts + n
    out[0:4, :] = sums
    width = out.shape[1]
    for g in range(4):
        out[4 + g : 5 + g, :] = jnp.broadcast_to(counts[:, 128 * g : 128 * g + 1], (1, width))


def column_call(*pieces):
    width = pieces[0].shape[1]
    return pl.pallas_call(
        column_kernel,
        grid=(1,),
        out_shape=jax.ShapeDtypeStruct((8, width), F32),
        in_specs=[pl.BlockSpec((16, width), functools.partial(lambda last, b: (last, 0), p.shape[0] // 16 - 1)) for p in pieces],
        out_specs=pl.BlockSpec((8, width), lambda b: (0, 0)),
        compiler_params=params(),
        name="column_sums",
    )(*pieces)


def first_kernel(start, turned, shifts, goals, again, alone, first, middle, *refs):
    hands, (held_in, one_in, two_in, held, one, two, x, out, sent) = refs[:HANDS], refs[HANDS:]
    del one_in, two_in, held_in
    part, width = middle.shape
    x[0:part, :] = first[0:part, :]
    x[part : 2 * part, :] = middle[...]
    for h, hand in enumerate(hands):
        for turn in range(hand.shape[0] // 16):
            block = 2 * part + 16 * (h + HANDS * turn)
            x[block : block + 16, :] = hand[16 * turn : 16 * turn + 16, :]
    span = SLOTS + 128
    base = 8 * part
    slot = iota((SLOTS, span), 0)
    group = 4
    stores = []
    for k in range(4 * part // SLOTS):
        begin = pl.multiple_of(start[k, 0], 128)
        hot = as_bf(slot == goals[0:1, pl.ds(begin, span)] - k * SLOTS)
        out[k * SLOTS : (k + 1) * SLOTS, :] = dot(hot, x[pl.ds(begin, span), :]).astype(BF)
        if k % group == group - 1:
            size = group * SLOTS
            lines = pl.ds((k + 1) * SLOTS - size, size)
            to = held.at[pl.ds(base + (k + 1) * SLOTS - size, size)]
            stores.append(pltpu.make_async_copy(out.at[lines], to, sent.at[k // group]))
            stores[-1].start()
            score = scores(out[lines, :], turned[...])
            m_one = margins(score, shifts[0:1, 0:1], 0, width)
            m_two = margins(score, shifts[1:2, 0:1], 2, width)
            for i in range(size // 128):
                line = (k + 1) * SLOTS // 128 - size // 128 + i
                line = slice(line, line + 1)
                lanes = slice(128 * i, 128 * (i + 1))
                one[line, :] = jnp.where(alone[line, :] > 0.5, m_one[:, lanes], again[line, :])
                two[line, :] = jnp.where(alone[line, :] > 0.5, m_two[:, lanes], 0.0)
    for store in stores:
        store.wait()


def first_call(start, turned, shifts, goals, again, alone, first, middle, hands, held, one, two):
    width = held.shape[1]
    cap = goals.shape[1]
    lines = cap // 128
    return pl.pallas_call(
        first_kernel,
        grid=(1,),
        out_shape=[
            jax.ShapeDtypeStruct(held.shape, BF),
            jax.ShapeDtypeStruct(one.shape, F32),
            jax.ShapeDtypeStruct(two.shape, F32),
        ],
        in_specs=[spec(pltpu.SMEM)] + [spec(pltpu.VMEM)] * (HANDS + 7) + [spec(pl.ANY)] * 3,
        out_specs=[
            spec(pl.ANY),
            pl.BlockSpec((lines, 128), lambda k: (2, 0)),
            pl.BlockSpec((lines, 128), lambda k: (2, 0)),
        ],
        scratch_shapes=[
            pltpu.VMEM((cap, width), BF),
            pltpu.VMEM((cap, width), BF),
            pltpu.SemaphoreType.DMA((cap // BLK,)),
        ],
        input_output_aliases={8 + HANDS: 0, 9 + HANDS: 1, 10 + HANDS: 2},
        compiler_params=params(),
        cost_estimate=pl.CostEstimate(flops=3 * 10**9, bytes_accessed=7 * 10**6, transcendentals=0),
        name="first_slots",
    )(start, turned, shifts, goals, again, alone, first, middle, *hands, held, one, two)


def local(vectors, child_labels):
    ways = lax.axis_size("cube")
    top = ways // 2
    nxt = ways // 4
    me = lax.axis_index("cube")
    here = jnp.stack([(me // top) & 1, (me // nxt) & 1]).astype(I32)
    after = lax.optimization_barrier
    pos, off, every, leavers = plan_call(here, child_labels)
    counts = [leavers] + [swap(leavers, bits) for bits in (nxt, top, top | nxt)]
    first, middle, rest = sort_call(here, child_labels, pos, off, every, vectors)
    first, *counts = after((first, *counts))
    first_in = swap(first, top)
    second = second_send_call(off, pos, first, vectors)
    second_in = swap(second, nxt)
    rest, second = after((rest, second))
    own, *hands = deal_call(rest, *counts)
    hands = [own] + [swap(hand, h + 1) for h, hand in enumerate(hands)]
    after_deal, hands[1] = after((pos, hands[1]))
    meta = rank_call(off, after_deal)
    held = own_call(after_deal, vectors)
    limit = rest.shape[0]
    step = limit // 32
    held, meta, hands[7] = after((held, meta, hands[7]))
    packed, longest, begins = pack_call(step, hands)
    bit = HANDS
    while bit < nxt:
        longest = jnp.maximum(longest, swap(longest, bit))
        bit *= 2

    def cross(size):
        def branch(rows, first_in, meta):
            got = jnp.pad(swap(rows[:size], top), ((0, limit - size), (0, 0))) if size else jnp.zeros_like(rows)
            return got, swap(first_in, nxt), swap(meta, top)

        return branch

    sizes = range(0, limit + 1, step)
    packed, first_in = after((packed, first_in))
    packed_in, relay, meta_in = lax.switch(longest[0, 0], [cross(size) for size in sizes], packed, first_in, meta)
    middle, packed_in = after((middle, packed_in))
    middle_in = swap(middle, top)
    own, *hands = part_call(begins, packed_in)
    hands = [own] + [swap(hand, h + 1) for h, hand in enumerate(hands)]
    second_in, hands[1] = after((second_in, hands[1]))
    total = column_call(first, second_in, first_in, relay)
    bit = 1
    while bit < nxt:
        total = total + swap(total, bit)
        bit *= 2
    cents, turned, shifts, one, two = centre_call(here, total, child_labels, vectors)
    held, two, again, alone, start, goals = second_call(
        turned, shifts, second_in, relay, first_in, meta_in, counts[2], held, two
    )
    held, one, two = first_call(
        start, turned, shifts, goals, again, alone, first_in, middle_in, hands, held, one, two
    )
    return held, one.reshape(-1), two.reshape(-1), cents


def solution(mesh):
    return jax.shard_map(
        local,
        mesh=mesh,
        in_specs=(P("cube", None), P(None, "cube")),
        out_specs=(P("cube", None), P("cube"), P("cube"), P()),
        check_vma=False,
    )
```

profile of v0, /device:TPU:0, one launch (start us, length us, event | category | flops | bytes accessed | tf_op | source)
XLA Modules:
  0.0 140.2 jit_solution(11172220191382966213)
XLA Ops:
  2.4 5.1 %collective-permute-start.100 = (s32[8,128]{1,0:T(8,128)S(1)}, s32[8,128]{1,0:T(8,128)S(1)}, u32[]{:S(2)}, u32[]{:S(2)}) collective-permute-start(s32[8,128]{1,0:T(8,128)S(1)} %get-tuple-element.366.own), channel_id=1, source_target_pairs={{0,24},{1,25},{2,26},{3,27},{4,28},{5,29},{6,30},{7,31},{8,16},{9,... | collective-permute-start | bytes 12296 | tf_op jit(solution)/shard_map/ppermute | solution.py:20
  8.2 3.8 %sort_leavers.1 = (bf16[528,768]{1,0:T(8,128)(2,1)S(1)}, bf16[512,768]{1,0:T(8,128)(2,1)S(1)}, bf16[1024,768]{1,0:T(8,128)(2,1)S(1)}) custom-call(s32[2]{0:T(128)S(1)} %pad_add_fusion.here, s32[2,4096]{1,0:T(2,128)S(1)} %copy-done.2, s32[128,256]{1,0:T(8,128)S(1)} %get-tuple-element.378.pos_ref.pos, s32[128,128]{1,0:T(8,128)S(1)} %get-tuple-element.359.off_ref.off, ...), custom_call_target="tpu_custom_call" | custom-call | flops 8000000000 | bytes 10000000 | tf_op jit(solution)/shard_map/sort_leavers/pallas_call | solution.py:172
  12.0 2.3 %collective-permute-start.109 = (bf16[528,768]{1,0:T(8,128)(2,1)S(1)}, bf16[528,768]{1,0:T(8,128)(2,1)}, u32[]{:S(2)}, u32[]{:S(2)}) collective-permute-start(bf16[528,768]{1,0:T(8,128)(2,1)S(1)} %get-tuple-element.363.first.own), channel_id=1, source_target_pairs={{0,16},{1,17},{2,18},{3,19},{4,20},{5,21},{6,22},{7,23},{8,24},{9,... | collective-permute-start | bytes 2433032 | tf_op jit(solution)/shard_map/ppermute | solution.py:20
  14.4 1.5 %second_send.1 = bf16[528,768]{1,0:T(8,128)(2,1)S(1)} custom-call(s32[128,128]{1,0:T(8,128)S(1)} %get-tuple-element.359.off_ref.off, s32[128,256]{1,0:T(8,128)S(1)} %get-tuple-element.378.pos_ref.pos, bf16[528,768]{1,0:T(8,128)(2,1)S(1)} %get-tuple-element.363.first.own, bf16[4096,768]{1,0:T(8,128)(2,1)S(1)} %copy-done), custom_call_target="tpu_custom_call" | custom-call | flops 100000000 | bytes 1000000 | tf_op jit(solution)/shard_map/second_send/pallas_call | solution.py:318
  16.1 1.6 %collective-permute-start.103 = (bf16[144,768]{1,0:T(8,128)(2,1)S(1)}, bf16[144,768]{1,0:T(8,128)(2,1)S(1)}, u32[]{:S(2)}, u32[]{:S(2)}) collective-permute-start(bf16[144,768]{1,0:T(8,128)(2,1)S(1)} %get-tuple-element.373), channel_id=1, source_target_pairs={{0,2},{1,3},{2,0},{3,1},{4,6},{5,7},{6,4},{7,5},{8,10},{9,11},{10,... | collective-permute-start | bytes 663560 | tf_op jit(solution)/shard_map/ppermute | solution.py:20
  17.9 2.4 %collective-permute-start.108 = (bf16[144,768]{1,0:T(8,128)(2,1)S(1)}, bf16[144,768]{1,0:T(8,128)(2,1)S(1)}, u32[]{:S(2)}, u32[]{:S(2)}) collective-permute-start(bf16[144,768]{1,0:T(8,128)(2,1)S(1)} %get-tuple-element.379), channel_id=1, source_target_pairs={{0,7},{1,6},{2,5},{3,4},{4,3},{5,2},{6,1},{7,0},{8,15},{9,14},{10,... | collective-permute-start | bytes 663560 | tf_op jit(solution)/shard_map/ppermute | solution.py:20
  20.4 2.0 %collective-permute-start.101 = (bf16[528,768]{1,0:T(8,128)(2,1)S(1)}, bf16[528,768]{1,0:T(8,128)(2,1)S(1)}, u32[]{:S(2)}, u32[]{:S(2)}) collective-permute-start(bf16[528,768]{1,0:T(8,128)(2,1)S(1)} %second_send.1), channel_id=1, source_target_pairs={{0,8},{1,9},{2,10},{3,11},{4,12},{5,13},{6,14},{7,15},{8,0},{9,1},... | collective-permute-start | bytes 2433032 | tf_op jit(solution)/shard_map/ppermute | solution.py:20
  22.4 2.0 %collective-permute-done.103.refs_2_ = bf16[144,768]{1,0:T(8,128)(2,1)S(1)} collective-permute-done((bf16[144,768]{1,0:T(8,128)(2,1)S(1)}, bf16[144,768]{1,0:T(8,128)(2,1)S(1)}, u32[]{:S(2)}, u32[]{:S(2)}) %collective-permute-start.103) | collective-permute-done | bytes 221216 | tf_op jit(solution)/shard_map/ppermute | solution.py:20
  24.4 1.5 %collective-permute-start.105 = (bf16[144,768]{1,0:T(8,128)(2,1)S(1)}, bf16[144,768]{1,0:T(8,128)(2,1)S(1)}, u32[]{:S(2)}, u32[]{:S(2)}) collective-permute-start(bf16[144,768]{1,0:T(8,128)(2,1)S(1)} %get-tuple-element.375), channel_id=1, source_target_pairs={{0,4},{1,5},{2,6},{3,7},{4,0},{5,1},{6,2},{7,3},{8,12},{9,13},{10,... | collective-permute-start | bytes 663560 | tf_op jit(solution)/shard_map/ppermute | solution.py:20
  25.9 2.3 %collective-permute-done.104.refs_3_ = bf16[144,768]{1,0:T(8,128)(2,1)S(1)} collective-permute-done((bf16[144,768]{1,0:T(8,128)(2,1)S(1)}, bf16[144,768]{1,0:T(8,128)(2,1)S(1)}, u32[]{:S(2)}, u32[]{:S(2)}) %collective-permute-start.104) | collective-permute-done | bytes 221216 | tf_op jit(solution)/shard_map/ppermute | solution.py:20
  28.2 2.1 %collective-permute-start.106 = (bf16[144,768]{1,0:T(8,128)(2,1)S(1)}, bf16[144,768]{1,0:T(8,128)(2,1)S(1)}, u32[]{:S(2)}, u32[]{:S(2)}) collective-permute-start(bf16[144,768]{1,0:T(8,128)(2,1)S(1)} %get-tuple-element.376), channel_id=1, source_target_pairs={{0,5},{1,4},{2,7},{3,6},{4,1},{5,0},{6,3},{7,2},{8,13},{9,12},{10,... | collective-permute-start | bytes 663560 | tf_op jit(solution)/shard_map/ppermute | solution.py:20
  30.3 3.7 %collective-permute-done.108.refs_7_ = bf16[144,768]{1,0:T(8,128)(2,1)S(1)} collective-permute-done((bf16[144,768]{1,0:T(8,128)(2,1)S(1)}, bf16[144,768]{1,0:T(8,128)(2,1)S(1)}, u32[]{:S(2)}, u32[]{:S(2)}) %collective-permute-start.108) | collective-permute-done | bytes 221216 | tf_op jit(solution)/shard_map/ppermute | solution.py:20
  34.0 1.5 %collective-permute-start.107 = (bf16[144,768]{1,0:T(8,128)(2,1)S(1)}, bf16[144,768]{1,0:T(8,128)(2,1)S(1)}, u32[]{:S(2)}, u32[]{:S(2)}) collective-permute-start(bf16[144,768]{1,0:T(8,128)(2,1)S(1)} %get-tuple-element.377), channel_id=1, source_target_pairs={{0,6},{1,7},{2,4},{3,5},{4,2},{5,3},{6,0},{7,1},{8,14},{9,15},{10,... | collective-permute-start | bytes 663560 | tf_op jit(solution)/shard_map/ppermute | solution.py:20
  35.5 2.0 %list_ranks.1 = s32[8,256]{1,0:T(8,128)S(1)} custom-call(s32[128,128]{1,0:T(8,128)S(1)} %get-tuple-element.359.off_ref.off, s32[128,256]{1,0:T(8,128)S(1)} %get-tuple-element.378.pos_ref.pos), custom_call_target="tpu_custom_call" | custom-call | flops 100000000 | bytes 1000000 | tf_op jit(solution)/shard_map/list_ranks/pallas_call | solution.py:353
  37.4 4.1 %own_slots.1.held_in = bf16[7168,768]{1,0:T(8,128)(2,1)} custom-call(s32[128,256]{1,0:T(8,128)S(1)} %get-tuple-element.378.pos_ref.pos, bf16[4096,768]{1,0:T(8,128)(2,1)S(1)} %copy-done), custom_call_target="tpu_custom_call" | custom-call | flops 100000000 | bytes 1000000 | tf_op jit(solution)/shard_map/own_slots/pallas_call | solution.py:375
  41.5 2.7 %collective-permute-done.106.refs_5_ = bf16[144,768]{1,0:T(8,128)(2,1)S(1)} collective-permute-done((bf16[144,768]{1,0:T(8,128)(2,1)S(1)}, bf16[144,768]{1,0:T(8,128)(2,1)S(1)}, u32[]{:S(2)}, u32[]{:S(2)}) %collective-permute-start.106) | collective-permute-done | bytes 221216 | tf_op jit(solution)/shard_map/ppermute | solution.py:20
  45.7 4.1 %collective-permute-done.109.b.first = bf16[528,768]{1,0:T(8,128)(2,1)} collective-permute-done((bf16[528,768]{1,0:T(8,128)(2,1)S(1)}, bf16[528,768]{1,0:T(8,128)(2,1)}, u32[]{:S(2)}, u32[]{:S(2)}) %collective-permute-start.109) | collective-permute-done | bytes 811040 | tf_op jit(solution)/shard_map/ppermute | solution.py:20
  49.8 48.5 %conditional.1 = (bf16[1024,768]{1,0:T(8,128)(2,1)}, bf16[528,768]{1,0:T(8,128)(2,1)}, s32[8,256]{1,0:T(8,128)}) conditional(s32[]{:T(128)} %bitcast.2, (bf16[528,768]{1,0:T(8,128)(2,1)}, s32[8,256]{1,0:T(8,128)S(1)}) %tuple.152, (bf16[1024,768]{1,0:T(8,128)(2,1)S(1)}, bf16[528,768]{1,0:T(8,128)(2,1)}, ...), branch_computations={%region_0.1_spmd, %region_1.2_spmd, %region_2.3_spmd, %region_3.4_... | conditional | bytes 15515794 | solution.py:670
  50.0 3.7 %collective-permute-start.63 = (bf16[528,768]{1,0:T(8,128)(2,1)}, bf16[528,768]{1,0:T(8,128)(2,1)}, u32[]{:S(2)}, u32[]{:S(2)}) collective-permute-start(bf16[528,768]{1,0:T(8,128)(2,1)} %get-tuple-element.259), channel_id=1, source_target_pairs={{0,8},{1,9},{2,10},{3,11},{4,12},{5,13},{6,14},{7,15},{8,0},{9,1},... | collective-permute-start | bytes 2433032 | tf_op jit(solution)/shard_map/cond/branch_21_fun/ppermute | solution.py:20
  53.8 43.3 %collective-permute-done.62 = bf16[672,768]{1,0:T(8,128)(2,1)S(1)} collective-permute-done((bf16[672,768]{1,0:T(8,128)(2,1)S(1)}, bf16[672,768]{1,0:T(8,128)(2,1)S(1)}, u32[]{:S(2)}, u32[]{:S(2)}) %collective-permute-start.62) | collective-permute-done | bytes 1032224 | tf_op jit(solution)/shard_map/cond/branch_21_fun/ppermute | solution.py:20
  98.3 2.1 %part_pack.1 = (bf16[128,768]{1,0:T(8,128)(2,1)S(1)}, bf16[128,768]{1,0:T(8,128)(2,1)S(1)}, bf16[128,768]{1,0:T(8,128)(2,1)S(1)}, bf16[128,768]{1,0:T(8,128)(2,1...) custom-call(s32[8,128]{1,0:T(8,128)S(1)} %get-tuple-element.381.begi, ...), custom_call_target="tpu_custom_call" | custom-call | bytes 3000000 | tf_op jit(solution)/shard_map/part_pack/pallas_call | solution.py:275
  100.6 1.5 %collective-permute-start.115 = (bf16[128,768]{1,0:T(8,128)(2,1)S(1)}, bf16[128,768]{1,0:T(8,128)(2,1)S(1)}, u32[]{:S(2)}, u32[]{:S(2)}) collective-permute-start(bf16[128,768]{1,0:T(8,128)(2,1)S(1)} %get-tuple-element.405), channel_id=1, source_target_pairs={{0,2},{1,3},{2,0},{3,1},{4,6},{5,7},{6,4},{7,5},{8,10},{9,11},{10,... | collective-permute-start | bytes 589832 | tf_op jit(solution)/shard_map/ppermute | solution.py:20
  104.5 1.4 %collective-permute-start.112 = (f32[8,768]{1,0:T(8,128)S(1)}, f32[8,768]{1,0:T(8,128)S(1)}, u32[]{:S(2)}, u32[]{:S(2)}) collective-permute-start(f32[8,768]{1,0:T(8,128)S(1)} %add.73), channel_id=1, source_target_pairs={{0,2},{1,3},{2,0},{3,1},{4,6},{5,7},{6,4},{7,5},{8,10},{9,11},{10,... | collective-permute-start | bytes 73736 | tf_op jit(solution)/shard_map/ppermute | solution.py:20
  105.9 6.7 %collective-permute-done.112 = f32[8,768]{1,0:T(8,128)S(1)} collective-permute-done((f32[8,768]{1,0:T(8,128)S(1)}, f32[8,768]{1,0:T(8,128)S(1)}, u32[]{:S(2)}, u32[]{:S(2)}) %collective-permute-start.112) | collective-permute-done | bytes 24608 | tf_op jit(solution)/shard_map/ppermute | solution.py:20
  112.6 1.5 %collective-permute-start.113 = (f32[8,768]{1,0:T(8,128)S(1)}, f32[8,768]{1,0:T(8,128)S(1)}, u32[]{:S(2)}, u32[]{:S(2)}) collective-permute-start(f32[8,768]{1,0:T(8,128)S(1)} %add.74), channel_id=1, source_target_pairs={{0,4},{1,5},{2,6},{3,7},{4,0},{5,1},{6,2},{7,3},{8,12},{9,13},{10,... | collective-permute-start | bytes 73736 | tf_op jit(solution)/shard_map/ppermute | solution.py:20
  114.7 2.5 %collective-permute-start.119 = (bf16[128,768]{1,0:T(8,128)(2,1)S(1)}, bf16[128,768]{1,0:T(8,128)(2,1)S(1)}, u32[]{:S(2)}, u32[]{:S(2)}) collective-permute-start(bf16[128,768]{1,0:T(8,128)(2,1)S(1)} %get-tuple-element.409), channel_id=1, source_target_pairs={{0,6},{1,7},{2,4},{3,5},{4,2},{5,3},{6,0},{7,1},{8,14},{9,15},{10,... | collective-permute-start | bytes 589832 | tf_op jit(solution)/shard_map/ppermute | solution.py:20
  117.2 1.3 collective-permute-start.120
  118.5 2.8 %copy-done.1 = bf16[4096,768]{1,0:T(8,128)(2,1)S(1)} copy-done((bf16[4096,768]{1,0:T(8,128)(2,1)S(1)}, bf16[4096,768]{1,0:T(8,128)(2,1)}, u32[]{:S(2)}) %copy-start.1) | copy-done | bytes 6291480
  121.3 4.6 %own_margins.1 = (f32[6,768]{1,0:T(8,128)}, bf16[768,128]{1,0:T(8,128)(2,1)S(1)}, f32[8,128]{1,0:T(8,128)S(1)}, f32[48,128]{1,0:T(8,128)}, f32[56,128]{1,0:T(8,128)}) custom-call(s32[2]{0:T(128)S(1)} %pad_add_fusion.here, f32[8,768]{1,0:T(8,128)S(1)} %add.75.total, s32[2,4096]{1,0:T(2,128)S(1)} %copy-done.3, bf16[4096,768]{1,0:T(8,128)(2,1)S(1)} %copy-done.1), custom_call_target="tpu_custom_call" | custom-call | flops 100000000 | bytes 100000 | tf_op jit(solution)/shard_map/own_margins/pallas_call | solution.py:438
  125.9 4.3 %second_slots.1 = (bf16[7168,768]{1,0:T(8,128)(2,1)}, f32[56,128]{1,0:T(8,128)}, f32[16,128]{1,0:T(8,128)S(1)}, f32[16,128]{1,0:T(8,128)S(1)}, s32[16,128]{1,0:T(8,128)S(1)}, /*index=5*/s32[8,2048]{1,0:T(8,128)S(1)}) custom-call(bf16[768,128]{1,0:T(8,128)(2,1)S(1)} %get-tuple-element.393.turned, ...), custom_call_target="tpu_custom_call", output_to_operand_aliasing={{0}: (7, {}), {1}: (8, {})} | custom-call | flops 100000000 | bytes 100000 | tf_op jit(solution)/shard_map/second_slots/pallas_call | solution.py:513
  131.2 2.8 %collective-permute-done.114.middle = bf16[512,768]{1,0:T(8,128)(2,1)S(1)} collective-permute-done((bf16[512,768]{1,0:T(8,128)(2,1)S(1)}, bf16[512,768]{1,0:T(8,128)(2,1)S(1)}, u32[]{:S(2)}, u32[]{:S(2)}) %collective-permute-start.114) | collective-permute-done | bytes 786464 | tf_op jit(solution)/shard_map/ppermute | solution.py:20
  134.0 6.1 %first_slots.1 = (bf16[7168,768]{1,0:T(8,128)(2,1)}, f32[48,128]{1,0:T(8,128)}, f32[56,128]{1,0:T(8,128)}) custom-call(s32[16,128]{1,0:T(8,128)S(1)} %get-tuple-element.398.start, bf16[768,128]{1,0:T(8,128)(2,1)S(1)} %get-tuple-element.393.turned, ...), custom_call_target="tpu_custom_call", output_to_operand_aliasing={{0}: (16, {}), {1}: (17, {}), {2}: (18, {})} | custom-call | flops 3000000000 | bytes 7000000 | tf_op jit(solution)/shard_map/first_slots/pallas_call | solution.py:606
  (48 shorter events, 9.3 us)
Async XLA Ops:
  0.7 0.8 copy-start.2
  1.5 6.7 %copy-start = (bf16[4096,768]{1,0:T(8,128)(2,1)S(1)}, bf16[4096,768]{1,0:T(8,128)(2,1)}, u32[]{:S(2)}) copy-start(bf16[4096,768]{1,0:T(8,128)(2,1)} %x_ref.1) | copy-start | bytes 18874372
  2.4 9.6 %collective-permute-start.100 = (s32[8,128]{1,0:T(8,128)S(1)}, s32[8,128]{1,0:T(8,128)S(1)}, u32[]{:S(2)}, u32[]{:S(2)}) collective-permute-start(s32[8,128]{1,0:T(8,128)S(1)} %get-tuple-element.366.own), channel_id=1, source_target_pairs={{0,24},{1,25},{2,26},{3,27},{4,28},{5,29},{6,30},{7,31},{8,16},{9,... | collective-permute-start | bytes 12296 | tf_op jit(solution)/shard_map/ppermute | solution.py:20
  7.5 4.5 %collective-permute-start.99 = (s32[8,128]{1,0:T(8,128)S(1)}, s32[8,128]{1,0:T(8,128)S(1)}, u32[]{:S(2)}, u32[]{:S(2)}) collective-permute-start(s32[8,128]{1,0:T(8,128)S(1)} %get-tuple-element.366.own), channel_id=1, source_target_pairs={{0,16},{1,17},{2,18},{3,19},{4,20},{5,21},{6,22},{7,23},{8,24},{9,... | collective-permute-start | bytes 12296 | tf_op jit(solution)/shard_map/ppermute | solution.py:20
  7.5 4.5 %collective-permute-start.98 = (s32[8,128]{1,0:T(8,128)S(1)}, s32[8,128]{1,0:T(8,128)S(1)}, u32[]{:S(2)}, u32[]{:S(2)}) collective-permute-start(s32[8,128]{1,0:T(8,128)S(1)} %get-tuple-element.366.own), channel_id=1, source_target_pairs={{0,8},{1,9},{2,10},{3,11},{4,12},{5,13},{6,14},{7,15},{8,0},{9,1},... | collective-permute-start | bytes 12296 | tf_op jit(solution)/shard_map/ppermute | solution.py:20
  12.0 37.8 %collective-permute-start.109 = (bf16[528,768]{1,0:T(8,128)(2,1)S(1)}, bf16[528,768]{1,0:T(8,128)(2,1)}, u32[]{:S(2)}, u32[]{:S(2)}) collective-permute-start(bf16[528,768]{1,0:T(8,128)(2,1)S(1)} %get-tuple-element.363.first.own), channel_id=1, source_target_pairs={{0,16},{1,17},{2,18},{3,19},{4,20},{5,21},{6,22},{7,23},{8,24},{9,... | collective-permute-start | bytes 2433032 | tf_op jit(solution)/shard_map/ppermute | solution.py:20
  16.0 4.4 %collective-permute-start.102 = (bf16[144,768]{1,0:T(8,128)(2,1)S(1)}, bf16[144,768]{1,0:T(8,128)(2,1)S(1)}, u32[]{:S(2)}, u32[]{:S(2)}) collective-permute-start(bf16[144,768]{1,0:T(8,128)(2,1)S(1)} %get-tuple-element.371), channel_id=1, source_target_pairs={{0,1},{1,0},{2,3},{3,2},{4,5},{5,4},{6,7},{7,6},{8,9},{9,8},{10,11... | collective-permute-start | bytes 663560 | tf_op jit(solution)/shard_map/ppermute | solution.py:20
  16.1 8.3 %collective-permute-start.103 = (bf16[144,768]{1,0:T(8,128)(2,1)S(1)}, bf16[144,768]{1,0:T(8,128)(2,1)S(1)}, u32[]{:S(2)}, u32[]{:S(2)}) collective-permute-start(bf16[144,768]{1,0:T(8,128)(2,1)S(1)} %get-tuple-element.373), channel_id=1, source_target_pairs={{0,2},{1,3},{2,0},{3,1},{4,6},{5,7},{6,4},{7,5},{8,10},{9,11},{10,... | collective-permute-start | bytes 663560 | tf_op jit(solution)/shard_map/ppermute | solution.py:20
  17.6 10.6 %collective-permute-start.104 = (bf16[144,768]{1,0:T(8,128)(2,1)S(1)}, bf16[144,768]{1,0:T(8,128)(2,1)S(1)}, u32[]{:S(2)}, u32[]{:S(2)}) collective-permute-start(bf16[144,768]{1,0:T(8,128)(2,1)S(1)} %get-tuple-element.374), channel_id=1, source_target_pairs={{0,3},{1,2},{2,1},{3,0},{4,7},{5,6},{6,5},{7,4},{8,11},{9,10},{10,... | collective-permute-start | bytes 663560 | tf_op jit(solution)/shard_map/ppermute | solution.py:20
  17.9 16.1 %collective-permute-start.108 = (bf16[144,768]{1,0:T(8,128)(2,1)S(1)}, bf16[144,768]{1,0:T(8,128)(2,1)S(1)}, u32[]{:S(2)}, u32[]{:S(2)}) collective-permute-start(bf16[144,768]{1,0:T(8,128)(2,1)S(1)} %get-tuple-element.379), channel_id=1, source_target_pairs={{0,7},{1,6},{2,5},{3,4},{4,3},{5,2},{6,1},{7,0},{8,15},{9,14},{10,... | collective-permute-start | bytes 663560 | tf_op jit(solution)/shard_map/ppermute | solution.py:20
  20.4 82.1 %collective-permute-start.101 = (bf16[528,768]{1,0:T(8,128)(2,1)S(1)}, bf16[528,768]{1,0:T(8,128)(2,1)S(1)}, u32[]{:S(2)}, u32[]{:S(2)}) collective-permute-start(bf16[528,768]{1,0:T(8,128)(2,1)S(1)} %second_send.1), channel_id=1, source_target_pairs={{0,8},{1,9},{2,10},{3,11},{4,12},{5,13},{6,14},{7,15},{8,0},{9,1},... | collective-permute-start | bytes 2433032 | tf_op jit(solution)/shard_map/ppermute | solution.py:20
  24.4 17.1 %collective-permute-start.105 = (bf16[144,768]{1,0:T(8,128)(2,1)S(1)}, bf16[144,768]{1,0:T(8,128)(2,1)S(1)}, u32[]{:S(2)}, u32[]{:S(2)}) collective-permute-start(bf16[144,768]{1,0:T(8,128)(2,1)S(1)} %get-tuple-element.375), channel_id=1, source_target_pairs={{0,4},{1,5},{2,6},{3,7},{4,0},{5,1},{6,2},{7,3},{8,12},{9,13},{10,... | collective-permute-start | bytes 663560 | tf_op jit(solution)/shard_map/ppermute | solution.py:20
  28.2 16.0 %collective-permute-start.106 = (bf16[144,768]{1,0:T(8,128)(2,1)S(1)}, bf16[144,768]{1,0:T(8,128)(2,1)S(1)}, u32[]{:S(2)}, u32[]{:S(2)}) collective-permute-start(bf16[144,768]{1,0:T(8,128)(2,1)S(1)} %get-tuple-element.376), channel_id=1, source_target_pairs={{0,5},{1,4},{2,7},{3,6},{4,1},{5,0},{6,3},{7,2},{8,13},{9,12},{10,... | collective-permute-start | bytes 663560 | tf_op jit(solution)/shard_map/ppermute | solution.py:20
  34.0 10.2 %collective-permute-start.107 = (bf16[144,768]{1,0:T(8,128)(2,1)S(1)}, bf16[144,768]{1,0:T(8,128)(2,1)S(1)}, u32[]{:S(2)}, u32[]{:S(2)}) collective-permute-start(bf16[144,768]{1,0:T(8,128)(2,1)S(1)} %get-tuple-element.377), channel_id=1, source_target_pairs={{0,6},{1,7},{2,4},{3,5},{4,2},{5,3},{6,0},{7,1},{8,14},{9,15},{10,... | collective-permute-start | bytes 663560 | tf_op jit(solution)/shard_map/ppermute | solution.py:20
  49.9 47.2 %collective-permute-start.62 = (bf16[672,768]{1,0:T(8,128)(2,1)S(1)}, bf16[672,768]{1,0:T(8,128)(2,1)S(1)}, u32[]{:S(2)}, u32[]{:S(2)}) collective-permute-start(bf16[672,768]{1,0:T(8,128)(2,1)S(1)} %slice.84), channel_id=1, source_target_pairs={{0,16},{1,17},{2,18},{3,19},{4,20},{5,21},{6,22},{7,23},{8,24},{9,... | collective-permute-start | bytes 3096584 | tf_op jit(solution)/shard_map/cond/branch_21_fun/ppermute | solution.py:20
  50.0 48.3 %collective-permute-start.63 = (bf16[528,768]{1,0:T(8,128)(2,1)}, bf16[528,768]{1,0:T(8,128)(2,1)}, u32[]{:S(2)}, u32[]{:S(2)}) collective-permute-start(bf16[528,768]{1,0:T(8,128)(2,1)} %get-tuple-element.259), channel_id=1, source_target_pairs={{0,8},{1,9},{2,10},{3,11},{4,12},{5,13},{6,14},{7,15},{8,0},{9,1},... | collective-permute-start | bytes 2433032 | tf_op jit(solution)/shard_map/cond/branch_21_fun/ppermute | solution.py:20
  53.7 44.6 %collective-permute-start.64 = (s32[8,256]{1,0:T(8,128)S(1)}, s32[8,256]{1,0:T(8,128)}, u32[]{:S(2)}, u32[]{:S(2)}) collective-permute-start(s32[8,256]{1,0:T(8,128)S(1)} %get-tuple-element.260), channel_id=1, source_target_pairs={{0,16},{1,17},{2,18},{3,19},{4,20},{5,21},{6,22},{7,23},{8,24},{9,... | collective-permute-start | bytes 24584 | tf_op jit(solution)/shard_map/cond/branch_21_fun/ppermute | solution.py:20
  98.3 35.7 %collective-permute-start.114 = (bf16[512,768]{1,0:T(8,128)(2,1)S(1)}, bf16[512,768]{1,0:T(8,128)(2,1)S(1)}, u32[]{:S(2)}, u32[]{:S(2)}) collective-permute-start(bf16[512,768]{1,0:T(8,128)(2,1)S(1)} %get-tuple-element.402), channel_id=1, source_target_pairs={{0,16},{1,17},{2,18},{3,19},{4,20},{5,21},{6,22},{7,23},{8,24},{9,... | collective-permute-start | bytes 2359304 | tf_op jit(solution)/shard_map/ppermute | solution.py:20
  100.5 1.9 %collective-permute-start.110 = (bf16[128,768]{1,0:T(8,128)(2,1)S(1)}, bf16[128,768]{1,0:T(8,128)(2,1)S(1)}, u32[]{:S(2)}, u32[]{:S(2)}) collective-permute-start(bf16[128,768]{1,0:T(8,128)(2,1)S(1)} %get-tuple-element.390), channel_id=1, source_target_pairs={{0,1},{1,0},{2,3},{3,2},{4,5},{5,4},{6,7},{7,6},{8,9},{9,8},{10,11... | collective-permute-start | bytes 589832 | tf_op jit(solution)/shard_map/ppermute | solution.py:20
  100.6 14.1 %collective-permute-start.115 = (bf16[128,768]{1,0:T(8,128)(2,1)S(1)}, bf16[128,768]{1,0:T(8,128)(2,1)S(1)}, u32[]{:S(2)}, u32[]{:S(2)}) collective-permute-start(bf16[128,768]{1,0:T(8,128)(2,1)S(1)} %get-tuple-element.405), channel_id=1, source_target_pairs={{0,2},{1,3},{2,0},{3,1},{4,6},{5,7},{6,4},{7,5},{8,10},{9,11},{10,... | collective-permute-start | bytes 589832 | tf_op jit(solution)/shard_map/ppermute | solution.py:20
  102.0 12.6 %collective-permute-start.116 = (bf16[128,768]{1,0:T(8,128)(2,1)S(1)}, bf16[128,768]{1,0:T(8,128)(2,1)S(1)}, u32[]{:S(2)}, u32[]{:S(2)}) collective-permute-start(bf16[128,768]{1,0:T(8,128)(2,1)S(1)} %get-tuple-element.406), channel_id=1, source_target_pairs={{0,3},{1,2},{2,1},{3,0},{4,7},{5,6},{6,5},{7,4},{8,11},{9,10},{10,... | collective-permute-start | bytes 589832 | tf_op jit(solution)/shard_map/ppermute | solution.py:20
  102.4 16.1 %copy-start.3 = (s32[2,4096]{1,0:T(2,128)S(1)}, s32[2,4096]{1,0:T(2,128)}, u32[]{:S(2)}) copy-start(s32[2,4096]{1,0:T(2,128)} %labels.5) | copy-start | bytes 98308
  103.3 1.2 collective-permute-start.111
  104.5 8.1 %collective-permute-start.112 = (f32[8,768]{1,0:T(8,128)S(1)}, f32[8,768]{1,0:T(8,128)S(1)}, u32[]{:S(2)}, u32[]{:S(2)}) collective-permute-start(f32[8,768]{1,0:T(8,128)S(1)} %add.73), channel_id=1, source_target_pairs={{0,2},{1,3},{2,0},{3,1},{4,6},{5,7},{6,4},{7,5},{8,10},{9,11},{10,... | collective-permute-start | bytes 73736 | tf_op jit(solution)/shard_map/ppermute | solution.py:20
  112.6 4.6 %collective-permute-start.113 = (f32[8,768]{1,0:T(8,128)S(1)}, f32[8,768]{1,0:T(8,128)S(1)}, u32[]{:S(2)}, u32[]{:S(2)}) collective-permute-start(f32[8,768]{1,0:T(8,128)S(1)} %add.74), channel_id=1, source_target_pairs={{0,4},{1,5},{2,6},{3,7},{4,0},{5,1},{6,2},{7,3},{8,12},{9,13},{10,... | collective-permute-start | bytes 73736 | tf_op jit(solution)/shard_map/ppermute | solution.py:20
  114.1 16.3 %collective-permute-start.117 = (bf16[128,768]{1,0:T(8,128)(2,1)S(1)}, bf16[128,768]{1,0:T(8,128)(2,1)S(1)}, u32[]{:S(2)}, u32[]{:S(2)}) collective-permute-start(bf16[128,768]{1,0:T(8,128)(2,1)S(1)} %get-tuple-element.407), channel_id=1, source_target_pairs={{0,4},{1,5},{2,6},{3,7},{4,0},{5,1},{6,2},{7,3},{8,12},{9,13},{10,... | collective-permute-start | bytes 589832 | tf_op jit(solution)/shard_map/ppermute | solution.py:20
  114.7 16.5 %collective-permute-start.118 = (bf16[128,768]{1,0:T(8,128)(2,1)S(1)}, bf16[128,768]{1,0:T(8,128)(2,1)S(1)}, u32[]{:S(2)}, u32[]{:S(2)}) collective-permute-start(bf16[128,768]{1,0:T(8,128)(2,1)S(1)} %get-tuple-element.408), channel_id=1, source_target_pairs={{0,5},{1,4},{2,7},{3,6},{4,1},{5,0},{6,3},{7,2},{8,13},{9,12},{10,... | collective-permute-start | bytes 589832 | tf_op jit(solution)/shard_map/ppermute | solution.py:20
  114.7 16.5 %collective-permute-start.119 = (bf16[128,768]{1,0:T(8,128)(2,1)S(1)}, bf16[128,768]{1,0:T(8,128)(2,1)S(1)}, u32[]{:S(2)}, u32[]{:S(2)}) collective-permute-start(bf16[128,768]{1,0:T(8,128)(2,1)S(1)} %get-tuple-element.409), channel_id=1, source_target_pairs={{0,6},{1,7},{2,4},{3,5},{4,2},{5,3},{6,0},{7,1},{8,14},{9,15},{10,... | collective-permute-start | bytes 589832 | tf_op jit(solution)/shard_map/ppermute | solution.py:20
  117.2 14.0 %collective-permute-start.120 = (bf16[128,768]{1,0:T(8,128)(2,1)S(1)}, bf16[128,768]{1,0:T(8,128)(2,1)S(1)}, u32[]{:S(2)}, u32[]{:S(2)}) collective-permute-start(bf16[128,768]{1,0:T(8,128)(2,1)S(1)} %get-tuple-element.410), channel_id=1, source_target_pairs={{0,7},{1,6},{2,5},{3,4},{4,3},{5,2},{6,1},{7,0},{8,15},{9,14},{10,... | collective-permute-start | bytes 589832 | tf_op jit(solution)/shard_map/ppermute | solution.py:20
  118.5 2.8 %copy-start.1 = (bf16[4096,768]{1,0:T(8,128)(2,1)S(1)}, bf16[4096,768]{1,0:T(8,128)(2,1)}, u32[]{:S(2)}) copy-start(bf16[4096,768]{1,0:T(8,128)(2,1)} %x_ref.1) | copy-start | bytes 18874372
where the time goes:
time: 140 us
  waiting for transfers between devices  69.3 us (50%)
  starting transfers between devices  33 us (24%)
  Pallas kernels  30.8 us (22%)
  local copies, waits for them, and re-layouts  5.37 us (4%)
  between operations  1.63 us (1%)
    ppermute x26, waiting for transfers between devices, swap(): lax.ppermute(x, 'cube', [(i, i ^ bits) for i in range(lax.axis_size('cube...  69.3 us
    ppermute x26, starting transfers between devices, swap(): lax.ppermute(x, 'cube', [(i, i ^ bits) for i in range(lax.axis_size('cube...  33 us
    pallas_call x1, Pallas kernels, first_call(): pl.pallas_call(first_kernel, grid=(1,), out_shape=[jax.ShapeDtypeStruct(h...  6.06 us
    pallas_call x1, Pallas kernels, centre_call(): pl.pallas_call(centre_kernel, grid=(rows // 1024,), out_shape=[jax.ShapeD...  4.62 us
    pallas_call x1, Pallas kernels, second_call(): pl.pallas_call(second_kernel, grid=(1,), out_shape=[jax.ShapeDtypeStruct(...  4.35 us
    pallas_call x1, Pallas kernels, own_call(): pl.pallas_call(own_kernel, grid=(rows // 1024,), out_shape=jax.ShapeDtype...  4.06 us
    pallas_call x1, Pallas kernels, sort_call(): pl.pallas_call(sort_kernel, out_shape=[jax.ShapeDtypeStruct((part + 16, w...  3.8 us
    unnamed x8, local copies, waits for them, and re-layouts  3.54 us
  transfers between devices with their start and end apart: 26, of which 11 were waited for; matrix products, arithmetic and copies ran while one was open for 1% of the time, Pallas kernels for 17%

commit v1 on v0

--- a/solution.py
+++ b/solution.py
@@ -403,33 +403,40 @@
         ref[start + k : start + k + 1, :] = values[:, 128 * k : 128 * (k + 1)]
 
 
-def centre_kernel(here, total, labels, x_ref, cents, turned, shifts, one, two):
-    width = x_ref.shape[1]
-    lines = labels.shape[1]
-
-    @pl.when(pl.program_id(0) == 0)
-    def _():
-        sums, counts = total[0:4, :], total[4:8, :]
-        low = (sums[0:1] + sums[1:2]) / (counts[0:1] + counts[1:2])
-        high = (sums[2:3] + sums[3:4]) / (counts[2:3] + counts[3:4])
-        groups = sums / counts
-        cents[0:1, :] = low
-        cents[1:2, :] = high
-        cents[2:6, :] = groups
-        top = here[0] == 1
-        left = jnp.where(top, groups[2:3], groups[0:1])
-        right = jnp.where(top, groups[3:4], groups[1:2])
-        rows = jnp.concatenate([low, high, left, right] * 3 + [jnp.zeros((116, width), F32)], axis=0)
-        turned[...] = rows.T.astype(BF)
-        for k, (a, b) in enumerate(((low, high), (left, right))):
-            shift = 0.5 * (jnp.sum(b * b, axis=1, keepdims=True) - jnp.sum(a * a, axis=1, keepdims=True))
-            shifts[k : k + 1, :] = jnp.broadcast_to(shift, (1, 128))
-
-    score = scores(x_ref[pl.ds(pl.program_id(0) * lines, lines), :], turned[...])
+def centre_kernel(here, total, labels, x_hbm, cents, turned, shifts, one, two, x, sem):
+    rows, width = x.shape
+    part = 1024
+    loads = [
+        pltpu.make_async_copy(x_hbm.at[pl.ds(k * part, part)], x.at[pl.ds(k * part, part)], sem.at[k])
+        for k in range(rows // part)
+    ]
+    for load in loads:
+        load.start()
+    sums, counts = total[0:4, :], total[4:8, :]
+    low = (sums[0:1] + sums[1:2]) / (counts[0:1] + counts[1:2])
+    high = (sums[2:3] + sums[3:4]) / (counts[2:3] + counts[3:4])
+    groups = sums / counts
+    cents[0:1, :] = low
+    cents[1:2, :] = high
+    cents[2:6, :] = groups
+    top = here[0] == 1
+    left = jnp.where(top, groups[2:3], groups[0:1])
+    right = jnp.where(top, groups[3:4], groups[1:2])
+    columns = jnp.concatenate([low, high, left, right] * 3 + [jnp.zeros((116, width), F32)], axis=0).T.astype(BF)
+    turned[...] = columns
+    gaps = []
+    for k, (a, b) in enumerate(((low, high), (left, right))):
+        gaps.append(0.5 * (jnp.sum(b * b, axis=1, keepdims=True) - jnp.sum(a * a, axis=1, keepdims=True)))
+        shifts[k : k + 1, :] = jnp.broadcast_to(gaps[k], (1, 128))
+    shifts[2:, :] = jnp.zeros((6, 128), F32)
     stay = labels[0:1, :] == here[0]
     keep = stay & (labels[1:2, :] == here[1])
-    put_lines(one, 0, jnp.where(stay, margins(score, shifts[0:1, 0:1], 0, width), 0.0))
-    put_lines(two, 0, jnp.where(keep, margins(score, shifts[1:2, 0:1], 2, width), 0.0))
+    for k, load in enumerate(loads):
+        load.wait()
+        lanes = slice(k * part, (k + 1) * part)
+        score = scores(x[lanes, :], columns)
+        put_lines(one, k * part // 128, jnp.where(stay[:, lanes], margins(score, gaps[0], 0, width), 0.0))
+        put_lines(two, k * part // 128, jnp.where(keep[:, lanes], margins(score, gaps[1], 2, width), 0.0))
 
 
 def centre_call(here, total, labels, vectors):
@@ -437,7 +444,7 @@
     cap = rows // 2
     return pl.pallas_call(
         centre_kernel,
-        grid=(rows // 1024,),
+        grid=(1,),
         out_shape=[
             jax.ShapeDtypeStruct((6, width), F32),
             jax.ShapeDtypeStruct((width, 128), BF),
@@ -445,26 +452,22 @@
             jax.ShapeDtypeStruct(((rows + cap) // 128, 128), F32),
             jax.ShapeDtypeStruct(((rows + cap + cap // 2) // 128, 128), F32),
         ],
-        in_specs=[
-            spec(pltpu.SMEM),
-            pl.BlockSpec((8, width), lambda b: (0, 0)),
-            pl.BlockSpec((2, 1024), lambda b: (0, b)),
-            spec(pltpu.VMEM),
-        ],
+        in_specs=[spec(pltpu.SMEM), spec(pltpu.VMEM), spec(pltpu.VMEM), spec(pltpu.HBM)],
         out_specs=[
             pl.BlockSpec((6, width), lambda b: (0, 0)),
             pl.BlockSpec((width, 128), lambda b: (0, 0)),
             pl.BlockSpec((8, 128), lambda b: (0, 0)),
-            pl.BlockSpec((8, 128), lambda b: (b, 0)),
-            pl.BlockSpec((8, 128), lambda b: (b, 0)),
-        ],
+            pl.BlockSpec((rows // 128, 128), lambda b: (0, 0)),
+            pl.BlockSpec((rows // 128, 128), lambda b: (0, 0)),
+        ],
+        scratch_shapes=[pltpu.VMEM((rows, width), BF), pltpu.SemaphoreType.DMA((rows // 1024,))],
         compiler_params=params(),
         cost_estimate=pl.CostEstimate(flops=10**8, bytes_accessed=10**5, transcendentals=0),
         name="own_margins",
     )(here, total, labels, vectors)
 
 
-def second_kernel(turned, shifts, second, relay, first, meta, leavers, held_in, two_in, held, two, again, alone, start, goals):
+def second_kernel(turned, shifts, second, relay, first, meta, leavers, held_in, two_in, held, two, again, alone, start, bounds, goals):
     del held_in, two_in
     half = second.shape[0] - 16
     slots = held.shape[0]
@@ -502,6 +505,13 @@
     begin = jnp.sum(jnp.where(earlier, 1.0, 0.0), axis=1, keepdims=True).astype(I32)
     begin = jnp.minimum((begin >> 7) << 7, cap - SLOTS - 128)
     start[...] = jnp.broadcast_to(begin, start.shape)
+    lane = iota((8, cap), 1)
+    edge = 2 * SLOTS * iota((8, cap), 0)
+    before = jnp.sum(jnp.where((lane < both) | (place < edge), 1.0, 0.0), axis=1, keepdims=True)
+    until = jnp.sum(jnp.where((lane < both) | (place < edge + 2 * SLOTS), 1.0, 0.0), axis=1, keepdims=True)
+    low = jnp.sum(jnp.where(until <= half, 1.0, 0.0), axis=0, keepdims=True).astype(I32)
+    high = jnp.sum(jnp.where(before < 2 * half, 1.0, 0.0), axis=0, keepdims=True).astype(I32)
+    bounds[...] = jnp.broadcast_to(jnp.where(iota((8, 1), 0) == 0, low, high), bounds.shape)
     goals[...] = jnp.broadcast_to(jnp.where(iota((1, cap), 1) < both, -1, place), goals.shape)
 
 
@@ -519,6 +529,7 @@
             jax.ShapeDtypeStruct((cap // 128, 128), F32),
             jax.ShapeDtypeStruct((cap // 128, 128), F32),
             jax.ShapeDtypeStruct((cap // SLOTS, 128), I32),
+            jax.ShapeDtypeStruct((8, 128), I32),
             jax.ShapeDtypeStruct((8, cap), I32),
         ],
         in_specs=[spec(pltpu.VMEM)] * 7 + [spec(pl.ANY)] * 2,
@@ -528,6 +539,7 @@
             pl.BlockSpec((cap // 128, 128), lambda b: (0, 0)),
             pl.BlockSpec((cap // 128, 128), lambda b: (0, 0)),
             pl.BlockSpec((cap // SLOTS, 128), lambda b: (0, 0)),
+            pl.BlockSpec((8, 128), lambda b: (0, 0)),
             pl.BlockSpec((8, cap), lambda b: (0, 0)),
         ],
         input_output_aliases={7: 0, 8: 1},
@@ -561,72 +573,97 @@
     )(*pieces)
 
 
-def first_kernel(start, turned, shifts, goals, again, alone, first, middle, *refs):
+def first_kernel(late, start, bounds, turned, shifts, goals, again, alone, first, *refs):
+    middle, refs = (refs[0], refs[1:]) if late else (None, refs)
     hands, (held_in, one_in, two_in, held, one, two, x, out, sent) = refs[:HANDS], refs[HANDS:]
-    del one_in, two_in, held_in
-    part, width = middle.shape
+    del held_in
+    width = first.shape[1]
+    part = first.shape[0] - 16
+    pairs = 4 * part // (2 * SLOTS)
     x[0:part, :] = first[0:part, :]
-    x[part : 2 * part, :] = middle[...]
+    x[part : 2 * part, :] = middle[...] if late else jnp.zeros((part, width), BF)
     for h, hand in enumerate(hands):
         for turn in range(hand.shape[0] // 16):
             block = 2 * part + 16 * (h + HANDS * turn)
             x[block : block + 16, :] = hand[16 * turn : 16 * turn + 16, :]
+    if late:
+        one[...] = one_in[...]
+        two[...] = two_in[...]
+    else:
+        one[...] = jnp.zeros_like(one)
+        two[...] = jnp.zeros_like(two)
     span = SLOTS + 128
     base = 8 * part
     slot = iota((SLOTS, span), 0)
-    group = 4
-    stores = []
-    for k in range(4 * part // SLOTS):
-        begin = pl.multiple_of(start[k, 0], 128)
-        hot = as_bf(slot == goals[0:1, pl.ds(begin, span)] - k * SLOTS)
-        out[k * SLOTS : (k + 1) * SLOTS, :] = dot(hot, x[pl.ds(begin, span), :]).astype(BF)
-        if k % group == group - 1:
-            size = group * SLOTS
-            lines = pl.ds((k + 1) * SLOTS - size, size)
-            to = held.at[pl.ds(base + (k + 1) * SLOTS - size, size)]
-            stores.append(pltpu.make_async_copy(out.at[lines], to, sent.at[k // group]))
-            stores[-1].start()
-            score = scores(out[lines, :], turned[...])
-            m_one = margins(score, shifts[0:1, 0:1], 0, width)
-            m_two = margins(score, shifts[1:2, 0:1], 2, width)
-            for i in range(size // 128):
-                line = (k + 1) * SLOTS // 128 - size // 128 + i
-                line = slice(line, line + 1)
-                lanes = slice(128 * i, 128 * (i + 1))
-                one[line, :] = jnp.where(alone[line, :] > 0.5, m_one[:, lanes], again[line, :])
-                two[line, :] = jnp.where(alone[line, :] > 0.5, m_two[:, lanes], 0.0)
-    for store in stores:
-        store.wait()
-
-
-def first_call(start, turned, shifts, goals, again, alone, first, middle, hands, held, one, two):
+
+    def store(pair):
+        lines = pl.multiple_of(pair * 2 * SLOTS, 2 * SLOTS)
+        to = held.at[pl.ds(base + lines, 2 * SLOTS)]
+        return pltpu.make_async_copy(out.at[pl.ds(lines, 2 * SLOTS)], to, sent.at[pair])
+
+    def place(pair, _):
+        lines = pl.multiple_of(pair * 2 * SLOTS, 2 * SLOTS)
+        rows = []
+        for i in range(2):
+            begin = pl.multiple_of((start[2 * pair + i, 0] // 128) * 128, 128)
+            hot = as_bf(slot == goals[0:1, pl.ds(begin, span)] - (lines + i * SLOTS))
+            rows.append(dot(hot, x[pl.ds(begin, span), :]).astype(BF))
+        rows = jnp.concatenate(rows, axis=0)
+        out[pl.ds(lines, 2 * SLOTS), :] = rows
+        store(pair).start()
+        score = scores(rows, turned[...])
+        m_one = margins(score, shifts[0:1, 0:1], 0, width)
+        m_two = margins(score, shifts[1:2, 0:1], 2, width)
+        for i in range(2):
+            line = pl.ds(2 * pair + i, 1)
+            lanes = slice(SLOTS * i, SLOTS * (i + 1))
+            one[line, :] = jnp.where(alone[line, :] > 0.5, m_one[:, lanes], again[line, :])
+            two[line, :] = jnp.where(alone[line, :] > 0.5, m_two[:, lanes], 0.0)
+        return 0
+
+    def finish(pair, _):
+        store(pair).wait()
+        return 0
+
+    low = jnp.minimum(bounds[0, 0], pairs)
+    high = jnp.clip(bounds[1, 0], low, pairs)
+    ranges = [(low, high)] if late else [(0, low), (high, pairs)]
+    for work in (place, finish):
+        for begin, end in ranges:
+            lax.fori_loop(begin, end, work, 0)
+
+
+def first_call(start, bounds, turned, shifts, goals, again, alone, first, middle, hands, held, one, two):
     width = held.shape[1]
     cap = goals.shape[1]
     lines = cap // 128
-    return pl.pallas_call(
-        first_kernel,
+    late = middle is not None
+    pieces = [first, *([middle] if late else []), *hands]
+    block = pl.BlockSpec((lines, 128), lambda k: (2, 0))
+    given = 7 + len(pieces)
+    return pl.pallas_call(
+        functools.partial(first_kernel, late),
         grid=(1,),
         out_shape=[
             jax.ShapeDtypeStruct(held.shape, BF),
             jax.ShapeDtypeStruct(one.shape, F32),
             jax.ShapeDtypeStruct(two.shape, F32),
         ],
-        in_specs=[spec(pltpu.SMEM)] + [spec(pltpu.VMEM)] * (HANDS + 7) + [spec(pl.ANY)] * 3,
-        out_specs=[
-            spec(pl.ANY),
-            pl.BlockSpec((lines, 128), lambda k: (2, 0)),
-            pl.BlockSpec((lines, 128), lambda k: (2, 0)),
-        ],
+        in_specs=[spec(pltpu.SMEM)] * 2
+        + [spec(pltpu.VMEM)] * (given - 2)
+        + [spec(pl.ANY)]
+        + ([block] * 2 if late else [spec(pl.ANY)] * 2),
+        out_specs=[spec(pl.ANY), block, block],
         scratch_shapes=[
             pltpu.VMEM((cap, width), BF),
             pltpu.VMEM((cap, width), BF),
-            pltpu.SemaphoreType.DMA((cap // BLK,)),
-        ],
-        input_output_aliases={8 + HANDS: 0, 9 + HANDS: 1, 10 + HANDS: 2},
-        compiler_params=params(),
-        cost_estimate=pl.CostEstimate(flops=3 * 10**9, bytes_accessed=7 * 10**6, transcendentals=0),
-        name="first_slots",
-    )(start, turned, shifts, goals, again, alone, first, middle, *hands, held, one, two)
+            pltpu.SemaphoreType.DMA((cap // (2 * SLOTS),)),
+        ],
+        input_output_aliases={given: 0, given + 1: 1, given + 2: 2},
+        compiler_params=params(),
+        cost_estimate=pl.CostEstimate(flops=10**9, bytes_accessed=10**6, transcendentals=0),
+        name="last_slots" if late else "first_slots",
+    )(start, bounds, turned, shifts, goals, again, alone, *pieces, held, one, two)
 
 
 def local(vectors, child_labels):
@@ -679,12 +716,12 @@
         total = total + swap(total, bit)
         bit *= 2
     cents, turned, shifts, one, two = centre_call(here, total, child_labels, vectors)
-    held, two, again, alone, start, goals = second_call(
+    held, two, again, alone, start, bounds, goals = second_call(
         turned, shifts, second_in, relay, first_in, meta_in, counts[2], held, two
     )
-    held, one, two = first_call(
-        start, turned, shifts, goals, again, alone, first_in, middle_in, hands, held, one, two
-    )
+    known = start, bounds, turned, shifts, goals, again, alone, first_in
+    held, one, two = first_call(*known, None, hands, held, one, two)
+    held, one, two = first_call(*known, middle_in, hands, held, one, two)
     return held, one.reshape(-1), two.reshape(-1), cents
 
 

time: 140 us -> 144 us (1.029)
  Pallas kernels: 30.8 us -> 36.3 us
  waiting for transfers between devices: 69.3 us -> 67.5 us
    pallas_call x2 -> x3, Pallas kernels: 10.7 us -> 16.2 us  [the longest x2 9.85 us: first_call(): pl.pallas_call(functools.partial(first_kernel, late), grid=(1,), out_shap...]
    ppermute x26, waiting for transfers between devices: 69.3 us -> 67.5 us  [swap(): lax.ppermute(x, 'cube', [(i, i ^ bits) for i in range(lax.axis_size('cube...]
  transfers between devices with their start and end apart: 26 -> 26, of which waited for: 11 -> 8; matrix products, arithmetic and copies ran while one was open for 1% -> 1% of each run, Pallas kernels for 17% -> 21%
where the time goes in v1:
time: 144 us
  waiting for transfers between devices  67.5 us (47%)
  Pallas kernels  36.3 us (25%)
  starting transfers between devices  33.2 us (23%)
  local copies, waits for them, and re-layouts  5.37 us (4%)
  between operations  1.68 us (1%)
    ppermute x26, waiting for transfers between devices, swap(): lax.ppermute(x, 'cube', [(i, i ^ bits) for i in range(lax.axis_size('cube...  67.5 us
    ppermute x26, starting transfers between devices, swap(): lax.ppermute(x, 'cube', [(i, i ^ bits) for i in range(lax.axis_size('cube...  33.2 us
    pallas_call x2, Pallas kernels, first_call(): pl.pallas_call(functools.partial(first_kernel, late), grid=(1,), out_shap...  9.85 us
    pallas_call x1, Pallas kernels, centre_call(): pl.pallas_call(centre_kernel, grid=(1,), out_shape=[jax.ShapeDtypeStruct(...  6.3 us
    pallas_call x1, Pallas kernels, second_call(): pl.pallas_call(second_kernel, grid=(1,), out_shape=[jax.ShapeDtypeStruct(...  4.36 us
    pallas_call x1, Pallas kernels, own_call(): pl.pallas_call(own_kernel, grid=(rows // 1024,), out_shape=jax.ShapeDtype...  4.06 us
    pallas_call x1, Pallas kernels, sort_call(): pl.pallas_call(sort_kernel, out_shape=[jax.ShapeDtypeStruct((part + 16, w...  3.81 us
    unnamed x8, local copies, waits for them, and re-layouts  3.54 us
  transfers between devices with their start and end apart: 26, of which 8 were waited for; matrix products, arithmetic and copies ran while one was open for 1% of the time, Pallas kernels for 21%

profile of v1, /device:TPU:0, one launch (start us, length us, event | category | flops | bytes accessed | tf_op | source)
XLA Modules:
  0.0 144.2 jit_solution(14095281347910657493)
XLA Ops:
  2.4 5.1 %collective-permute-start.100 = (s32[8,128]{1,0:T(8,128)S(1)}, s32[8,128]{1,0:T(8,128)S(1)}, u32[]{:S(2)}, u32[]{:S(2)}) collective-permute-start(s32[8,128]{1,0:T(8,128)S(1)} %get-tuple-element.370.own), channel_id=1, source_target_pairs={{0,24},{1,25},{2,26},{3,27},{4,28},{5,29},{6,30},{7,31},{8,16},{9,... | collective-permute-start | bytes 12296 | tf_op jit(solution)/shard_map/ppermute | solution.py:20
  8.2 3.8 %sort_leavers.1 = (bf16[528,768]{1,0:T(8,128)(2,1)S(1)}, bf16[512,768]{1,0:T(8,128)(2,1)S(1)}, bf16[1024,768]{1,0:T(8,128)(2,1)S(1)}) custom-call(s32[2]{0:T(128)S(1)} %pad_add_fusion.here, s32[2,4096]{1,0:T(2,128)S(1)} %copy-done.2, s32[128,256]{1,0:T(8,128)S(1)} %get-tuple-element.382.pos_ref.pos, s32[128,128]{1,0:T(8,128)S(1)} %get-tuple-element.363.off_ref.off, ...), custom_call_target="tpu_custom_call" | custom-call | flops 8000000000 | bytes 10000000 | tf_op jit(solution)/shard_map/sort_leavers/pallas_call | solution.py:172
  12.0 2.3 %collective-permute-start.109 = (bf16[528,768]{1,0:T(8,128)(2,1)S(1)}, bf16[528,768]{1,0:T(8,128)(2,1)}, u32[]{:S(2)}, u32[]{:S(2)}) collective-permute-start(bf16[528,768]{1,0:T(8,128)(2,1)S(1)} %get-tuple-element.367.first.own), channel_id=1, source_target_pairs={{0,16},{1,17},{2,18},{3,19},{4,20},{5,21},{6,22},{7,23},{8,24},{9,... | collective-permute-start | bytes 2433032 | tf_op jit(solution)/shard_map/ppermute | solution.py:20
  14.3 1.5 %second_send.1 = bf16[528,768]{1,0:T(8,128)(2,1)S(1)} custom-call(s32[128,128]{1,0:T(8,128)S(1)} %get-tuple-element.363.off_ref.off, s32[128,256]{1,0:T(8,128)S(1)} %get-tuple-element.382.pos_ref.pos, bf16[528,768]{1,0:T(8,128)(2,1)S(1)} %get-tuple-element.367.first.own, bf16[4096,768]{1,0:T(8,128)(2,1)S(1)} %copy-done), custom_call_target="tpu_custom_call" | custom-call | flops 100000000 | bytes 1000000 | tf_op jit(solution)/shard_map/second_send/pallas_call | solution.py:318
  16.1 1.6 %collective-permute-start.103 = (bf16[144,768]{1,0:T(8,128)(2,1)S(1)}, bf16[144,768]{1,0:T(8,128)(2,1)S(1)}, u32[]{:S(2)}, u32[]{:S(2)}) collective-permute-start(bf16[144,768]{1,0:T(8,128)(2,1)S(1)} %get-tuple-element.377), channel_id=1, source_target_pairs={{0,2},{1,3},{2,0},{3,1},{4,6},{5,7},{6,4},{7,5},{8,10},{9,11},{10,... | collective-permute-start | bytes 663560 | tf_op jit(solution)/shard_map/ppermute | solution.py:20
  17.9 2.4 %collective-permute-start.108 = (bf16[144,768]{1,0:T(8,128)(2,1)S(1)}, bf16[144,768]{1,0:T(8,128)(2,1)S(1)}, u32[]{:S(2)}, u32[]{:S(2)}) collective-permute-start(bf16[144,768]{1,0:T(8,128)(2,1)S(1)} %get-tuple-element.383), channel_id=1, source_target_pairs={{0,7},{1,6},{2,5},{3,4},{4,3},{5,2},{6,1},{7,0},{8,15},{9,14},{10,... | collective-permute-start | bytes 663560 | tf_op jit(solution)/shard_map/ppermute | solution.py:20
  20.3 2.0 %collective-permute-start.101 = (bf16[528,768]{1,0:T(8,128)(2,1)S(1)}, bf16[528,768]{1,0:T(8,128)(2,1)S(1)}, u32[]{:S(2)}, u32[]{:S(2)}) collective-permute-start(bf16[528,768]{1,0:T(8,128)(2,1)S(1)} %second_send.1), channel_id=1, source_target_pairs={{0,8},{1,9},{2,10},{3,11},{4,12},{5,13},{6,14},{7,15},{8,0},{9,1},... | collective-permute-start | bytes 2433032 | tf_op jit(solution)/shard_map/ppermute | solution.py:20
  22.4 2.0 %collective-permute-done.103.refs_2_ = bf16[144,768]{1,0:T(8,128)(2,1)S(1)} collective-permute-done((bf16[144,768]{1,0:T(8,128)(2,1)S(1)}, bf16[144,768]{1,0:T(8,128)(2,1)S(1)}, u32[]{:S(2)}, u32[]{:S(2)}) %collective-permute-start.103) | collective-permute-done | bytes 221216 | tf_op jit(solution)/shard_map/ppermute | solution.py:20
  24.4 1.5 %collective-permute-start.105 = (bf16[144,768]{1,0:T(8,128)(2,1)S(1)}, bf16[144,768]{1,0:T(8,128)(2,1)S(1)}, u32[]{:S(2)}, u32[]{:S(2)}) collective-permute-start(bf16[144,768]{1,0:T(8,128)(2,1)S(1)} %get-tuple-element.379), channel_id=1, source_target_pairs={{0,4},{1,5},{2,6},{3,7},{4,0},{5,1},{6,2},{7,3},{8,12},{9,13},{10,... | collective-permute-start | bytes 663560 | tf_op jit(solution)/shard_map/ppermute | solution.py:20
  25.9 2.3 %collective-permute-done.104.refs_3_ = bf16[144,768]{1,0:T(8,128)(2,1)S(1)} collective-permute-done((bf16[144,768]{1,0:T(8,128)(2,1)S(1)}, bf16[144,768]{1,0:T(8,128)(2,1)S(1)}, u32[]{:S(2)}, u32[]{:S(2)}) %collective-permute-start.104) | collective-permute-done | bytes 221216 | tf_op jit(solution)/shard_map/ppermute | solution.py:20
  28.2 2.1 %collective-permute-start.106 = (bf16[144,768]{1,0:T(8,128)(2,1)S(1)}, bf16[144,768]{1,0:T(8,128)(2,1)S(1)}, u32[]{:S(2)}, u32[]{:S(2)}) collective-permute-start(bf16[144,768]{1,0:T(8,128)(2,1)S(1)} %get-tuple-element.380), channel_id=1, source_target_pairs={{0,5},{1,4},{2,7},{3,6},{4,1},{5,0},{6,3},{7,2},{8,13},{9,12},{10,... | collective-permute-start | bytes 663560 | tf_op jit(solution)/shard_map/ppermute | solution.py:20
  30.3 3.6 %collective-permute-done.108.refs_7_ = bf16[144,768]{1,0:T(8,128)(2,1)S(1)} collective-permute-done((bf16[144,768]{1,0:T(8,128)(2,1)S(1)}, bf16[144,768]{1,0:T(8,128)(2,1)S(1)}, u32[]{:S(2)}, u32[]{:S(2)}) %collective-permute-start.108) | collective-permute-done | bytes 221216 | tf_op jit(solution)/shard_map/ppermute | solution.py:20
  34.0 1.4 collective-permute-start.107
  35.4 2.0 %list_ranks.1 = s32[8,256]{1,0:T(8,128)S(1)} custom-call(s32[128,128]{1,0:T(8,128)S(1)} %get-tuple-element.363.off_ref.off, s32[128,256]{1,0:T(8,128)S(1)} %get-tuple-element.382.pos_ref.pos), custom_call_target="tpu_custom_call" | custom-call | flops 100000000 | bytes 1000000 | tf_op jit(solution)/shard_map/list_ranks/pallas_call | solution.py:353
  37.4 4.1 %own_slots.1.held_in = bf16[7168,768]{1,0:T(8,128)(2,1)} custom-call(s32[128,256]{1,0:T(8,128)S(1)} %get-tuple-element.382.pos_ref.pos, bf16[4096,768]{1,0:T(8,128)(2,1)S(1)} %copy-done), custom_call_target="tpu_custom_call" | custom-call | flops 100000000 | bytes 1000000 | tf_op jit(solution)/shard_map/own_slots/pallas_call | solution.py:375
  41.5 2.7 %collective-permute-done.106.refs_5_ = bf16[144,768]{1,0:T(8,128)(2,1)S(1)} collective-permute-done((bf16[144,768]{1,0:T(8,128)(2,1)S(1)}, bf16[144,768]{1,0:T(8,128)(2,1)S(1)}, u32[]{:S(2)}, u32[]{:S(2)}) %collective-permute-start.106) | collective-permute-done | bytes 221216 | tf_op jit(solution)/shard_map/ppermute | solution.py:20
  45.7 4.1 %collective-permute-done.109.b.first = bf16[528,768]{1,0:T(8,128)(2,1)} collective-permute-done((bf16[528,768]{1,0:T(8,128)(2,1)S(1)}, bf16[528,768]{1,0:T(8,128)(2,1)}, u32[]{:S(2)}, u32[]{:S(2)}) %collective-permute-start.109) | collective-permute-done | bytes 811040 | tf_op jit(solution)/shard_map/ppermute | solution.py:20
  49.8 50.6 %conditional.1 = (bf16[1024,768]{1,0:T(8,128)(2,1)}, bf16[528,768]{1,0:T(8,128)(2,1)}, s32[8,256]{1,0:T(8,128)}) conditional(s32[]{:T(128)} %bitcast.2, (bf16[528,768]{1,0:T(8,128)(2,1)}, s32[8,256]{1,0:T(8,128)S(1)}) %tuple.152, (bf16[1024,768]{1,0:T(8,128)(2,1)S(1)}, bf16[528,768]{1,0:T(8,128)(2,1)}, ...), branch_computations={%region_0.1_spmd, %region_1.2_spmd, %region_2.3_spmd, %region_3.4_... | conditional | bytes 15515794 | solution.py:707
  50.0 3.7 %collective-permute-start.66 = (bf16[528,768]{1,0:T(8,128)(2,1)}, bf16[528,768]{1,0:T(8,128)(2,1)}, u32[]{:S(2)}, u32[]{:S(2)}) collective-permute-start(bf16[528,768]{1,0:T(8,128)(2,1)} %get-tuple-element.262), channel_id=1, source_target_pairs={{0,8},{1,9},{2,10},{3,11},{4,12},{5,13},{6,14},{7,15},{8,0},{9,1},... | collective-permute-start | bytes 2433032 | tf_op jit(solution)/shard_map/cond/branch_22_fun/ppermute | solution.py:20
  53.8 45.3 %collective-permute-done.65 = bf16[704,768]{1,0:T(8,128)(2,1)S(1)} collective-permute-done((bf16[704,768]{1,0:T(8,128)(2,1)S(1)}, bf16[704,768]{1,0:T(8,128)(2,1)S(1)}, u32[]{:S(2)}, u32[]{:S(2)}) %collective-permute-start.65) | collective-permute-done | bytes 1081376 | tf_op jit(solution)/shard_map/cond/branch_22_fun/ppermute | solution.py:20
  100.4 2.1 %part_pack.1 = (bf16[128,768]{1,0:T(8,128)(2,1)S(1)}, bf16[128,768]{1,0:T(8,128)(2,1)S(1)}, bf16[128,768]{1,0:T(8,128)(2,1)S(1)}, bf16[128,768]{1,0:T(8,128)(2,1...) custom-call(s32[8,128]{1,0:T(8,128)S(1)} %get-tuple-element.385.begi, ...), custom_call_target="tpu_custom_call" | custom-call | bytes 3000000 | tf_op jit(solution)/shard_map/part_pack/pallas_call | solution.py:275
  102.6 1.6 %collective-permute-start.115 = (bf16[128,768]{1,0:T(8,128)(2,1)S(1)}, bf16[128,768]{1,0:T(8,128)(2,1)S(1)}, u32[]{:S(2)}, u32[]{:S(2)}) collective-permute-start(bf16[128,768]{1,0:T(8,128)(2,1)S(1)} %get-tuple-element.410), channel_id=1, source_target_pairs={{0,2},{1,3},{2,0},{3,1},{4,6},{5,7},{6,4},{7,5},{8,10},{9,11},{10,... | collective-permute-start | bytes 589832 | tf_op jit(solution)/shard_map/ppermute | solution.py:20
  106.5 1.5 %collective-permute-start.112 = (f32[8,768]{1,0:T(8,128)S(1)}, f32[8,768]{1,0:T(8,128)S(1)}, u32[]{:S(2)}, u32[]{:S(2)}) collective-permute-start(f32[8,768]{1,0:T(8,128)S(1)} %add.73), channel_id=1, source_target_pairs={{0,2},{1,3},{2,0},{3,1},{4,6},{5,7},{6,4},{7,5},{8,10},{9,11},{10,... | collective-permute-start | bytes 73736 | tf_op jit(solution)/shard_map/ppermute | solution.py:20
  108.1 6.6 %collective-permute-done.112 = f32[8,768]{1,0:T(8,128)S(1)} collective-permute-done((f32[8,768]{1,0:T(8,128)S(1)}, f32[8,768]{1,0:T(8,128)S(1)}, u32[]{:S(2)}, u32[]{:S(2)}) %collective-permute-start.112) | collective-permute-done | bytes 24608 | tf_op jit(solution)/shard_map/ppermute | solution.py:20
  114.7 1.6 %collective-permute-start.113 = (f32[8,768]{1,0:T(8,128)S(1)}, f32[8,768]{1,0:T(8,128)S(1)}, u32[]{:S(2)}, u32[]{:S(2)}) collective-permute-start(f32[8,768]{1,0:T(8,128)S(1)} %add.74), channel_id=1, source_target_pairs={{0,4},{1,5},{2,6},{3,7},{4,0},{5,1},{6,2},{7,3},{8,12},{9,13},{10,... | collective-permute-start | bytes 73736 | tf_op jit(solution)/shard_map/ppermute | solution.py:20
  116.7 2.5 %collective-permute-start.119 = (bf16[128,768]{1,0:T(8,128)(2,1)S(1)}, bf16[128,768]{1,0:T(8,128)(2,1)S(1)}, u32[]{:S(2)}, u32[]{:S(2)}) collective-permute-start(bf16[128,768]{1,0:T(8,128)(2,1)S(1)} %get-tuple-element.414), channel_id=1, source_target_pairs={{0,6},{1,7},{2,4},{3,5},{4,2},{5,3},{6,0},{7,1},{8,14},{9,15},{10,... | collective-permute-start | bytes 589832 | tf_op jit(solution)/shard_map/ppermute | solution.py:20
  119.2 1.4 collective-permute-start.120
  120.7 2.8 %copy-done.1 = bf16[4096,768]{1,0:T(8,128)(2,1)S(1)} copy-done((bf16[4096,768]{1,0:T(8,128)(2,1)S(1)}, bf16[4096,768]{1,0:T(8,128)(2,1)}, u32[]{:S(2)}) %copy-start.1) | copy-done | bytes 6291480
  123.4 6.3 %own_margins.1 = (f32[6,768]{1,0:T(8,128)}, bf16[768,128]{1,0:T(8,128)(2,1)S(1)}, f32[8,128]{1,0:T(8,128)S(1)}, f32[48,128]{1,0:T(8,128)}, f32[56,128]{1,0:T(8,128)}) custom-call(s32[2]{0:T(128)S(1)} %pad_add_fusion.here, f32[8,768]{1,0:T(8,128)S(1)} %add.75.total, s32[2,4096]{1,0:T(2,128)S(1)} %copy-done.3, bf16[4096,768]{1,0:T(8,128)(2,1)S(1)} %copy-done.1), custom_call_target="tpu_custom_call" | custom-call | flops 100000000 | bytes 100000 | tf_op jit(solution)/shard_map/own_margins/pallas_call | solution.py:445
  129.7 4.4 %second_slots.1 = (bf16[7168,768]{1,0:T(8,128)(2,1)}, f32[56,128]{1,0:T(8,128)}, f32[16,128]{1,0:T(8,128)S(1)}, f32[16,128]{1,0:T(8,128)S(1)}, s32[16,128]{1,0:T...) custom-call(bf16[768,128]{1,0:T(8,128)(2,1)S(1)} %get-tuple-element.397.tu, ...), custom_call_target="tpu_custom_call", output_to_operand_aliasing={{0}: (7, {}), {1}: (8, {})} | custom-call | flops 100000000 | bytes 100000 | tf_op jit(solution)/shard_map/second_slots/pallas_call | solution.py:523
  134.2 4.9 %first_slots.1 = (bf16[7168,768]{1,0:T(8,128)(2,1)}, f32[48,128]{1,0:T(8,128)}, f32[56,128]{1,0:T(8,128)}) custom-call(s32[16,128]{1,0:T(8,128)S(1)} %get-tuple-element.402.start, s32[8,128]{1,0:T(8,128)S(1)} %get-tuple-element.403.bounds, ...), custom_call_target="tpu_custom_call", output_to_operand_aliasing={{0}: (16, {}), {1}: (17, {}), {2}: (18, {})} | custom-call | flops 1000000000 | bytes 1000000 | tf_op jit(solution)/shard_map/first_slots/pallas_call | solution.py:644
  139.1 4.9 %last_slots.1 = (bf16[7168,768]{1,0:T(8,128)(2,1)}, f32[48,128]{1,0:T(8,128)}, f32[56,128]{1,0:T(8,128)}) custom-call(s32[16,128]{1,0:T(8,128)S(1)} %get-tuple-element.402.start, s32[8,128]{1,0:T(8,128)S(1)} %get-tuple-element.403.bounds, ...), custom_call_target="tpu_custom_call", output_to_operand_aliasing={{0}: (17, {}), {1}: (18, {}), {2}: (19, {})} | custom-call | flops 1000000000 | bytes 1000000 | tf_op jit(solution)/shard_map/last_slots/pallas_call | solution.py:644
  (49 shorter events, 8.2 us)
Async XLA Ops:
  0.7 0.8 copy-start.2
  1.5 6.7 %copy-start = (bf16[4096,768]{1,0:T(8,128)(2,1)S(1)}, bf16[4096,768]{1,0:T(8,128)(2,1)}, u32[]{:S(2)}) copy-start(bf16[4096,768]{1,0:T(8,128)(2,1)} %x_hbm.1) | copy-start | bytes 18874372
  2.4 9.6 %collective-permute-start.100 = (s32[8,128]{1,0:T(8,128)S(1)}, s32[8,128]{1,0:T(8,128)S(1)}, u32[]{:S(2)}, u32[]{:S(2)}) collective-permute-start(s32[8,128]{1,0:T(8,128)S(1)} %get-tuple-element.370.own), channel_id=1, source_target_pairs={{0,24},{1,25},{2,26},{3,27},{4,28},{5,29},{6,30},{7,31},{8,16},{9,... | collective-permute-start | bytes 12296 | tf_op jit(solution)/shard_map/ppermute | solution.py:20
  7.5 4.5 %collective-permute-start.99 = (s32[8,128]{1,0:T(8,128)S(1)}, s32[8,128]{1,0:T(8,128)S(1)}, u32[]{:S(2)}, u32[]{:S(2)}) collective-permute-start(s32[8,128]{1,0:T(8,128)S(1)} %get-tuple-element.370.own), channel_id=1, source_target_pairs={{0,16},{1,17},{2,18},{3,19},{4,20},{5,21},{6,22},{7,23},{8,24},{9,... | collective-permute-start | bytes 12296 | tf_op jit(solution)/shard_map/ppermute | solution.py:20
  7.5 4.5 %collective-permute-start.98 = (s32[8,128]{1,0:T(8,128)S(1)}, s32[8,128]{1,0:T(8,128)S(1)}, u32[]{:S(2)}, u32[]{:S(2)}) collective-permute-start(s32[8,128]{1,0:T(8,128)S(1)} %get-tuple-element.370.own), channel_id=1, source_target_pairs={{0,8},{1,9},{2,10},{3,11},{4,12},{5,13},{6,14},{7,15},{8,0},{9,1},... | collective-permute-start | bytes 12296 | tf_op jit(solution)/shard_map/ppermute | solution.py:20
  12.0 37.8 %collective-permute-start.109 = (bf16[528,768]{1,0:T(8,128)(2,1)S(1)}, bf16[528,768]{1,0:T(8,128)(2,1)}, u32[]{:S(2)}, u32[]{:S(2)}) collective-permute-start(bf16[528,768]{1,0:T(8,128)(2,1)S(1)} %get-tuple-element.367.first.own), channel_id=1, source_target_pairs={{0,16},{1,17},{2,18},{3,19},{4,20},{5,21},{6,22},{7,23},{8,24},{9,... | collective-permute-start | bytes 2433032 | tf_op jit(solution)/shard_map/ppermute | solution.py:20
  16.0 4.4 %collective-permute-start.102 = (bf16[144,768]{1,0:T(8,128)(2,1)S(1)}, bf16[144,768]{1,0:T(8,128)(2,1)S(1)}, u32[]{:S(2)}, u32[]{:S(2)}) collective-permute-start(bf16[144,768]{1,0:T(8,128)(2,1)S(1)} %get-tuple-element.375), channel_id=1, source_target_pairs={{0,1},{1,0},{2,3},{3,2},{4,5},{5,4},{6,7},{7,6},{8,9},{9,8},{10,11... | collective-permute-start | bytes 663560 | tf_op jit(solution)/shard_map/ppermute | solution.py:20
  16.1 8.3 %collective-permute-start.103 = (bf16[144,768]{1,0:T(8,128)(2,1)S(1)}, bf16[144,768]{1,0:T(8,128)(2,1)S(1)}, u32[]{:S(2)}, u32[]{:S(2)}) collective-permute-start(bf16[144,768]{1,0:T(8,128)(2,1)S(1)} %get-tuple-element.377), channel_id=1, source_target_pairs={{0,2},{1,3},{2,0},{3,1},{4,6},{5,7},{6,4},{7,5},{8,10},{9,11},{10,... | collective-permute-start | bytes 663560 | tf_op jit(solution)/shard_map/ppermute | solution.py:20
  17.6 10.6 %collective-permute-start.104 = (bf16[144,768]{1,0:T(8,128)(2,1)S(1)}, bf16[144,768]{1,0:T(8,128)(2,1)S(1)}, u32[]{:S(2)}, u32[]{:S(2)}) collective-permute-start(bf16[144,768]{1,0:T(8,128)(2,1)S(1)} %get-tuple-element.378), channel_id=1, source_target_pairs={{0,3},{1,2},{2,1},{3,0},{4,7},{5,6},{6,5},{7,4},{8,11},{9,10},{10,... | collective-permute-start | bytes 663560 | tf_op jit(solution)/shard_map/ppermute | solution.py:20
  17.9 16.1 %collective-permute-start.108 = (bf16[144,768]{1,0:T(8,128)(2,1)S(1)}, bf16[144,768]{1,0:T(8,128)(2,1)S(1)}, u32[]{:S(2)}, u32[]{:S(2)}) collective-permute-start(bf16[144,768]{1,0:T(8,128)(2,1)S(1)} %get-tuple-element.383), channel_id=1, source_target_pairs={{0,7},{1,6},{2,5},{3,4},{4,3},{5,2},{6,1},{7,0},{8,15},{9,14},{10,... | collective-permute-start | bytes 663560 | tf_op jit(solution)/shard_map/ppermute | solution.py:20
  20.3 84.1 %collective-permute-start.101 = (bf16[528,768]{1,0:T(8,128)(2,1)S(1)}, bf16[528,768]{1,0:T(8,128)(2,1)S(1)}, u32[]{:S(2)}, u32[]{:S(2)}) collective-permute-start(bf16[528,768]{1,0:T(8,128)(2,1)S(1)} %second_send.1), channel_id=1, source_target_pairs={{0,8},{1,9},{2,10},{3,11},{4,12},{5,13},{6,14},{7,15},{8,0},{9,1},... | collective-permute-start | bytes 2433032 | tf_op jit(solution)/shard_map/ppermute | solution.py:20
  24.4 17.1 %collective-permute-start.105 = (bf16[144,768]{1,0:T(8,128)(2,1)S(1)}, bf16[144,768]{1,0:T(8,128)(2,1)S(1)}, u32[]{:S(2)}, u32[]{:S(2)}) collective-permute-start(bf16[144,768]{1,0:T(8,128)(2,1)S(1)} %get-tuple-element.379), channel_id=1, source_target_pairs={{0,4},{1,5},{2,6},{3,7},{4,0},{5,1},{6,2},{7,3},{8,12},{9,13},{10,... | collective-permute-start | bytes 663560 | tf_op jit(solution)/shard_map/ppermute | solution.py:20
  28.2 16.0 %collective-permute-start.106 = (bf16[144,768]{1,0:T(8,128)(2,1)S(1)}, bf16[144,768]{1,0:T(8,128)(2,1)S(1)}, u32[]{:S(2)}, u32[]{:S(2)}) collective-permute-start(bf16[144,768]{1,0:T(8,128)(2,1)S(1)} %get-tuple-element.380), channel_id=1, source_target_pairs={{0,5},{1,4},{2,7},{3,6},{4,1},{5,0},{6,3},{7,2},{8,13},{9,12},{10,... | collective-permute-start | bytes 663560 | tf_op jit(solution)/shard_map/ppermute | solution.py:20
  34.0 10.2 %collective-permute-start.107 = (bf16[144,768]{1,0:T(8,128)(2,1)S(1)}, bf16[144,768]{1,0:T(8,128)(2,1)S(1)}, u32[]{:S(2)}, u32[]{:S(2)}) collective-permute-start(bf16[144,768]{1,0:T(8,128)(2,1)S(1)} %get-tuple-element.381), channel_id=1, source_target_pairs={{0,6},{1,7},{2,4},{3,5},{4,2},{5,3},{6,0},{7,1},{8,14},{9,15},{10,... | collective-permute-start | bytes 663560 | tf_op jit(solution)/shard_map/ppermute | solution.py:20
  49.9 49.2 %collective-permute-start.65 = (bf16[704,768]{1,0:T(8,128)(2,1)S(1)}, bf16[704,768]{1,0:T(8,128)(2,1)S(1)}, u32[]{:S(2)}, u32[]{:S(2)}) collective-permute-start(bf16[704,768]{1,0:T(8,128)(2,1)S(1)} %slice.85), channel_id=1, source_target_pairs={{0,16},{1,17},{2,18},{3,19},{4,20},{5,21},{6,22},{7,23},{8,24},{9,... | collective-permute-start | bytes 3244040 | tf_op jit(solution)/shard_map/cond/branch_22_fun/ppermute | solution.py:20
  50.0 50.4 %collective-permute-start.66 = (bf16[528,768]{1,0:T(8,128)(2,1)}, bf16[528,768]{1,0:T(8,128)(2,1)}, u32[]{:S(2)}, u32[]{:S(2)}) collective-permute-start(bf16[528,768]{1,0:T(8,128)(2,1)} %get-tuple-element.262), channel_id=1, source_target_pairs={{0,8},{1,9},{2,10},{3,11},{4,12},{5,13},{6,14},{7,15},{8,0},{9,1},... | collective-permute-start | bytes 2433032 | tf_op jit(solution)/shard_map/cond/branch_22_fun/ppermute | solution.py:20
  53.7 46.6 %collective-permute-start.67 = (s32[8,256]{1,0:T(8,128)S(1)}, s32[8,256]{1,0:T(8,128)}, u32[]{:S(2)}, u32[]{:S(2)}) collective-permute-start(s32[8,256]{1,0:T(8,128)S(1)} %get-tuple-element.263), channel_id=1, source_target_pairs={{0,16},{1,17},{2,18},{3,19},{4,20},{5,21},{6,22},{7,23},{8,24},{9,... | collective-permute-start | bytes 24584 | tf_op jit(solution)/shard_map/cond/branch_22_fun/ppermute | solution.py:20
  100.4 38.7 %collective-permute-start.114 = (bf16[512,768]{1,0:T(8,128)(2,1)S(1)}, bf16[512,768]{1,0:T(8,128)(2,1)S(1)}, u32[]{:S(2)}, u32[]{:S(2)}) collective-permute-start(bf16[512,768]{1,0:T(8,128)(2,1)S(1)} %get-tuple-element.407), channel_id=1, source_target_pairs={{0,16},{1,17},{2,18},{3,19},{4,20},{5,21},{6,22},{7,23},{8,24},{9,... | collective-permute-start | bytes 2359304 | tf_op jit(solution)/shard_map/ppermute | solution.py:20
  102.5 1.9 %collective-permute-start.110 = (bf16[128,768]{1,0:T(8,128)(2,1)S(1)}, bf16[128,768]{1,0:T(8,128)(2,1)S(1)}, u32[]{:S(2)}, u32[]{:S(2)}) collective-permute-start(bf16[128,768]{1,0:T(8,128)(2,1)S(1)} %get-tuple-element.394), channel_id=1, source_target_pairs={{0,1},{1,0},{2,3},{3,2},{4,5},{5,4},{6,7},{7,6},{8,9},{9,8},{10,11... | collective-permute-start | bytes 589832 | tf_op jit(solution)/shard_map/ppermute | solution.py:20
  102.6 14.1 %collective-permute-start.115 = (bf16[128,768]{1,0:T(8,128)(2,1)S(1)}, bf16[128,768]{1,0:T(8,128)(2,1)S(1)}, u32[]{:S(2)}, u32[]{:S(2)}) collective-permute-start(bf16[128,768]{1,0:T(8,128)(2,1)S(1)} %get-tuple-element.410), channel_id=1, source_target_pairs={{0,2},{1,3},{2,0},{3,1},{4,6},{5,7},{6,4},{7,5},{8,10},{9,11},{10,... | collective-permute-start | bytes 589832 | tf_op jit(solution)/shard_map/ppermute | solution.py:20
  104.2 12.5 %collective-permute-start.116 = (bf16[128,768]{1,0:T(8,128)(2,1)S(1)}, bf16[128,768]{1,0:T(8,128)(2,1)S(1)}, u32[]{:S(2)}, u32[]{:S(2)}) collective-permute-start(bf16[128,768]{1,0:T(8,128)(2,1)S(1)} %get-tuple-element.411), channel_id=1, source_target_pairs={{0,3},{1,2},{2,1},{3,0},{4,7},{5,6},{6,5},{7,4},{8,11},{9,10},{10,... | collective-permute-start | bytes 589832 | tf_op jit(solution)/shard_map/ppermute | solution.py:20
  104.5 16.2 %copy-start.3 = (s32[2,4096]{1,0:T(2,128)S(1)}, s32[2,4096]{1,0:T(2,128)}, u32[]{:S(2)}) copy-start(s32[2,4096]{1,0:T(2,128)} %labels.5) | copy-start | bytes 98308
  105.3 1.2 collective-permute-start.111
  106.5 8.1 %collective-permute-start.112 = (f32[8,768]{1,0:T(8,128)S(1)}, f32[8,768]{1,0:T(8,128)S(1)}, u32[]{:S(2)}, u32[]{:S(2)}) collective-permute-start(f32[8,768]{1,0:T(8,128)S(1)} %add.73), channel_id=1, source_target_pairs={{0,2},{1,3},{2,0},{3,1},{4,6},{5,7},{6,4},{7,5},{8,10},{9,11},{10,... | collective-permute-start | bytes 73736 | tf_op jit(solution)/shard_map/ppermute | solution.py:20
  114.7 4.5 %collective-permute-start.113 = (f32[8,768]{1,0:T(8,128)S(1)}, f32[8,768]{1,0:T(8,128)S(1)}, u32[]{:S(2)}, u32[]{:S(2)}) collective-permute-start(f32[8,768]{1,0:T(8,128)S(1)} %add.74), channel_id=1, source_target_pairs={{0,4},{1,5},{2,6},{3,7},{4,0},{5,1},{6,2},{7,3},{8,12},{9,13},{10,... | collective-permute-start | bytes 73736 | tf_op jit(solution)/shard_map/ppermute | solution.py:20
  116.2 17.9 %collective-permute-start.117 = (bf16[128,768]{1,0:T(8,128)(2,1)S(1)}, bf16[128,768]{1,0:T(8,128)(2,1)S(1)}, u32[]{:S(2)}, u32[]{:S(2)}) collective-permute-start(bf16[128,768]{1,0:T(8,128)(2,1)S(1)} %get-tuple-element.412), channel_id=1, source_target_pairs={{0,4},{1,5},{2,6},{3,7},{4,0},{5,1},{6,2},{7,3},{8,12},{9,13},{10,... | collective-permute-start | bytes 589832 | tf_op jit(solution)/shard_map/ppermute | solution.py:20
  116.7 17.4 %collective-permute-start.118 = (bf16[128,768]{1,0:T(8,128)(2,1)S(1)}, bf16[128,768]{1,0:T(8,128)(2,1)S(1)}, u32[]{:S(2)}, u32[]{:S(2)}) collective-permute-start(bf16[128,768]{1,0:T(8,128)(2,1)S(1)} %get-tuple-element.413), channel_id=1, source_target_pairs={{0,5},{1,4},{2,7},{3,6},{4,1},{5,0},{6,3},{7,2},{8,13},{9,12},{10,... | collective-permute-start | bytes 589832 | tf_op jit(solution)/shard_map/ppermute | solution.py:20
  116.7 17.4 %collective-permute-start.119 = (bf16[128,768]{1,0:T(8,128)(2,1)S(1)}, bf16[128,768]{1,0:T(8,128)(2,1)S(1)}, u32[]{:S(2)}, u32[]{:S(2)}) collective-permute-start(bf16[128,768]{1,0:T(8,128)(2,1)S(1)} %get-tuple-element.414), channel_id=1, source_target_pairs={{0,6},{1,7},{2,4},{3,5},{4,2},{5,3},{6,0},{7,1},{8,14},{9,15},{10,... | collective-permute-start | bytes 589832 | tf_op jit(solution)/shard_map/ppermute | solution.py:20
  119.2 15.0 %collective-permute-start.120 = (bf16[128,768]{1,0:T(8,128)(2,1)S(1)}, bf16[128,768]{1,0:T(8,128)(2,1)S(1)}, u32[]{:S(2)}, u32[]{:S(2)}) collective-permute-start(bf16[128,768]{1,0:T(8,128)(2,1)S(1)} %get-tuple-element.415), channel_id=1, source_target_pairs={{0,7},{1,6},{2,5},{3,4},{4,3},{5,2},{6,1},{7,0},{8,15},{9,14},{10,... | collective-permute-start | bytes 589832 | tf_op jit(solution)/shard_map/ppermute | solution.py:20
  120.6 2.8 %copy-start.1 = (bf16[4096,768]{1,0:T(8,128)(2,1)S(1)}, bf16[4096,768]{1,0:T(8,128)(2,1)}, u32[]{:S(2)}) copy-start(bf16[4096,768]{1,0:T(8,128)(2,1)} %x_hbm.1) | copy-start | bytes 18874372

commit v2 on v1

--- a/solution.py
+++ b/solution.py
@@ -279,7 +279,7 @@
         out_specs=[spec(pl.ANY)] * HANDS,
         scratch_shapes=[pltpu.SemaphoreType.DMA((HANDS,))],
         compiler_params=params(),
-        cost_estimate=pl.CostEstimate(flops=0, bytes_accessed=3 * 10**6, transcendentals=0),
+        cost_estimate=pl.CostEstimate(flops=2 * 10**10, bytes_accessed=3 * 10**6, transcendentals=0),
         name="part_pack",
     )(begins, pack_in)
 
@@ -403,15 +403,74 @@
         ref[start + k : start + k + 1, :] = values[:, 128 * k : 128 * (k + 1)]
 
 
-def centre_kernel(here, total, labels, x_hbm, cents, turned, shifts, one, two, x, sem):
+def split(values):
+    terms = []
+    for value in values:
+        high = value.astype(BF).astype(F32)
+        middle = (value - high).astype(BF).astype(F32)
+        terms += [high, middle, value - high - middle]
+    return jnp.concatenate(terms + [jnp.zeros((16 - len(terms), values[0].shape[1]), F32)], axis=0).astype(BF)
+
+
+def second_kernel(second, relay, first, meta, held_in, held, copy, known, start, bounds, goals):
+    del held_in
+    half = second.shape[0] - 16
+    slots = held.shape[0]
+    cap = 2 * slots
+    have = count_at(second[half:, :], 5)
+    more = count_at(relay[half:, :], 4)
+    both = count_at(first[half:, :], 4)
+    lane = iota((1, half), 1)
+    goal = jnp.where(lane < more, lane + have, -1)
+    moved = dot(as_bf(iota((slots, half), 0) == goal), relay[0:half, :]).astype(BF)
+    held[0:half, :] = moved[0:half] + second[0:half, :]
+    held[half:, :] = moved[half:]
+    copy[...] = held[...]
+    known[...] = jnp.broadcast_to(jnp.where(iota((8, 1), 0) == 0, have + more, both), known.shape)
+    place = jnp.concatenate([meta[k : k + 1, :] for k in range(8)], axis=1)
+    lines = cap // SLOTS
+    own = iota((1, cap), 1) < both
+    edge = SLOTS * iota((lines, cap), 0)
+    before = jnp.sum(jnp.where(own | (place < edge), 1.0, 0.0), axis=1, keepdims=True)
+    begin = jnp.minimum((before.astype(I32) >> 7) << 7, cap - SLOTS - 128)
+    start[...] = jnp.broadcast_to(begin, start.shape)
+    edge = 2 * SLOTS * iota((lines // 2, cap), 0)
+    before = jnp.sum(jnp.where(own | (place < edge), 1.0, 0.0), axis=1, keepdims=True)
+    until = jnp.sum(jnp.where(own | (place < edge + 2 * SLOTS), 1.0, 0.0), axis=1, keepdims=True)
+    low = jnp.sum(jnp.where(until <= half, 1.0, 0.0), axis=0, keepdims=True).astype(I32)
+    high = jnp.sum(jnp.where(before < 2 * half, 1.0, 0.0), axis=0, keepdims=True).astype(I32)
+    bounds[...] = jnp.broadcast_to(jnp.where(iota((8, 1), 0) == 0, low, high), bounds.shape)
+    goals[...] = jnp.broadcast_to(jnp.where(own, -1, place), goals.shape)
+
+
+def second_call(second, relay, first, meta, held):
+    half, width = second.shape
+    half -= 16
+    cap = 4 * half
+    slots = cap // 2
+    return pl.pallas_call(
+        second_kernel,
+        grid=(1,),
+        out_shape=[
+            jax.ShapeDtypeStruct(held.shape, BF),
+            jax.ShapeDtypeStruct((slots, width), BF),
+            jax.ShapeDtypeStruct((8, 128), I32),
+            jax.ShapeDtypeStruct((cap // SLOTS, 128), I32),
+            jax.ShapeDtypeStruct((8, 128), I32),
+            jax.ShapeDtypeStruct((8, cap), I32),
+        ],
+        in_specs=[spec(pltpu.VMEM)] * 4 + [spec(pl.ANY)],
+        out_specs=[pl.BlockSpec((slots, width), lambda b: (held.shape[0] // slots - 1, 0))] + [spec(pltpu.VMEM)] * 5,
+        input_output_aliases={4: 0},
+        compiler_params=params(),
+        cost_estimate=pl.CostEstimate(flops=10**8, bytes_accessed=10**5, transcendentals=0),
+        name="second_slots",
+    )(second, relay, first, meta, held)
+
+
+def centre_kernel(here, total, labels, x, second, first, meta, known, cents, turned, shifts, one, two, again):
     rows, width = x.shape
     part = 1024
-    loads = [
-        pltpu.make_async_copy(x_hbm.at[pl.ds(k * part, part)], x.at[pl.ds(k * part, part)], sem.at[k])
-        for k in range(rows // part)
-    ]
-    for load in loads:
-        load.start()
     sums, counts = total[0:4, :], total[4:8, :]
     low = (sums[0:1] + sums[1:2]) / (counts[0:1] + counts[1:2])
     high = (sums[2:3] + sums[3:4]) / (counts[2:3] + counts[3:4])
@@ -429,124 +488,48 @@
         gaps.append(0.5 * (jnp.sum(b * b, axis=1, keepdims=True) - jnp.sum(a * a, axis=1, keepdims=True)))
         shifts[k : k + 1, :] = jnp.broadcast_to(gaps[k], (1, 128))
     shifts[2:, :] = jnp.zeros((6, 128), F32)
+    one[rows // 128 :, :] = jnp.zeros((rows // 256, 128), F32)
+    two[rows // 128 : 3 * rows // 256, :] = jnp.zeros((rows // 256, 128), F32)
     stay = labels[0:1, :] == here[0]
     keep = stay & (labels[1:2, :] == here[1])
-    for k, load in enumerate(loads):
-        load.wait()
+    for k in range(rows // part):
         lanes = slice(k * part, (k + 1) * part)
         score = scores(x[lanes, :], columns)
         put_lines(one, k * part // 128, jnp.where(stay[:, lanes], margins(score, gaps[0], 0, width), 0.0))
         put_lines(two, k * part // 128, jnp.where(keep[:, lanes], margins(score, gaps[1], 2, width), 0.0))
-
-
-def centre_call(here, total, labels, vectors):
+    score = scores(second[...], columns)
+    live = iota((1, second.shape[0]), 1) < known[0:1, 0:1]
+    put_lines(two, 3 * rows // 256, jnp.where(live, margins(score, gaps[1], 2, width), 0.0))
+    half = first.shape[0] - 16
+    both = iota((1, half), 1) < known[1:2, 0:1]
+    score = scores(first[0:half, :], columns)
+    value = split([jnp.where(both, margins(score, gaps[0], 0, width), 0.0)])
+    goal = jnp.concatenate([meta[k : k + 1, :] for k in range(half // meta.shape[1])], axis=1)
+    goal = jnp.where(both, goal, -1)
+    for k in range(4 * half // BLK):
+        got = dot_t(value, as_bf(iota((BLK, half), 0) + k * BLK == goal))
+        put_lines(again, k * BLK // 128, got[0:1] + got[1:2] + got[2:3])
+
+
+def centre_call(here, total, labels, vectors, second, first, meta, known):
     rows, width = vectors.shape
     cap = rows // 2
     return pl.pallas_call(
         centre_kernel,
-        grid=(1,),
         out_shape=[
             jax.ShapeDtypeStruct((6, width), F32),
             jax.ShapeDtypeStruct((width, 128), BF),
             jax.ShapeDtypeStruct((8, 128), F32),
             jax.ShapeDtypeStruct(((rows + cap) // 128, 128), F32),
             jax.ShapeDtypeStruct(((rows + cap + cap // 2) // 128, 128), F32),
+            jax.ShapeDtypeStruct((cap // 128, 128), F32),
         ],
-        in_specs=[spec(pltpu.SMEM), spec(pltpu.VMEM), spec(pltpu.VMEM), spec(pltpu.HBM)],
-        out_specs=[
-            pl.BlockSpec((6, width), lambda b: (0, 0)),
-            pl.BlockSpec((width, 128), lambda b: (0, 0)),
-            pl.BlockSpec((8, 128), lambda b: (0, 0)),
-            pl.BlockSpec((rows // 128, 128), lambda b: (0, 0)),
-            pl.BlockSpec((rows // 128, 128), lambda b: (0, 0)),
-        ],
-        scratch_shapes=[pltpu.VMEM((rows, width), BF), pltpu.SemaphoreType.DMA((rows // 1024,))],
+        in_specs=[spec(pltpu.SMEM)] + [spec(pltpu.VMEM)] * 7,
+        out_specs=[spec(pltpu.VMEM)] * 6,
         compiler_params=params(),
         cost_estimate=pl.CostEstimate(flops=10**8, bytes_accessed=10**5, transcendentals=0),
-        name="own_margins",
-    )(here, total, labels, vectors)
-
-
-def second_kernel(turned, shifts, second, relay, first, meta, leavers, held_in, two_in, held, two, again, alone, start, bounds, goals):
-    del held_in, two_in
-    half = second.shape[0] - 16
-    slots = held.shape[0]
-    cap = 2 * slots
-    have = count_at(second[half:, :], 5)
-    more = count_at(relay[half:, :], 4)
-    both = count_at(first[half:, :], 4)
-    lane = iota((1, half), 1)
-    goal = jnp.where(lane < more, lane + have, -1)
-    moved = dot(as_bf(iota((slots, half), 0) == goal), relay[0:half, :]).astype(BF)
-    held[0:half, :] = moved[0:half] + second[0:half, :]
-    held[half:, :] = moved[half:]
-    score = scores(held[...], turned[...])
-    width = held.shape[1]
-    live = iota((1, slots), 1) < have + more
-    put_lines(two, 0, jnp.where(live, margins(score, shifts[1:2, 0:1], 2, width), 0.0))
-
-    score = scores(first[0:half, :], turned[...])
-    value = jnp.where(lane < both, margins(score, shifts[0:1, 0:1], 0, width), 0.0)
-    high = value.astype(BF).astype(F32)
-    middle = (value - high).astype(BF).astype(F32)
-    low = value - high - middle
-    value = jnp.concatenate([high, middle, low, jnp.ones((1, half), F32), jnp.zeros((12, half), F32)], axis=0).astype(BF)
-    place = jnp.concatenate([meta[k : k + 1, :] for k in range(8)], axis=1)
-    goal = jnp.where(lane < both, place[:, :half], -1)
-    for k in range(cap // BLK):
-        hot = as_bf(iota((BLK, half), 0) + k * BLK == goal)
-        got = dot_t(value, hot)
-        put_lines(again, k * BLK // 128, got[0:1] + got[1:2] + got[2:3])
-        free = (iota((1, BLK), 1) + k * BLK < leavers[0:1, 0:1]) & (got[3:4] < 0.5)
-        put_lines(alone, k * BLK // 128, jnp.where(free, 1.0, 0.0))
-    lines = cap // SLOTS
-    lane = iota((lines, cap), 1)
-    earlier = (lane < both) | (place < SLOTS * iota((lines, cap), 0))
-    begin = jnp.sum(jnp.where(earlier, 1.0, 0.0), axis=1, keepdims=True).astype(I32)
-    begin = jnp.minimum((begin >> 7) << 7, cap - SLOTS - 128)
-    start[...] = jnp.broadcast_to(begin, start.shape)
-    lane = iota((8, cap), 1)
-    edge = 2 * SLOTS * iota((8, cap), 0)
-    before = jnp.sum(jnp.where((lane < both) | (place < edge), 1.0, 0.0), axis=1, keepdims=True)
-    until = jnp.sum(jnp.where((lane < both) | (place < edge + 2 * SLOTS), 1.0, 0.0), axis=1, keepdims=True)
-    low = jnp.sum(jnp.where(until <= half, 1.0, 0.0), axis=0, keepdims=True).astype(I32)
-    high = jnp.sum(jnp.where(before < 2 * half, 1.0, 0.0), axis=0, keepdims=True).astype(I32)
-    bounds[...] = jnp.broadcast_to(jnp.where(iota((8, 1), 0) == 0, low, high), bounds.shape)
-    goals[...] = jnp.broadcast_to(jnp.where(iota((1, cap), 1) < both, -1, place), goals.shape)
-
-
-def second_call(turned, shifts, second, relay, first, meta, leavers, held, two):
-    half, width = second.shape
-    half -= 16
-    cap = 4 * half
-    slots = cap // 2
-    return pl.pallas_call(
-        second_kernel,
-        grid=(1,),
-        out_shape=[
-            jax.ShapeDtypeStruct(held.shape, BF),
-            jax.ShapeDtypeStruct(two.shape, F32),
-            jax.ShapeDtypeStruct((cap // 128, 128), F32),
-            jax.ShapeDtypeStruct((cap // 128, 128), F32),
-            jax.ShapeDtypeStruct((cap // SLOTS, 128), I32),
-            jax.ShapeDtypeStruct((8, 128), I32),
-            jax.ShapeDtypeStruct((8, cap), I32),
-        ],
-        in_specs=[spec(pltpu.VMEM)] * 7 + [spec(pl.ANY)] * 2,
-        out_specs=[
-            pl.BlockSpec((slots, width), lambda b: (held.shape[0] // slots - 1, 0)),
-            pl.BlockSpec((slots // 128, 128), lambda b: (held.shape[0] // slots - 1, 0)),
-            pl.BlockSpec((cap // 128, 128), lambda b: (0, 0)),
-            pl.BlockSpec((cap // 128, 128), lambda b: (0, 0)),
-            pl.BlockSpec((cap // SLOTS, 128), lambda b: (0, 0)),
-            pl.BlockSpec((8, 128), lambda b: (0, 0)),
-            pl.BlockSpec((8, cap), lambda b: (0, 0)),
-        ],
-        input_output_aliases={7: 0, 8: 1},
-        compiler_params=params(),
-        cost_estimate=pl.CostEstimate(flops=10**8, bytes_accessed=10**5, transcendentals=0),
-        name="second_slots",
-    )(turned, shifts, second, relay, first, meta, leavers, held, two)
+        name="all_margins",
+    )(here, total, labels, vectors, second, first, meta, known)
 
 
 def column_kernel(own, a, b, c, out):
@@ -573,25 +556,40 @@
     )(*pieces)
 
 
-def first_kernel(late, start, bounds, turned, shifts, goals, again, alone, first, *refs):
-    middle, refs = (refs[0], refs[1:]) if late else (None, refs)
-    hands, (held_in, one_in, two_in, held, one, two, x, out, sent) = refs[:HANDS], refs[HANDS:]
+def first_kernel(late, start, bounds, turned, shifts, goals, again, first, *refs):
+    (middle, past, *refs) = refs if late else (None, None, *refs)
+    hands, refs = refs[:HANDS], refs[HANDS:]
+    held_in, one_in, two_in, held, one, two, values, x, out, sent = refs
     del held_in
     width = first.shape[1]
     part = first.shape[0] - 16
     pairs = 4 * part // (2 * SLOTS)
-    x[0:part, :] = first[0:part, :]
+
+    def weigh(begin):
+        lanes = slice(begin, begin + part)
+        score = scores(x[lanes, :], turned[...])
+        m_one = margins(score, shifts[0:1, 0:1], 0, width)
+        values[:, lanes] = split([m_one, margins(score, shifts[1:2, 0:1], 2, width)])
+
+    reach = 2 * SLOTS
+    low = part - reach if late else 0
+    x[low:part, :] = first[low:part, :]
     x[part : 2 * part, :] = middle[...] if late else jnp.zeros((part, width), BF)
     for h, hand in enumerate(hands):
-        for turn in range(hand.shape[0] // 16):
+        for turn in range(reach // 16 // HANDS if late else hand.shape[0] // 16):
             block = 2 * part + 16 * (h + HANDS * turn)
             x[block : block + 16, :] = hand[16 * turn : 16 * turn + 16, :]
     if late:
         one[...] = one_in[...]
         two[...] = two_in[...]
+        values[...] = past[...]
+        weigh(part)
     else:
         one[...] = jnp.zeros_like(one)
         two[...] = jnp.zeros_like(two)
+        values[:, part : 2 * part] = jnp.zeros((16, part), BF)
+        for k in (0, 2, 3):
+            weigh(k * part)
     span = SLOTS + 128
     base = 8 * part
     slot = iota((SLOTS, span), 0)
@@ -602,23 +600,16 @@
         return pltpu.make_async_copy(out.at[pl.ds(lines, 2 * SLOTS)], to, sent.at[pair])
 
     def place(pair, _):
-        lines = pl.multiple_of(pair * 2 * SLOTS, 2 * SLOTS)
-        rows = []
         for i in range(2):
+            lines = pl.multiple_of(pair * 2 * SLOTS + i * SLOTS, SLOTS)
             begin = pl.multiple_of((start[2 * pair + i, 0] // 128) * 128, 128)
-            hot = as_bf(slot == goals[0:1, pl.ds(begin, span)] - (lines + i * SLOTS))
-            rows.append(dot(hot, x[pl.ds(begin, span), :]).astype(BF))
-        rows = jnp.concatenate(rows, axis=0)
-        out[pl.ds(lines, 2 * SLOTS), :] = rows
+            hot = as_bf(slot == goals[0:1, pl.ds(begin, span)] - lines)
+            out[pl.ds(lines, SLOTS), :] = dot(hot, x[pl.ds(begin, span), :]).astype(BF)
+            got = dot_t(values[:, pl.ds(begin, span)], hot)
+            line = pl.ds(2 * pair + i, 1)
+            one[line, :] = got[0:1] + got[1:2] + got[2:3] + again[line, :]
+            two[line, :] = got[3:4] + got[4:5] + got[5:6]
         store(pair).start()
-        score = scores(rows, turned[...])
-        m_one = margins(score, shifts[0:1, 0:1], 0, width)
-        m_two = margins(score, shifts[1:2, 0:1], 2, width)
-        for i in range(2):
-            line = pl.ds(2 * pair + i, 1)
-            lanes = slice(SLOTS * i, SLOTS * (i + 1))
-            one[line, :] = jnp.where(alone[line, :] > 0.5, m_one[:, lanes], again[line, :])
-            two[line, :] = jnp.where(alone[line, :] > 0.5, m_two[:, lanes], 0.0)
         return 0
 
     def finish(pair, _):
@@ -633,14 +624,15 @@
             lax.fori_loop(begin, end, work, 0)
 
 
-def first_call(start, bounds, turned, shifts, goals, again, alone, first, middle, hands, held, one, two):
+def first_call(start, bounds, turned, shifts, goals, again, first, added, hands, held, one, two):
     width = held.shape[1]
     cap = goals.shape[1]
     lines = cap // 128
-    late = middle is not None
-    pieces = [first, *([middle] if late else []), *hands]
+    late = bool(added)
+    pieces = [first, *added, *hands]
     block = pl.BlockSpec((lines, 128), lambda k: (2, 0))
-    given = 7 + len(pieces)
+    given = 6 + len(pieces)
+    kept = jax.ShapeDtypeStruct((16, cap), BF)
     return pl.pallas_call(
         functools.partial(first_kernel, late),
         grid=(1,),
@@ -648,22 +640,24 @@
             jax.ShapeDtypeStruct(held.shape, BF),
             jax.ShapeDtypeStruct(one.shape, F32),
             jax.ShapeDtypeStruct(two.shape, F32),
-        ],
+        ]
+        + ([] if late else [kept]),
         in_specs=[spec(pltpu.SMEM)] * 2
         + [spec(pltpu.VMEM)] * (given - 2)
         + [spec(pl.ANY)]
         + ([block] * 2 if late else [spec(pl.ANY)] * 2),
-        out_specs=[spec(pl.ANY), block, block],
-        scratch_shapes=[
+        out_specs=[spec(pl.ANY), block, block] + ([] if late else [spec(pltpu.VMEM)]),
+        scratch_shapes=([pltpu.VMEM((16, cap), BF)] if late else [])
+        + [
             pltpu.VMEM((cap, width), BF),
             pltpu.VMEM((cap, width), BF),
             pltpu.SemaphoreType.DMA((cap // (2 * SLOTS),)),
         ],
         input_output_aliases={given: 0, given + 1: 1, given + 2: 2},
         compiler_params=params(),
-        cost_estimate=pl.CostEstimate(flops=10**9, bytes_accessed=10**6, transcendentals=0),
+        cost_estimate=pl.CostEstimate(flops=10**8, bytes_accessed=10**5, transcendentals=0),
         name="last_slots" if late else "first_slots",
-    )(start, bounds, turned, shifts, goals, again, alone, *pieces, held, one, two)
+    )(start, bounds, turned, shifts, goals, again, *pieces, held, one, two)
 
 
 def local(vectors, child_labels):
@@ -708,20 +702,27 @@
     middle, packed_in = after((middle, packed_in))
     middle_in = swap(middle, top)
     own, *hands = part_call(begins, packed_in)
-    hands = [own] + [swap(hand, h + 1) for h, hand in enumerate(hands)]
-    second_in, hands[1] = after((second_in, hands[1]))
+    held, copy, known, start, bounds, goals = second_call(second_in, relay, first_in, meta_in, held)
+    own, second_in, relay = after((own, second_in, relay))
     total = column_call(first, second_in, first_in, relay)
+    sent = [None] * (HANDS - 1)
     bit = 1
     while bit < nxt:
-        total = total + swap(total, bit)
+        if bit < HANDS:
+            ready = range(bit - 1, 2 * bit - 1)
+            total, *late = after((total + swap(total, bit), *[hands[h] for h in ready]))
+            for h, hand in zip(ready, late):
+                sent[h] = swap(hand, h + 1)
+        else:
+            total = total + swap(total, bit)
         bit *= 2
-    cents, turned, shifts, one, two = centre_call(here, total, child_labels, vectors)
-    held, two, again, alone, start, bounds, goals = second_call(
-        turned, shifts, second_in, relay, first_in, meta_in, counts[2], held, two
+    hands = [own, *sent]
+    cents, turned, shifts, one, two, again = centre_call(
+        here, total, child_labels, vectors, copy, first_in, meta_in, known
     )
-    known = start, bounds, turned, shifts, goals, again, alone, first_in
-    held, one, two = first_call(*known, None, hands, held, one, two)
-    held, one, two = first_call(*known, middle_in, hands, held, one, two)
+    told = start, bounds, turned, shifts, goals, again, first_in
+    held, one, two, values = first_call(*told, (), hands, held, one, two)
+    held, one, two = first_call(*told, (middle_in, values), hands, held, one, two)
     return held, one.reshape(-1), two.reshape(-1), cents
 
 

time: 144 us -> 154 us (1.069); the launches traced: 144 us -> 152 us
  waiting for transfers between devices: 67.5 us -> 76.4 us
  local copies, waits for them, and re-layouts: 5.37 us -> 2.62 us
    ppermute x26, waiting for transfers between devices: 67.5 us -> 76.4 us  [swap(): lax.ppermute(x, 'cube', [(i, i ^ bits) for i in range(lax.axis_size('cube...]
    unnamed x8 -> x10, local copies, waits for them, and re-layouts: 3.54 us -> 0.77 us
    pallas_call x1, Pallas kernels: 6.3 us -> 8.05 us  [centre_call(): pl.pallas_call(centre_kernel, out_shape=[jax.ShapeDtypeStruct((6, width),...]
  transfers between devices with their start and end apart: 26 -> 26, of which waited for: 8 -> 10; matrix products, arithmetic and copies ran while one was open for 1% -> 1% of each run, Pallas kernels for 21% -> 21%
where the time goes in v2:
time: 154 us; the launch traced here: 152 us
  waiting for transfers between devices  76.4 us (50%)
  Pallas kernels  37.5 us (24%)
  starting transfers between devices  33.9 us (22%)
  local copies, waits for them, and re-layouts  2.62 us (2%)
  between operations  1.65 us (1%)
    ppermute x26, waiting for transfers between devices, swap(): lax.ppermute(x, 'cube', [(i, i ^ bits) for i in range(lax.axis_size('cube...  76.4 us
    ppermute x26, starting transfers between devices, swap(): lax.ppermute(x, 'cube', [(i, i ^ bits) for i in range(lax.axis_size('cube...  33.9 us
    pallas_call x2, Pallas kernels, first_call(): pl.pallas_call(functools.partial(first_kernel, late), grid=(1,), out_shap...  9.98 us
    pallas_call x1, Pallas kernels, centre_call(): pl.pallas_call(centre_kernel, out_shape=[jax.ShapeDtypeStruct((6, width),...  8.05 us
    pallas_call x1, Pallas kernels, own_call(): pl.pallas_call(own_kernel, grid=(rows // 1024,), out_shape=jax.ShapeDtype...  4.06 us
    pallas_call x1, Pallas kernels, sort_call(): pl.pallas_call(sort_kernel, out_shape=[jax.ShapeDtypeStruct((part + 16, w...  3.81 us
    pallas_call x1, Pallas kernels, second_call(): pl.pallas_call(second_kernel, grid=(1,), out_shape=[jax.ShapeDtypeStruct(...  3.74 us
  transfers between devices with their start and end apart: 26, of which 10 were waited for; matrix products, arithmetic and copies ran while one was open for 1% of the time, Pallas kernels for 21%

profile of v2, /device:TPU:0, one launch (start us, length us, event | category | flops | bytes accessed | tf_op | source)
XLA Modules:
  0.0 152.3 jit_solution(4317070947571386631)
XLA Ops:
  2.4 5.1 %collective-permute-start.100 = (s32[8,128]{1,0:T(8,128)S(1)}, s32[8,128]{1,0:T(8,128)S(1)}, u32[]{:S(2)}, u32[]{:S(2)}) collective-permute-start(s32[8,128]{1,0:T(8,128)S(1)} %get-tuple-element.382.own), channel_id=1, source_target_pairs={{0,24},{1,25},{2,26},{3,27},{4,28},{5,29},{6,30},{7,31},{8,16},{9,... | collective-permute-start | bytes 12296 | tf_op jit(solution)/shard_map/ppermute | solution.py:20
  8.2 3.8 %sort_leavers.1 = (bf16[528,768]{1,0:T(8,128)(2,1)S(1)}, bf16[512,768]{1,0:T(8,128)(2,1)S(1)}, bf16[1024,768]{1,0:T(8,128)(2,1)S(1)}) custom-call(s32[2]{0:T(128)S(1)} %pad_add_fusion.here, s32[2,4096]{1,0:T(2,128)S(1)} %copy-done.1, s32[128,256]{1,0:T(8,128)S(1)} %get-tuple-element.394.pos_ref.pos, s32[128,128]{1,0:T(8,128)S(1)} %get-tuple-element.374.off_ref.off, ...), custom_call_target="tpu_custom_call" | custom-call | flops 8000000000 | bytes 10000000 | tf_op jit(solution)/shard_map/sort_leavers/pallas_call | solution.py:172
  12.0 2.3 %collective-permute-start.109 = (bf16[528,768]{1,0:T(8,128)(2,1)S(1)}, bf16[528,768]{1,0:T(8,128)(2,1)}, u32[]{:S(2)}, u32[]{:S(2)}) collective-permute-start(bf16[528,768]{1,0:T(8,128)(2,1)S(1)} %get-tuple-element.379.first.own), channel_id=1, source_target_pairs={{0,16},{1,17},{2,18},{3,19},{4,20},{5,21},{6,22},{7,23},{8,24},{9,... | collective-permute-start | bytes 2433032 | tf_op jit(solution)/shard_map/ppermute | solution.py:20
  14.3 1.5 second_send.1
  16.1 1.6 %collective-permute-start.103 = (bf16[144,768]{1,0:T(8,128)(2,1)S(1)}, bf16[144,768]{1,0:T(8,128)(2,1)S(1)}, u32[]{:S(2)}, u32[]{:S(2)}) collective-permute-start(bf16[144,768]{1,0:T(8,128)(2,1)S(1)} %get-tuple-element.389), channel_id=1, source_target_pairs={{0,2},{1,3},{2,0},{3,1},{4,6},{5,7},{6,4},{7,5},{8,10},{9,11},{10,... | collective-permute-start | bytes 663560 | tf_op jit(solution)/shard_map/ppermute | solution.py:20
  18.9 1.5 collective-permute-start.104
  20.9 3.5 %collective-permute-done.103.refs_2_ = bf16[144,768]{1,0:T(8,128)(2,1)S(1)} collective-permute-done((bf16[144,768]{1,0:T(8,128)(2,1)S(1)}, bf16[144,768]{1,0:T(8,128)(2,1)S(1)}, u32[]{:S(2)}, u32[]{:S(2)}) %collective-permute-start.103) | collective-permute-done | bytes 221216 | tf_op jit(solution)/shard_map/ppermute | solution.py:20
  24.7 4.6 %collective-permute-done.108.refs_7_ = bf16[144,768]{1,0:T(8,128)(2,1)S(1)} collective-permute-done((bf16[144,768]{1,0:T(8,128)(2,1)S(1)}, bf16[144,768]{1,0:T(8,128)(2,1)S(1)}, u32[]{:S(2)}, u32[]{:S(2)}) %collective-permute-start.108) | collective-permute-done | bytes 221216 | tf_op jit(solution)/shard_map/ppermute | solution.py:20
  29.2 1.5 collective-permute-start.107
  30.7 2.0 %list_ranks.1 = s32[8,256]{1,0:T(8,128)S(1)} custom-call(s32[128,128]{1,0:T(8,128)S(1)} %get-tuple-element.374.off_ref.off, s32[128,256]{1,0:T(8,128)S(1)} %get-tuple-element.394.pos_ref.pos), custom_call_target="tpu_custom_call" | custom-call | flops 100000000 | bytes 1000000 | tf_op jit(solution)/shard_map/list_ranks/pallas_call | solution.py:353
  32.7 4.1 %own_slots.1.held_in = bf16[7168,768]{1,0:T(8,128)(2,1)} custom-call(s32[128,256]{1,0:T(8,128)S(1)} %get-tuple-element.394.pos_ref.pos, bf16[4096,768]{1,0:T(8,128)(2,1)S(1)} %copy-done), custom_call_target="tpu_custom_call" | custom-call | flops 100000000 | bytes 1000000 | tf_op jit(solution)/shard_map/own_slots/pallas_call | solution.py:375
  36.8 2.0 %collective-permute-start.101 = (bf16[528,768]{1,0:T(8,128)(2,1)S(1)}, bf16[528,768]{1,0:T(8,128)(2,1)S(1)}, u32[]{:S(2)}, u32[]{:S(2)}) collective-permute-start(bf16[528,768]{1,0:T(8,128)(2,1)S(1)} %second_send.1), channel_id=1, source_target_pairs={{0,8},{1,9},{2,10},{3,11},{4,12},{5,13},{6,14},{7,15},{8,0},{9,1},... | collective-permute-start | bytes 2433032 | tf_op jit(solution)/shard_map/ppermute | solution.py:20
  38.8 2.5 %collective-permute-done.106.refs_5_ = bf16[144,768]{1,0:T(8,128)(2,1)S(1)} collective-permute-done((bf16[144,768]{1,0:T(8,128)(2,1)S(1)}, bf16[144,768]{1,0:T(8,128)(2,1)S(1)}, u32[]{:S(2)}, u32[]{:S(2)}) %collective-permute-start.106) | collective-permute-done | bytes 221216 | tf_op jit(solution)/shard_map/ppermute | solution.py:20
  42.8 7.0 %collective-permute-done.109.first.b = bf16[528,768]{1,0:T(8,128)(2,1)} collective-permute-done((bf16[528,768]{1,0:T(8,128)(2,1)S(1)}, bf16[528,768]{1,0:T(8,128)(2,1)}, u32[]{:S(2)}, u32[]{:S(2)}) %collective-permute-start.109) | collective-permute-done | bytes 811040 | tf_op jit(solution)/shard_map/ppermute | solution.py:20
  49.8 58.0 %conditional.1 = (bf16[1024,768]{1,0:T(8,128)(2,1)}, bf16[528,768]{1,0:T(8,128)(2,1)}, s32[8,256]{1,0:T(8,128)}) conditional(s32[]{:T(128)} %bitcast.2, (bf16[528,768]{1,0:T(8,128)(2,1)}, s32[8,256]{1,0:T(8,128)S(1)}) %tuple.155, (bf16[1024,768]{1,0:T(8,128)(2,1)S(1)}, bf16[528,768]{1,0:T(8,128)(2,1)}, ...), branch_computations={%region_0.1_spmd, %region_1.2_spmd, %region_2.3_spmd, %region_3.4_... | conditional | bytes 15515794 | solution.py:701
  49.9 3.7 %collective-permute-start.66 = (bf16[528,768]{1,0:T(8,128)(2,1)}, bf16[528,768]{1,0:T(8,128)(2,1)}, u32[]{:S(2)}, u32[]{:S(2)}) collective-permute-start(bf16[528,768]{1,0:T(8,128)(2,1)} %get-tuple-element.262), channel_id=1, source_target_pairs={{0,8},{1,9},{2,10},{3,11},{4,12},{5,13},{6,14},{7,15},{8,0},{9,1},... | collective-permute-start | bytes 2433032 | tf_op jit(solution)/shard_map/cond/branch_22_fun/ppermute | solution.py:20
  53.8 45.5 %collective-permute-done.65 = bf16[704,768]{1,0:T(8,128)(2,1)S(1)} collective-permute-done((bf16[704,768]{1,0:T(8,128)(2,1)S(1)}, bf16[704,768]{1,0:T(8,128)(2,1)S(1)}, u32[]{:S(2)}, u32[]{:S(2)}) %collective-permute-start.65) | collective-permute-done | bytes 1081376 | tf_op jit(solution)/shard_map/cond/branch_22_fun/ppermute | solution.py:20
  100.5 7.3 %collective-permute-done.66 = bf16[528,768]{1,0:T(8,128)(2,1)} collective-permute-done((bf16[528,768]{1,0:T(8,128)(2,1)}, bf16[528,768]{1,0:T(8,128)(2,1)}, u32[]{:S(2)}, u32[]{:S(2)}) %collective-permute-start.66) | collective-permute-done | bytes 811040 | tf_op jit(solution)/shard_map/cond/branch_22_fun/ppermute | solution.py:20
  107.8 1.3 collective-permute-start.113
  109.1 2.1 %part_pack.1 = (bf16[128,768]{1,0:T(8,128)(2,1)S(1)}, bf16[128,768]{1,0:T(8,128)(2,1)S(1)}, bf16[128,768]{1,0:T(8,128)(2,1)S(1)}, bf16[128,768]{1,0:T(8,128)(2,1...) custom-call(s32[8,128]{1,0:T(8,128)S(1)} %get-tuple-element.407.begi, ...), custom_call_target="tpu_custom_call" | custom-call | flops 20000000000 | bytes 3000000 | tf_op jit(solution)/shard_map/part_pack/pallas_call | solution.py:275
  113.3 1.5 collective-permute-start.111
  114.8 2.3 %collective-permute-done.111 = f32[8,768]{1,0:T(8,128)S(1)} collective-permute-done((f32[8,768]{1,0:T(8,128)S(1)}, f32[8,768]{1,0:T(8,128)S(1)}, u32[]{:S(2)}, u32[]{:S(2)}) %collective-permute-start.111) | collective-permute-done | bytes 24608 | tf_op jit(solution)/shard_map/ppermute | solution.py:20
  117.1 1.5 collective-permute-start.115
  118.6 1.5 %collective-permute-start.112 = (f32[8,768]{1,0:T(8,128)S(1)}, f32[8,768]{1,0:T(8,128)S(1)}, u32[]{:S(2)}, u32[]{:S(2)}) collective-permute-start(f32[8,768]{1,0:T(8,128)S(1)} %add.74), channel_id=1, source_target_pairs={{0,4},{1,5},{2,6},{3,7},{4,0},{5,1},{6,2},{7,3},{8,12},{9,13},{10,... | collective-permute-start | bytes 73736 | tf_op jit(solution)/shard_map/ppermute | solution.py:20
  120.2 2.3 %collective-permute-done.112 = f32[8,768]{1,0:T(8,128)S(1)} collective-permute-done((f32[8,768]{1,0:T(8,128)S(1)}, f32[8,768]{1,0:T(8,128)S(1)}, u32[]{:S(2)}, u32[]{:S(2)}) %collective-permute-start.112) | collective-permute-done | bytes 24608 | tf_op jit(solution)/shard_map/ppermute | solution.py:20
  122.5 1.5 %collective-permute-start.117 = (bf16[128,768]{1,0:T(8,128)(2,1)S(1)}, bf16[128,768]{1,0:T(8,128)(2,1)S(1)}, u32[]{:S(2)}, u32[]{:S(2)}) collective-permute-start(bf16[128,768]{1,0:T(8,128)(2,1)S(1)} %get-tuple-element.435), channel_id=1, source_target_pairs={{0,4},{1,5},{2,6},{3,7},{4,0},{5,1},{6,2},{7,3},{8,12},{9,13},{10,... | collective-permute-start | bytes 589832 | tf_op jit(solution)/shard_map/ppermute | solution.py:20
  124.3 3.1 %collective-permute-start.119 = (bf16[128,768]{1,0:T(8,128)(2,1)S(1)}, bf16[128,768]{1,0:T(8,128)(2,1)S(1)}, u32[]{:S(2)}, u32[]{:S(2)}) collective-permute-start(bf16[128,768]{1,0:T(8,128)(2,1)S(1)} %get-tuple-element.437), channel_id=1, source_target_pairs={{0,6},{1,7},{2,4},{3,5},{4,2},{5,3},{6,0},{7,1},{8,14},{9,15},{10,... | collective-permute-start | bytes 589832 | tf_op jit(solution)/shard_map/ppermute | solution.py:20
  127.4 2.8 %collective-permute-start.120 = (bf16[128,768]{1,0:T(8,128)(2,1)S(1)}, bf16[128,768]{1,0:T(8,128)(2,1)S(1)}, u32[]{:S(2)}, u32[]{:S(2)}) collective-permute-start(bf16[128,768]{1,0:T(8,128)(2,1)S(1)} %get-tuple-element.438), channel_id=1, source_target_pairs={{0,7},{1,6},{2,5},{3,4},{4,3},{5,2},{6,1},{7,0},{8,15},{9,14},{10,... | collective-permute-start | bytes 589832 | tf_op jit(solution)/shard_map/ppermute | solution.py:20
  130.3 3.7 %second_slots.1 = (bf16[7168,768]{1,0:T(8,128)(2,1)}, bf16[1024,768]{1,0:T(8,128)(2,1)S(1)}, s32[8,128]{1,0:T(8,128)S(1)}, s32[16,128]{1,0:T(8,128)S(1)}, s32[8,128]{1,0:T(8,128)S(1)}, /*index=5*/s32[8,2048]{1,0:T(8,128)S(1)}) custom-call(bf16[528,768]{1,0:T(8,128)(2,1)S(1)} %collective-permute-done.101.second.a, ...), custom_call_target="tpu_custom_call", output_to_operand_aliasing={{0}: (4, {})} | custom-call | flops 100000000 | bytes 100000 | tf_op jit(solution)/shard_map/second_slots/pallas_call | solution.py:451
  134.0 8.1 %all_margins.1 = (f32[6,768]{1,0:T(8,128)}, bf16[768,128]{1,0:T(8,128)(2,1)S(1)}, f32[8,128]{1,0:T(8,128)S(1)}, f32[48,128]{1,0:T(8,128)}, f32[56,128]{1,0:T(8,128)}, /*index=5*/f32[16,128]{1,0:T(8,128)S(1)}) custom-call(s32[2]{0:T(128)S(1)} %pad_add_fusion.here, f32[8,768]{1,0:T(8,128)S(1)} %add.75.total, s32[2,4096]{1,0:T(2,128)S(1)} %copy-done.2, ...), custom_call_target="tpu_custom_call" | custom-call | flops 100000000 | bytes 100000 | tf_op jit(solution)/shard_map/all_margins/pallas_call | solution.py:517
  142.1 5.5 %first_slots.1 = (bf16[7168,768]{1,0:T(8,128)(2,1)}, f32[48,128]{1,0:T(8,128)}, f32[56,128]{1,0:T(8,128)}, bf16[16,2048]{1,0:T(8,128)(2,1)S(1)}) custom-call(s32[16,128]{1,0:T(8,128)S(1)} %get-tuple-element.405.start, s32[8,128]{1,0:T(8,128)S(1)} %get-tuple-element.406.bounds, ...), custom_call_target="tpu_custom_call", output_to_operand_aliasing={{0}: (15, {}), {1}: (16, {}), {2}: (17, {})} | custom-call | flops 100000000 | bytes 100000 | tf_op jit(solution)/shard_map/first_slots/pallas_call | solution.py:636
  147.7 4.4 %last_slots.1 = (bf16[7168,768]{1,0:T(8,128)(2,1)}, f32[48,128]{1,0:T(8,128)}, f32[56,128]{1,0:T(8,128)}) custom-call(s32[16,128]{1,0:T(8,128)S(1)} %get-tuple-element.405.start, s32[8,128]{1,0:T(8,128)S(1)} %get-tuple-element.406.bounds, ...), custom_call_target="tpu_custom_call", output_to_operand_aliasing={{0}: (17, {}), {1}: (18, {}), {2}: (19, {})} | custom-call | flops 100000000 | bytes 100000 | tf_op jit(solution)/shard_map/last_slots/pallas_call | solution.py:636
  (52 shorter events, 9.5 us)
Async XLA Ops:
  0.7 0.8 copy-start.1
  1.5 6.7 %copy-start = (bf16[4096,768]{1,0:T(8,128)(2,1)S(1)}, bf16[4096,768]{1,0:T(8,128)(2,1)}, u32[]{:S(2)}) copy-start(bf16[4096,768]{1,0:T(8,128)(2,1)} %x.69) | copy-start | bytes 18874372
  2.4 9.6 %collective-permute-start.100 = (s32[8,128]{1,0:T(8,128)S(1)}, s32[8,128]{1,0:T(8,128)S(1)}, u32[]{:S(2)}, u32[]{:S(2)}) collective-permute-start(s32[8,128]{1,0:T(8,128)S(1)} %get-tuple-element.382.own), channel_id=1, source_target_pairs={{0,24},{1,25},{2,26},{3,27},{4,28},{5,29},{6,30},{7,31},{8,16},{9,... | collective-permute-start | bytes 12296 | tf_op jit(solution)/shard_map/ppermute | solution.py:20
  7.5 4.5 %collective-permute-start.99 = (s32[8,128]{1,0:T(8,128)S(1)}, s32[8,128]{1,0:T(8,128)S(1)}, u32[]{:S(2)}, u32[]{:S(2)}) collective-permute-start(s32[8,128]{1,0:T(8,128)S(1)} %get-tuple-element.382.own), channel_id=1, source_target_pairs={{0,16},{1,17},{2,18},{3,19},{4,20},{5,21},{6,22},{7,23},{8,24},{9,... | collective-permute-start | bytes 12296 | tf_op jit(solution)/shard_map/ppermute | solution.py:20
  7.5 4.5 %collective-permute-start.98 = (s32[8,128]{1,0:T(8,128)S(1)}, s32[8,128]{1,0:T(8,128)S(1)}, u32[]{:S(2)}, u32[]{:S(2)}) collective-permute-start(s32[8,128]{1,0:T(8,128)S(1)} %get-tuple-element.382.own), channel_id=1, source_target_pairs={{0,8},{1,9},{2,10},{3,11},{4,12},{5,13},{6,14},{7,15},{8,0},{9,1},... | collective-permute-start | bytes 12296 | tf_op jit(solution)/shard_map/ppermute | solution.py:20
  12.0 37.8 %collective-permute-start.109 = (bf16[528,768]{1,0:T(8,128)(2,1)S(1)}, bf16[528,768]{1,0:T(8,128)(2,1)}, u32[]{:S(2)}, u32[]{:S(2)}) collective-permute-start(bf16[528,768]{1,0:T(8,128)(2,1)S(1)} %get-tuple-element.379.first.own), channel_id=1, source_target_pairs={{0,16},{1,17},{2,18},{3,19},{4,20},{5,21},{6,22},{7,23},{8,24},{9,... | collective-permute-start | bytes 2433032 | tf_op jit(solution)/shard_map/ppermute | solution.py:20
  16.0 4.3 %collective-permute-start.102 = (bf16[144,768]{1,0:T(8,128)(2,1)S(1)}, bf16[144,768]{1,0:T(8,128)(2,1)S(1)}, u32[]{:S(2)}, u32[]{:S(2)}) collective-permute-start(bf16[144,768]{1,0:T(8,128)(2,1)S(1)} %get-tuple-element.387), channel_id=1, source_target_pairs={{0,1},{1,0},{2,3},{3,2},{4,5},{5,4},{6,7},{7,6},{8,9},{9,8},{10,11... | collective-permute-start | bytes 663560 | tf_op jit(solution)/shard_map/ppermute | solution.py:20
  16.1 8.3 %collective-permute-start.103 = (bf16[144,768]{1,0:T(8,128)(2,1)S(1)}, bf16[144,768]{1,0:T(8,128)(2,1)S(1)}, u32[]{:S(2)}, u32[]{:S(2)}) collective-permute-start(bf16[144,768]{1,0:T(8,128)(2,1)S(1)} %get-tuple-element.389), channel_id=1, source_target_pairs={{0,2},{1,3},{2,0},{3,1},{4,6},{5,7},{6,4},{7,5},{8,10},{9,11},{10,... | collective-permute-start | bytes 663560 | tf_op jit(solution)/shard_map/ppermute | solution.py:20
  17.6 11.6 %collective-permute-start.108 = (bf16[144,768]{1,0:T(8,128)(2,1)S(1)}, bf16[144,768]{1,0:T(8,128)(2,1)S(1)}, u32[]{:S(2)}, u32[]{:S(2)}) collective-permute-start(bf16[144,768]{1,0:T(8,128)(2,1)S(1)} %get-tuple-element.395), channel_id=1, source_target_pairs={{0,7},{1,6},{2,5},{3,4},{4,3},{5,2},{6,1},{7,0},{8,15},{9,14},{10,... | collective-permute-start | bytes 663560 | tf_op jit(solution)/shard_map/ppermute | solution.py:20
  18.9 17.9 %collective-permute-start.104 = (bf16[144,768]{1,0:T(8,128)(2,1)S(1)}, bf16[144,768]{1,0:T(8,128)(2,1)S(1)}, u32[]{:S(2)}, u32[]{:S(2)}) collective-permute-start(bf16[144,768]{1,0:T(8,128)(2,1)S(1)} %get-tuple-element.390), channel_id=1, source_target_pairs={{0,3},{1,2},{2,1},{3,0},{4,7},{5,6},{6,5},{7,4},{8,11},{9,10},{10,... | collective-permute-start | bytes 663560 | tf_op jit(solution)/shard_map/ppermute | solution.py:20
  20.3 18.4 %collective-permute-start.105 = (bf16[144,768]{1,0:T(8,128)(2,1)S(1)}, bf16[144,768]{1,0:T(8,128)(2,1)S(1)}, u32[]{:S(2)}, u32[]{:S(2)}) collective-permute-start(bf16[144,768]{1,0:T(8,128)(2,1)S(1)} %get-tuple-element.391), channel_id=1, source_target_pairs={{0,4},{1,5},{2,6},{3,7},{4,0},{5,1},{6,2},{7,3},{8,12},{9,13},{10,... | collective-permute-start | bytes 663560 | tf_op jit(solution)/shard_map/ppermute | solution.py:20
  24.4 16.9 %collective-permute-start.106 = (bf16[144,768]{1,0:T(8,128)(2,1)S(1)}, bf16[144,768]{1,0:T(8,128)(2,1)S(1)}, u32[]{:S(2)}, u32[]{:S(2)}) collective-permute-start(bf16[144,768]{1,0:T(8,128)(2,1)S(1)} %get-tuple-element.392), channel_id=1, source_target_pairs={{0,5},{1,4},{2,7},{3,6},{4,1},{5,0},{6,3},{7,2},{8,13},{9,12},{10,... | collective-permute-start | bytes 663560 | tf_op jit(solution)/shard_map/ppermute | solution.py:20
  29.2 12.1 %collective-permute-start.107 = (bf16[144,768]{1,0:T(8,128)(2,1)S(1)}, bf16[144,768]{1,0:T(8,128)(2,1)S(1)}, u32[]{:S(2)}, u32[]{:S(2)}) collective-permute-start(bf16[144,768]{1,0:T(8,128)(2,1)S(1)} %get-tuple-element.393), channel_id=1, source_target_pairs={{0,6},{1,7},{2,4},{3,5},{4,2},{5,3},{6,0},{7,1},{8,14},{9,15},{10,... | collective-permute-start | bytes 663560 | tf_op jit(solution)/shard_map/ppermute | solution.py:20
  36.8 74.5 %collective-permute-start.101 = (bf16[528,768]{1,0:T(8,128)(2,1)S(1)}, bf16[528,768]{1,0:T(8,128)(2,1)S(1)}, u32[]{:S(2)}, u32[]{:S(2)}) collective-permute-start(bf16[528,768]{1,0:T(8,128)(2,1)S(1)} %second_send.1), channel_id=1, source_target_pairs={{0,8},{1,9},{2,10},{3,11},{4,12},{5,13},{6,14},{7,15},{8,0},{9,1},... | collective-permute-start | bytes 2433032 | tf_op jit(solution)/shard_map/ppermute | solution.py:20
  49.9 49.4 %collective-permute-start.65 = (bf16[704,768]{1,0:T(8,128)(2,1)S(1)}, bf16[704,768]{1,0:T(8,128)(2,1)S(1)}, u32[]{:S(2)}, u32[]{:S(2)}) collective-permute-start(bf16[704,768]{1,0:T(8,128)(2,1)S(1)} %slice.85), channel_id=1, source_target_pairs={{0,16},{1,17},{2,18},{3,19},{4,20},{5,21},{6,22},{7,23},{8,24},{9,... | collective-permute-start | bytes 3244040 | tf_op jit(solution)/shard_map/cond/branch_22_fun/ppermute | solution.py:20
  49.9 57.8 %collective-permute-start.66 = (bf16[528,768]{1,0:T(8,128)(2,1)}, bf16[528,768]{1,0:T(8,128)(2,1)}, u32[]{:S(2)}, u32[]{:S(2)}) collective-permute-start(bf16[528,768]{1,0:T(8,128)(2,1)} %get-tuple-element.262), channel_id=1, source_target_pairs={{0,8},{1,9},{2,10},{3,11},{4,12},{5,13},{6,14},{7,15},{8,0},{9,1},... | collective-permute-start | bytes 2433032 | tf_op jit(solution)/shard_map/cond/branch_22_fun/ppermute | solution.py:20
  53.7 46.8 %collective-permute-start.67 = (s32[8,256]{1,0:T(8,128)S(1)}, s32[8,256]{1,0:T(8,128)}, u32[]{:S(2)}, u32[]{:S(2)}) collective-permute-start(s32[8,256]{1,0:T(8,128)S(1)} %get-tuple-element.263), channel_id=1, source_target_pairs={{0,16},{1,17},{2,18},{3,19},{4,20},{5,21},{6,22},{7,23},{8,24},{9,... | collective-permute-start | bytes 24584 | tf_op jit(solution)/shard_map/cond/branch_22_fun/ppermute | solution.py:20
  107.8 39.9 %collective-permute-start.113 = (bf16[512,768]{1,0:T(8,128)(2,1)S(1)}, bf16[512,768]{1,0:T(8,128)(2,1)S(1)}, u32[]{:S(2)}, u32[]{:S(2)}) collective-permute-start(bf16[512,768]{1,0:T(8,128)(2,1)S(1)} %get-tuple-element.430), channel_id=1, source_target_pairs={{0,16},{1,17},{2,18},{3,19},{4,20},{5,21},{6,22},{7,23},{8,24},{9,... | collective-permute-start | bytes 2359304 | tf_op jit(solution)/shard_map/ppermute | solution.py:20
  112.1 1.2 collective-permute-start.110
  113.3 3.8 %collective-permute-start.111 = (f32[8,768]{1,0:T(8,128)S(1)}, f32[8,768]{1,0:T(8,128)S(1)}, u32[]{:S(2)}, u32[]{:S(2)}) collective-permute-start(f32[8,768]{1,0:T(8,128)S(1)} %add.73), channel_id=1, source_target_pairs={{0,2},{1,3},{2,0},{3,1},{4,6},{5,7},{6,4},{7,5},{8,10},{9,11},{10,... | collective-permute-start | bytes 73736 | tf_op jit(solution)/shard_map/ppermute | solution.py:20
  114.8 9.2 %collective-permute-start.114 = (bf16[128,768]{1,0:T(8,128)(2,1)S(1)}, bf16[128,768]{1,0:T(8,128)(2,1)S(1)}, u32[]{:S(2)}, u32[]{:S(2)}) collective-permute-start(bf16[128,768]{1,0:T(8,128)(2,1)S(1)} %get-tuple-element.432), channel_id=1, source_target_pairs={{0,1},{1,0},{2,3},{3,2},{4,5},{5,4},{6,7},{7,6},{8,9},{9,8},{10,11... | collective-permute-start | bytes 589832 | tf_op jit(solution)/shard_map/ppermute | solution.py:20
  117.1 7.2 %collective-permute-start.115 = (bf16[128,768]{1,0:T(8,128)(2,1)S(1)}, bf16[128,768]{1,0:T(8,128)(2,1)S(1)}, u32[]{:S(2)}, u32[]{:S(2)}) collective-permute-start(bf16[128,768]{1,0:T(8,128)(2,1)S(1)} %get-tuple-element.433), channel_id=1, source_target_pairs={{0,2},{1,3},{2,0},{3,1},{4,6},{5,7},{6,4},{7,5},{8,10},{9,11},{10,... | collective-permute-start | bytes 589832 | tf_op jit(solution)/shard_map/ppermute | solution.py:20
  118.6 8.8 %collective-permute-start.116 = (bf16[128,768]{1,0:T(8,128)(2,1)S(1)}, bf16[128,768]{1,0:T(8,128)(2,1)S(1)}, u32[]{:S(2)}, u32[]{:S(2)}) collective-permute-start(bf16[128,768]{1,0:T(8,128)(2,1)S(1)} %get-tuple-element.434), channel_id=1, source_target_pairs={{0,3},{1,2},{2,1},{3,0},{4,7},{5,6},{6,5},{7,4},{8,11},{9,10},{10,... | collective-permute-start | bytes 589832 | tf_op jit(solution)/shard_map/ppermute | solution.py:20
  118.6 3.8 %collective-permute-start.112 = (f32[8,768]{1,0:T(8,128)S(1)}, f32[8,768]{1,0:T(8,128)S(1)}, u32[]{:S(2)}, u32[]{:S(2)}) collective-permute-start(f32[8,768]{1,0:T(8,128)S(1)} %add.74), channel_id=1, source_target_pairs={{0,4},{1,5},{2,6},{3,7},{4,0},{5,1},{6,2},{7,3},{8,12},{9,13},{10,... | collective-permute-start | bytes 73736 | tf_op jit(solution)/shard_map/ppermute | solution.py:20
  122.5 19.6 %collective-permute-start.117 = (bf16[128,768]{1,0:T(8,128)(2,1)S(1)}, bf16[128,768]{1,0:T(8,128)(2,1)S(1)}, u32[]{:S(2)}, u32[]{:S(2)}) collective-permute-start(bf16[128,768]{1,0:T(8,128)(2,1)S(1)} %get-tuple-element.435), channel_id=1, source_target_pairs={{0,4},{1,5},{2,6},{3,7},{4,0},{5,1},{6,2},{7,3},{8,12},{9,13},{10,... | collective-permute-start | bytes 589832 | tf_op jit(solution)/shard_map/ppermute | solution.py:20
  124.0 18.1 %collective-permute-start.118 = (bf16[128,768]{1,0:T(8,128)(2,1)S(1)}, bf16[128,768]{1,0:T(8,128)(2,1)S(1)}, u32[]{:S(2)}, u32[]{:S(2)}) collective-permute-start(bf16[128,768]{1,0:T(8,128)(2,1)S(1)} %get-tuple-element.436), channel_id=1, source_target_pairs={{0,5},{1,4},{2,7},{3,6},{4,1},{5,0},{6,3},{7,2},{8,13},{9,12},{10,... | collective-permute-start | bytes 589832 | tf_op jit(solution)/shard_map/ppermute | solution.py:20
  124.3 17.8 %collective-permute-start.119 = (bf16[128,768]{1,0:T(8,128)(2,1)S(1)}, bf16[128,768]{1,0:T(8,128)(2,1)S(1)}, u32[]{:S(2)}, u32[]{:S(2)}) collective-permute-start(bf16[128,768]{1,0:T(8,128)(2,1)S(1)} %get-tuple-element.437), channel_id=1, source_target_pairs={{0,6},{1,7},{2,4},{3,5},{4,2},{5,3},{6,0},{7,1},{8,14},{9,15},{10,... | collective-permute-start | bytes 589832 | tf_op jit(solution)/shard_map/ppermute | solution.py:20
  127.4 14.7 %collective-permute-start.120 = (bf16[128,768]{1,0:T(8,128)(2,1)S(1)}, bf16[128,768]{1,0:T(8,128)(2,1)S(1)}, u32[]{:S(2)}, u32[]{:S(2)}) collective-permute-start(bf16[128,768]{1,0:T(8,128)(2,1)S(1)} %get-tuple-element.438), channel_id=1, source_target_pairs={{0,7},{1,6},{2,5},{3,4},{4,3},{5,2},{6,1},{7,0},{8,15},{9,14},{10,... | collective-permute-start | bytes 589832 | tf_op jit(solution)/shard_map/ppermute | solution.py:20
  130.3 3.7 %slice-start = ((s8[6291456]{0:T(1024)(128)(4,1)}), s8[4194304]{0:T(1024)(128)(4,1)S(1)}, s32[]{:S(2)}) async-start(s8[6291456]{0:T(1024)(128)(4,1)} %bitcast.5), calls=%async_computation | async-start | bytes 8388608
  130.3 3.7 %slice-start.1 = ((s8[6291456]{0:T(1024)(128)(4,1)}), s8[2097152]{0:T(1024)(128)(4,1)S(1)}, s32[]{:S(2)}) async-start(s8[6291456]{0:T(1024)(128)(4,1)} %bitcast.5), calls=%async_computation.1 | async-start | bytes 4194304
  130.3 3.7 %copy-start.2 = (s32[2,4096]{1,0:T(2,128)S(1)}, s32[2,4096]{1,0:T(2,128)}, u32[]{:S(2)}) copy-start(s32[2,4096]{1,0:T(2,128)} %labels.5) | copy-start | bytes 98308

commit v3 on v0

--- a/solution.py
+++ b/solution.py
@@ -112,7 +112,8 @@
     )(here, labels)
 
 
-def sort_kernel(here, labels, pos_ref, off_ref, every, x, first, middle, rest, buf, sums):
+def sort_kernel(here, labels, pos_ref, off_ref, every, x, first, middle, *refs):
+    hands, (buf, sums) = refs[:HANDS], refs[HANDS:]
     rows = labels.shape[1]
     blocks = rows // BLK
     cap = rows // 2
@@ -163,7 +164,10 @@
     first[0:part, :] = buf[0:part, :]
     first[part:, :] = pack(sums[0:4, :], counts + [kinds[0], kinds[2]], x.shape[1])
     middle[...] = buf[part : 2 * part, :]
-    rest[...] = buf[2 * part : cap, :]
+    for h, hand in enumerate(hands):
+        for turn in range(hand.shape[0] // 16):
+            block = 2 * part + 16 * (h + HANDS * turn)
+            hand[16 * turn : 16 * turn + 16, :] = buf[block : block + 16, :]
 
 
 def sort_call(here, labels, pos, off, every, vectors):
@@ -174,74 +178,55 @@
         out_shape=[
             jax.ShapeDtypeStruct((part + 16, width), BF),
             jax.ShapeDtypeStruct((part, width), BF),
-            jax.ShapeDtypeStruct((2 * part, width), BF),
+            *[jax.ShapeDtypeStruct((2 * part // HANDS, width), BF)] * HANDS,
         ],
         in_specs=[spec(pltpu.SMEM)] + [spec(pltpu.VMEM)] * 5,
-        out_specs=[spec(pltpu.VMEM)] * 3,
+        out_specs=[spec(pltpu.VMEM)] * (2 + HANDS),
         scratch_shapes=[pltpu.VMEM((rows // 2 + BLK + 16, width), BF), pltpu.VMEM((8, width), F32)],
         compiler_params=params(),
-        cost_estimate=pl.CostEstimate(flops=8 * 10**9, bytes_accessed=10 * 10**6, transcendentals=0),
+        cost_estimate=pl.CostEstimate(flops=10**4, bytes_accessed=10**3, transcendentals=0),
         name="sort_leavers",
     )(here, labels, pos, off, every, vectors)
 
 
-def deal_kernel(rest, own, near, top, far, *hands):
-    rows, width = rest.shape
-    turns = rows // 16 // HANDS
-    counts = jnp.concatenate([ref[0:1, :] for ref in (own, near, top, far)], axis=1)
-    counts = jnp.concatenate([counts, jnp.zeros((1, width - 512), I32)], axis=1)
-    upper, lower = (counts >> 8).astype(F32), (counts & 255).astype(F32)
-    tail = jnp.concatenate([upper, lower, jnp.zeros((14, width), F32)], axis=0).astype(BF)
-    for h, hand in enumerate(hands):
-        for turn in range(turns):
-            block = 16 * (h + HANDS * turn)
-            hand[16 * turn : 16 * turn + 16, :] = rest[block : block + 16, :]
-        hand[16 * turns :, :] = tail
-
-
-def deal_call(rest, *counts):
-    rows, width = rest.shape
-    turns = rows // 16 // HANDS
-    return pl.pallas_call(
-        deal_kernel,
-        out_shape=[jax.ShapeDtypeStruct((16 * turns + 16, width), BF)] * HANDS,
-        in_specs=[spec(pltpu.VMEM)] * 5,
-        out_specs=[spec(pltpu.VMEM)] * HANDS,
-        compiler_params=params(),
-        cost_estimate=pl.CostEstimate(flops=0, bytes_accessed=10**5, transcendentals=0),
-        name="deal_rest",
-    )(rest, *counts)
-
-
-def pack_kernel(step, *refs):
+def pack_kernel(step, me, counts, *refs):
     hands, (out, longest, begins) = refs[:HANDS], refs[HANDS:]
-    rows = hands[0].shape[0] - 16
+    rows = hands[0].shape[0]
+    ways = counts.shape[0] // 8
+    full = (jnp.maximum(counts[...] - rows * HANDS, 0) + 15) >> 4
+    longest_pack = jnp.zeros((1, 128), I32)
+    for group in range(ways // HANDS):
+        lines = [full[8 * (group * HANDS + h) : 8 * (group * HANDS + h) + 1] for h in range(HANDS)]
+        for other in range(HANDS):
+            size = jnp.zeros((1, 128), I32)
+            for h in range(HANDS):
+                size = size + ((lines[other ^ h] + (HANDS - 1 - h)) >> 3)
+            longest_pack = jnp.maximum(longest_pack, size)
+    per = step // 16
+    longest[...] = jnp.broadcast_to(jnp.minimum(longest_pack + per - 1, out.shape[0] // 16) // per, longest.shape)
+
+    def shares(device):
+        found = []
+        for h in range(HANDS):
+            line = pl.ds(pl.multiple_of(8 * (device ^ h), 8), 8)
+            blocks = (jnp.maximum(counts[line, :][0:1] - rows * HANDS, 0) + 15) >> 4
+            found.append((blocks + (HANDS - 1 - h)) >> 3)
+        return found
+
     out[...] = jnp.zeros_like(out)
-    full = []
-    for hand in hands:
-        count = hand[rows : rows + 2, 0:512].astype(F32)
-        count = (count[0:1] * 256.0 + count[1:2]).astype(I32)
-        full.append((jnp.maximum(count - rows * HANDS, 0) + 15) >> 4)
-    place = jnp.zeros((1, 512), I32)
-    for h, hand in enumerate(hands):
+    place = jnp.zeros((1, 128), I32)
+    for h, size in enumerate(shares(me[0])):
         base = pl.multiple_of(place[0, 0] * 16, 16)
-        out[pl.ds(base, rows), :] = hand[0:rows, :]
-        begins[h : h + 1, :] = place[:, 256:384] * 16
-        place = jnp.minimum(place + ((full[h] + (HANDS - 1 - h)) >> 3), (h + 1) * (rows // 16))
-    most = jnp.zeros((1, 512), I32)
-    for other in range(HANDS):
-        size = jnp.zeros((1, 512), I32)
-        for h in range(HANDS):
-            size = size + ((full[other ^ h] + (HANDS - 1 - h)) >> 3)
-        most = jnp.maximum(most, size)
-    most = jnp.max(most.astype(F32), axis=1, keepdims=True).astype(I32)
-    per = step // 16
-    longest[...] = jnp.broadcast_to(jnp.minimum(most + per - 1, out.shape[0] // 16) // per, longest.shape)
-
-
-def pack_call(step, hands):
+        out[pl.ds(base, rows), :] = hands[h][...]
+        place = jnp.minimum(place + size, (h + 1) * (rows // 16))
+    place = jnp.zeros((1, 128), I32)
+    for h, size in enumerate(shares(me[0] ^ (ways // 2))):
+        begins[h : h + 1, :] = place * 16
+        place = jnp.minimum(place + size, (h + 1) * (rows // 16))
+
+
+def pack_call(step, me, counts, hands):
     rows, width = hands[0].shape
-    rows -= 16
     return pl.pallas_call(
         functools.partial(pack_kernel, step),
         out_shape=[
@@ -249,12 +234,12 @@
             jax.ShapeDtypeStruct((8, 128), I32),
             jax.ShapeDtypeStruct((8, 128), I32),
         ],
-        in_specs=[spec(pltpu.VMEM)] * HANDS,
+        in_specs=[spec(pltpu.SMEM)] + [spec(pltpu.VMEM)] * (HANDS + 1),
         out_specs=[spec(pltpu.VMEM)] * 3,
         compiler_params=params(),
         cost_estimate=pl.CostEstimate(flops=0, bytes_accessed=10**5, transcendentals=0),
         name="pack_hands",
-    )(*hands)
+    )(me, counts, *hands)
 
 
 def part_kernel(begins, pack_in, *refs):
@@ -322,7 +307,7 @@
         out_specs=spec(pltpu.VMEM),
         scratch_shapes=[pltpu.VMEM((half + BLK + 16, width), BF)],
         compiler_params=params(),
-        cost_estimate=pl.CostEstimate(flops=10**8, bytes_accessed=10**6, transcendentals=0),
+        cost_estimate=pl.CostEstimate(flops=10**4, bytes_accessed=10**3, transcendentals=0),
         name="second_send",
     )(off, pos, first, x)
 
@@ -357,7 +342,7 @@
         out_specs=spec(pltpu.VMEM),
         scratch_shapes=[pltpu.VMEM((8, cap + BLK + 128), F32)],
         compiler_params=params(),
-        cost_estimate=pl.CostEstimate(flops=10**8, bytes_accessed=10**6, transcendentals=0),
+        cost_estimate=pl.CostEstimate(flops=10**4, bytes_accessed=10**3, transcendentals=0),
         name="list_ranks",
     )(off, pos)
 
@@ -379,7 +364,7 @@
         in_specs=[pl.BlockSpec((8 * 1024 // BLK, BLK), lambda b: (b, 0)), spec(pltpu.VMEM)],
         out_specs=pl.BlockSpec((1024, width), lambda b: (b, 0)),
         compiler_params=params(),
-        cost_estimate=pl.CostEstimate(flops=10**8, bytes_accessed=10**6, transcendentals=0),
+        cost_estimate=pl.CostEstimate(flops=10**4, bytes_accessed=10**3, transcendentals=0),
         name="own_slots",
     )(pos, x)
 
@@ -637,26 +622,21 @@
     here = jnp.stack([(me // top) & 1, (me // nxt) & 1]).astype(I32)
     after = lax.optimization_barrier
     pos, off, every, leavers = plan_call(here, child_labels)
-    counts = [leavers] + [swap(leavers, bits) for bits in (nxt, top, top | nxt)]
-    first, middle, rest = sort_call(here, child_labels, pos, off, every, vectors)
-    first, *counts = after((first, *counts))
+    counts = lax.all_gather(leavers, "cube", axis=0, tiled=True)
+    first, middle, own, *hands = sort_call(here, child_labels, pos, off, every, vectors)
     first_in = swap(first, top)
     second = second_send_call(off, pos, first, vectors)
     second_in = swap(second, nxt)
-    rest, second = after((rest, second))
-    own, *hands = deal_call(rest, *counts)
+    own, second, *hands = after((own, second, *hands))
     hands = [own] + [swap(hand, h + 1) for h, hand in enumerate(hands)]
     after_deal, hands[1] = after((pos, hands[1]))
     meta = rank_call(off, after_deal)
     held = own_call(after_deal, vectors)
-    limit = rest.shape[0]
+    limit = 2 * middle.shape[0]
     step = limit // 32
     held, meta, hands[7] = after((held, meta, hands[7]))
-    packed, longest, begins = pack_call(step, hands)
-    bit = HANDS
-    while bit < nxt:
-        longest = jnp.maximum(longest, swap(longest, bit))
-        bit *= 2
+    partner = lax.dynamic_slice_in_dim(counts, 8 * (me ^ top), 8, 0)
+    packed, longest, begins = pack_call(step, me.astype(I32)[None], counts, hands)
 
     def cross(size):
         def branch(rows, first_in, meta):
@@ -680,7 +660,7 @@
         bit *= 2
     cents, turned, shifts, one, two = centre_call(here, total, child_labels, vectors)
     held, two, again, alone, start, goals = second_call(
-        turned, shifts, second_in, relay, first_in, meta_in, counts[2], held, two
+        turned, shifts, second_in, relay, first_in, meta_in, partner, held, two
     )
     held, one, two = first_call(
         start, turned, shifts, goals, again, alone, first_in, middle_in, hands, held, one, two

time: 140 us -> 203 us (1.45)
  blocking collectives: 0 us -> 50.6 us
  Pallas kernels: 30.8 us -> 54 us
  waiting for transfers between devices: 69.3 us -> 60.6 us
  starting transfers between devices: 33 us -> 24.6 us
  local copies, waits for them, and re-layouts: 5.37 us -> 9.72 us
    all_gather x0 -> x1, blocking collectives: none -> 50.6 us  [local(): counts = lax.all_gather(leavers, 'cube', axis=0, tiled=True)]
    pallas_call x1, Pallas kernels: 2.15 us -> 25.6 us  [part_call(): pl.pallas_call(part_kernel, out_shape=[jax.ShapeDtypeStruct((rows // HAND...]
    ppermute x26 -> x23, waiting for transfers between devices: 69.3 us -> 60.6 us  [swap(): lax.ppermute(x, 'cube', [(i, i ^ bits) for i in range(lax.axis_size('cube...]
    ppermute x26 -> x23, starting transfers between devices: 33 us -> 24.6 us  [swap(): lax.ppermute(x, 'cube', [(i, i ^ bits) for i in range(lax.axis_size('cube...]
    unnamed x8 -> x24, local copies, waits for them, and re-layouts: 3.54 us -> 7.86 us
  transfers between devices with their start and end apart: 26 -> 23, of which waited for: 11 -> 8; matrix products, arithmetic and copies ran while one was open for 1% -> 1% of each run, Pallas kernels for 17% -> 21%
where the time goes in v3:
time: 203 us; the launch traced here: 201 us
  waiting for transfers between devices  60.6 us (30%)
  Pallas kernels  54 us (27%)
  blocking collectives  50.6 us (25%)
  starting transfers between devices  24.6 us (12%)
  local copies, waits for them, and re-layouts  9.72 us (5%)
    ppermute x23, waiting for transfers between devices, swap(): lax.ppermute(x, 'cube', [(i, i ^ bits) for i in range(lax.axis_size('cube...  60.6 us
    all_gather x1, blocking collectives, local(): counts = lax.all_gather(leavers, 'cube', axis=0, tiled=True)  50.6 us
    pallas_call x1, Pallas kernels, part_call(): pl.pallas_call(part_kernel, out_shape=[jax.ShapeDtypeStruct((rows // HAND...  25.6 us
    ppermute x23, starting transfers between devices, swap(): lax.ppermute(x, 'cube', [(i, i ^ bits) for i in range(lax.axis_size('cube...  24.6 us
    unnamed x24, local copies, waits for them, and re-layouts  7.86 us
    pallas_call x1, Pallas kernels, first_call(): pl.pallas_call(first_kernel, grid=(1,), out_shape=[jax.ShapeDtypeStruct(h...  6.07 us
    pallas_call x1, Pallas kernels, centre_call(): pl.pallas_call(centre_kernel, grid=(rows // 1024,), out_shape=[jax.ShapeD...  4.61 us
    pallas_call x1, Pallas kernels, second_call(): pl.pallas_call(second_kernel, grid=(1,), out_shape=[jax.ShapeDtypeStruct(...  4.42 us
  transfers between devices with their start and end apart: 23, of which 8 were waited for; matrix products, arithmetic and copies ran while one was open for 1% of the time, Pallas kernels for 21%

profile of v3, /device:TPU:0, one launch (start us, length us, event | category | flops | bytes accessed | tf_op | source)
XLA Modules:
  0.0 201.4 jit_solution(3322365503714630109)
XLA Ops:
  0.7 0.9 copy-done.7
  1.7 0.9 plan_places.1
  2.9 0.9 slice-done.1
  3.8 3.8 %sort_leavers.1 = (bf16[528,768]{1,0:T(8,128)(2,1)S(1)}, bf16[512,768]{1,0:T(8,128)(2,1)S(1)}, bf16[128,768]{1,0:T(8,128)(2,1)S(1)}, bf16[128,768]{1,0:T(8,128)(...) custom-call(s32[2]{0:T(128)S(1)} %pad_add_fusion.here, ...), custom_call_target="tpu_custom_call" | custom-call | flops 10000 | bytes 1000 | tf_op jit(solution)/shard_map/sort_leavers/pallas_call | solution.py:176
  7.6 0.9 copy-done.9
  8.5 4.0 %collective-permute-start.106 = (bf16[528,768]{1,0:T(8,128)(2,1)S(1)}, bf16[528,768]{1,0:T(8,128)(2,1)}, u32[]{:S(2)}, u32[]{:S(2)}) collective-permute-start(bf16[528,768]{1,0:T(8,128)(2,1)S(1)} %get-tuple-element.362.first.own), channel_id=1, source_target_pairs={{0,16},{1,17},{2,18},{3,19},{4,20},{5,21},{6,22},{7,23},{8,24},{9,... | collective-permute-start | bytes 2433032 | tf_op jit(solution)/shard_map/ppermute | solution.py:20
  12.6 1.3 second_send.1
  14.0 1.5 collective-permute-start.100
  15.8 2.4 %collective-permute-start.105 = (bf16[128,768]{1,0:T(8,128)(2,1)S(1)}, bf16[128,768]{1,0:T(8,128)(2,1)S(1)}, u32[]{:S(2)}, u32[]{:S(2)}) collective-permute-start(bf16[128,768]{1,0:T(8,128)(2,1)S(1)} %get-tuple-element.381), channel_id=1, source_target_pairs={{0,7},{1,6},{2,5},{3,4},{4,3},{5,2},{6,1},{7,0},{8,15},{9,14},{10,... | collective-permute-start | bytes 589832 | tf_op jit(solution)/shard_map/ppermute | solution.py:20
  18.2 1.6 collective-permute-start.98
  19.8 1.9 collective-permute-done.100.refs_2_
  21.7 1.5 collective-permute-start.102
  23.2 1.8 collective-permute-done.101.refs_3_
  25.0 2.1 %collective-permute-start.103 = (bf16[128,768]{1,0:T(8,128)(2,1)S(1)}, bf16[128,768]{1,0:T(8,128)(2,1)S(1)}, u32[]{:S(2)}, u32[]{:S(2)}) collective-permute-start(bf16[128,768]{1,0:T(8,128)(2,1)S(1)} %get-tuple-element.378), channel_id=1, source_target_pairs={{0,5},{1,4},{2,7},{3,6},{4,1},{5,0},{6,3},{7,2},{8,13},{9,12},{10,... | collective-permute-start | bytes 589832 | tf_op jit(solution)/shard_map/ppermute | solution.py:20
  27.2 3.1 %collective-permute-done.105.refs_7_ = bf16[128,768]{1,0:T(8,128)(2,1)S(1)} collective-permute-done((bf16[128,768]{1,0:T(8,128)(2,1)S(1)}, bf16[128,768]{1,0:T(8,128)(2,1)S(1)}, u32[]{:S(2)}, u32[]{:S(2)}) %collective-permute-start.105) | collective-permute-done | bytes 196640 | tf_op jit(solution)/shard_map/ppermute | solution.py:20
  30.3 1.4 collective-permute-start.104
  31.7 50.6 %all_gather.3.counts = s32[256,128]{1,0:T(8,128)S(1)} all-gather(s32[8,128]{1,0:T(8,128)S(1)} %get-tuple-element.363), channel_id=1, replica_groups=mesh['cube'=32] {'cube'}, dimensions={0}, use_global_device_ids=true | all-gather | bytes 135168 | tf_op jit(solution)/shard_map/all_gather | solution.py:625
  82.3 2.0 list_ranks.1
  84.3 4.1 %own_slots.1.held_in = bf16[7168,768]{1,0:T(8,128)(2,1)} custom-call(s32[128,256]{1,0:T(8,128)S(1)} %get-tuple-element.380.pos_ref.pos, bf16[4096,768]{1,0:T(8,128)(2,1)S(1)} %bitcast.7), custom_call_target="tpu_custom_call" | custom-call | flops 10000 | bytes 1000 | tf_op jit(solution)/shard_map/own_slots/pallas_call | solution.py:360
  89.9 48.8 %conditional.1 = (bf16[1024,768]{1,0:T(8,128)(2,1)}, bf16[528,768]{1,0:T(8,128)(2,1)}, s32[8,256]{1,0:T(8,128)}) conditional(s32[]{:T(128)} %bitcast.3, (bf16[528,768]{1,0:T(8,128)(2,1)}, s32[8,256]{1,0:T(8,128)S(1)}) %tuple.150, (bf16[1024,768]{1,0:T(8,128)(2,1)S(1)}, bf16[528,768]{1,0:T(8,128)(2,1)}, ...), branch_computations={%region_0.1_spmd, %region_1.2_spmd, %region_2.3_spmd, %region_3.4_... | conditional | bytes 15515794 | solution.py:650
  90.2 2.8 %collective-permute-start.64 = (s32[8,256]{1,0:T(8,128)S(1)}, s32[8,256]{1,0:T(8,128)}, u32[]{:S(2)}, u32[]{:S(2)}) collective-permute-start(s32[8,256]{1,0:T(8,128)S(1)} %get-tuple-element.260), channel_id=1, source_target_pairs={{0,16},{1,17},{2,18},{3,19},{4,20},{5,21},{6,22},{7,23},{8,24},{9,... | collective-permute-start | bytes 24584 | tf_op jit(solution)/shard_map/cond/branch_21_fun/ppermute | solution.py:20
  93.1 44.4 %collective-permute-done.62 = bf16[672,768]{1,0:T(8,128)(2,1)S(1)} collective-permute-done((bf16[672,768]{1,0:T(8,128)(2,1)S(1)}, bf16[672,768]{1,0:T(8,128)(2,1)S(1)}, u32[]{:S(2)}, u32[]{:S(2)}) %collective-permute-start.62) | collective-permute-done | bytes 1032224 | tf_op jit(solution)/shard_map/cond/branch_21_fun/ppermute | solution.py:20
  137.4 1.3 pad.113
  138.7 25.6 %part_pack.1 = (bf16[128,768]{1,0:T(8,128)(2,1)S(1)}, bf16[128,768]{1,0:T(8,128)(2,1)S(1)}, bf16[128,768]{1,0:T(8,128)(2,1)S(1)}, bf16[128,768]{1,0:T(8,128)(2,1...) custom-call(s32[8,128]{1,0:T(8,128)S(1)} %get-tuple-element.383.begi, ...), custom_call_target="tpu_custom_call" | custom-call | bytes 3000000 | tf_op jit(solution)/shard_map/part_pack/pallas_call | solution.py:260
  164.5 1.8 collective-permute-start.113
  169.4 7.1 %collective-permute-done.109 = f32[8,768]{1,0:T(8,128)S(1)} collective-permute-done((f32[8,768]{1,0:T(8,128)S(1)}, f32[8,768]{1,0:T(8,128)S(1)}, u32[]{:S(2)}, u32[]{:S(2)}) %collective-permute-start.109) | collective-permute-done | bytes 24608 | tf_op jit(solution)/shard_map/ppermute | solution.py:20
  176.5 2.0 %collective-permute-start.114 = (bf16[128,768]{1,0:T(8,128)(2,1)}, bf16[128,768]{1,0:T(8,128)(2,1)S(1)}, u32[]{:S(2)}, u32[]{:S(2)}) collective-permute-start(bf16[128,768]{1,0:T(8,128)(2,1)} %get-tuple-element.409), channel_id=1, source_target_pairs={{0,4},{1,5},{2,6},{3,7},{4,0},{5,1},{6,2},{7,3},{8,12},{9,13},{10,... | collective-permute-start | bytes 589832 | tf_op jit(solution)/shard_map/ppermute | solution.py:20
  180.7 1.7 collective-permute-start.117
  182.4 2.8 %copy-done = bf16[4096,768]{1,0:T(8,128)(2,1)S(1)} copy-done((bf16[4096,768]{1,0:T(8,128)(2,1)S(1)}, bf16[4096,768]{1,0:T(8,128)(2,1)}, u32[]{:S(2)}) %copy-start) | copy-done | bytes 6291480
  185.2 4.6 %own_margins.1 = (f32[6,768]{1,0:T(8,128)}, bf16[768,128]{1,0:T(8,128)(2,1)S(1)}, f32[8,128]{1,0:T(8,128)S(1)}, f32[48,128]{1,0:T(8,128)}, f32[56,128]{1,0:T(8,128)}) custom-call(s32[2]{0:T(128)S(1)} %pad_add_fusion.here, f32[8,768]{1,0:T(8,128)S(1)} %add.78.total, s32[2,4096]{1,0:T(2,128)S(1)} %copy-done.8, bf16[4096,768]{1,0:T(8,128)(2,1)S(1)} %copy-done), custom_call_target="tpu_custom_call" | custom-call | flops 100000000 | bytes 100000 | tf_op jit(solution)/shard_map/own_margins/pallas_call | solution.py:423
  189.8 4.4 %second_slots.1 = (bf16[7168,768]{1,0:T(8,128)(2,1)}, f32[56,128]{1,0:T(8,128)}, f32[16,128]{1,0:T(8,128)S(1)}, f32[16,128]{1,0:T(8,128)S(1)}, s32[16,128]{1,0:T(8,128)S(1)}, /*index=5*/s32[8,2048]{1,0:T(8,128)S(1)}) custom-call(bf16[768,128]{1,0:T(8,128)(2,1)S(1)} %get-tuple-element.395.turned, ...), custom_call_target="tpu_custom_call", output_to_operand_aliasing={{0}: (7, {}), {1}: (8, {})} | custom-call | flops 100000000 | bytes 100000 | tf_op jit(solution)/shard_map/second_slots/pallas_call | solution.py:498
  195.2 6.1 %first_slots.1 = (bf16[7168,768]{1,0:T(8,128)(2,1)}, f32[48,128]{1,0:T(8,128)}, f32[56,128]{1,0:T(8,128)}) custom-call(s32[16,128]{1,0:T(8,128)S(1)} %get-tuple-element.400.start, bf16[768,128]{1,0:T(8,128)(2,1)S(1)} %get-tuple-element.395.turned, ...), custom_call_target="tpu_custom_call", output_to_operand_aliasing={{0}: (16, {}), {1}: (17, {}), {2}: (18, {})} | custom-call | flops 3000000000 | bytes 7000000 | tf_op jit(solution)/shard_map/first_slots/pallas_call | solution.py:591
  (60 shorter events, 8.1 us)
Async XLA Ops:
  0.7 2.2 %slice-start = ((s8[6291456]{0:T(1024)(128)(4,1)}), s8[4194304]{0:T(1024)(128)(4,1)S(1)}, s32[]{:S(2)}) async-start(s8[6291456]{0:T(1024)(128)(4,1)} %bitcast.6), calls=%async_computation | async-start | bytes 8388608
  0.7 0.9 copy-start.7
  1.7 2.1 %slice-start.1 = ((s8[6291456]{0:T(1024)(128)(4,1)}), s8[2097152]{0:T(1024)(128)(4,1)S(1)}, s32[]{:S(2)}) async-start(s8[6291456]{0:T(1024)(128)(4,1)} %bitcast.6), calls=%async_computation.1 | async-start | bytes 4194304
  7.6 0.9 copy-start.9
  8.5 81.4 %collective-permute-start.106 = (bf16[528,768]{1,0:T(8,128)(2,1)S(1)}, bf16[528,768]{1,0:T(8,128)(2,1)}, u32[]{:S(2)}, u32[]{:S(2)}) collective-permute-start(bf16[528,768]{1,0:T(8,128)(2,1)S(1)} %get-tuple-element.362.first.own), channel_id=1, source_target_pairs={{0,16},{1,17},{2,18},{3,19},{4,20},{5,21},{6,22},{7,23},{8,24},{9,... | collective-permute-start | bytes 2433032 | tf_op jit(solution)/shard_map/ppermute | solution.py:20
  13.9 4.3 %collective-permute-start.99 = (bf16[128,768]{1,0:T(8,128)(2,1)S(1)}, bf16[128,768]{1,0:T(8,128)(2,1)S(1)}, u32[]{:S(2)}, u32[]{:S(2)}) collective-permute-start(bf16[128,768]{1,0:T(8,128)(2,1)S(1)} %get-tuple-element.373), channel_id=1, source_target_pairs={{0,1},{1,0},{2,3},{3,2},{4,5},{5,4},{6,7},{7,6},{8,9},{9,8},{10,11... | collective-permute-start | bytes 589832 | tf_op jit(solution)/shard_map/ppermute | solution.py:20
  14.0 7.8 %collective-permute-start.100 = (bf16[128,768]{1,0:T(8,128)(2,1)S(1)}, bf16[128,768]{1,0:T(8,128)(2,1)S(1)}, u32[]{:S(2)}, u32[]{:S(2)}) collective-permute-start(bf16[128,768]{1,0:T(8,128)(2,1)S(1)} %get-tuple-element.375), channel_id=1, source_target_pairs={{0,2},{1,3},{2,0},{3,1},{4,6},{5,7},{6,4},{7,5},{8,10},{9,11},{10,... | collective-permute-start | bytes 589832 | tf_op jit(solution)/shard_map/ppermute | solution.py:20
  15.5 9.6 %collective-permute-start.101 = (bf16[128,768]{1,0:T(8,128)(2,1)S(1)}, bf16[128,768]{1,0:T(8,128)(2,1)S(1)}, u32[]{:S(2)}, u32[]{:S(2)}) collective-permute-start(bf16[128,768]{1,0:T(8,128)(2,1)S(1)} %get-tuple-element.376), channel_id=1, source_target_pairs={{0,3},{1,2},{2,1},{3,0},{4,7},{5,6},{6,5},{7,4},{8,11},{9,10},{10,... | collective-permute-start | bytes 589832 | tf_op jit(solution)/shard_map/ppermute | solution.py:20
  15.8 14.5 %collective-permute-start.105 = (bf16[128,768]{1,0:T(8,128)(2,1)S(1)}, bf16[128,768]{1,0:T(8,128)(2,1)S(1)}, u32[]{:S(2)}, u32[]{:S(2)}) collective-permute-start(bf16[128,768]{1,0:T(8,128)(2,1)S(1)} %get-tuple-element.381), channel_id=1, source_target_pairs={{0,7},{1,6},{2,5},{3,4},{4,3},{5,2},{6,1},{7,0},{8,15},{9,14},{10,... | collective-permute-start | bytes 589832 | tf_op jit(solution)/shard_map/ppermute | solution.py:20
  18.2 148.1 %collective-permute-start.98 = (bf16[528,768]{1,0:T(8,128)(2,1)S(1)}, bf16[528,768]{1,0:T(8,128)(2,1)S(1)}, u32[]{:S(2)}, u32[]{:S(2)}) collective-permute-start(bf16[528,768]{1,0:T(8,128)(2,1)S(1)} %second_send.1), channel_id=1, source_target_pairs={{0,8},{1,9},{2,10},{3,11},{4,12},{5,13},{6,14},{7,15},{8,0},{9,1},... | collective-permute-start | bytes 2433032 | tf_op jit(solution)/shard_map/ppermute | solution.py:20
  21.7 66.6 %collective-permute-start.102 = (bf16[128,768]{1,0:T(8,128)(2,1)S(1)}, bf16[128,768]{1,0:T(8,128)(2,1)S(1)}, u32[]{:S(2)}, u32[]{:S(2)}) collective-permute-start(bf16[128,768]{1,0:T(8,128)(2,1)S(1)} %get-tuple-element.377), channel_id=1, source_target_pairs={{0,4},{1,5},{2,6},{3,7},{4,0},{5,1},{6,2},{7,3},{8,12},{9,13},{10,... | collective-permute-start | bytes 589832 | tf_op jit(solution)/shard_map/ppermute | solution.py:20
  25.0 63.3 %collective-permute-start.103 = (bf16[128,768]{1,0:T(8,128)(2,1)S(1)}, bf16[128,768]{1,0:T(8,128)(2,1)S(1)}, u32[]{:S(2)}, u32[]{:S(2)}) collective-permute-start(bf16[128,768]{1,0:T(8,128)(2,1)S(1)} %get-tuple-element.378), channel_id=1, source_target_pairs={{0,5},{1,4},{2,7},{3,6},{4,1},{5,0},{6,3},{7,2},{8,13},{9,12},{10,... | collective-permute-start | bytes 589832 | tf_op jit(solution)/shard_map/ppermute | solution.py:20
  30.3 58.1 %collective-permute-start.104 = (bf16[128,768]{1,0:T(8,128)(2,1)S(1)}, bf16[128,768]{1,0:T(8,128)(2,1)S(1)}, u32[]{:S(2)}, u32[]{:S(2)}) collective-permute-start(bf16[128,768]{1,0:T(8,128)(2,1)S(1)} %get-tuple-element.379), channel_id=1, source_target_pairs={{0,6},{1,7},{2,4},{3,5},{4,2},{5,3},{6,0},{7,1},{8,14},{9,15},{10,... | collective-permute-start | bytes 589832 | tf_op jit(solution)/shard_map/ppermute | solution.py:20
  90.1 47.4 %collective-permute-start.62 = (bf16[672,768]{1,0:T(8,128)(2,1)S(1)}, bf16[672,768]{1,0:T(8,128)(2,1)S(1)}, u32[]{:S(2)}, u32[]{:S(2)}) collective-permute-start(bf16[672,768]{1,0:T(8,128)(2,1)S(1)} %slice.84), channel_id=1, source_target_pairs={{0,16},{1,17},{2,18},{3,19},{4,20},{5,21},{6,22},{7,23},{8,24},{9,... | collective-permute-start | bytes 3096584 | tf_op jit(solution)/shard_map/cond/branch_21_fun/ppermute | solution.py:20
  90.1 48.6 %collective-permute-start.63 = (bf16[528,768]{1,0:T(8,128)(2,1)}, bf16[528,768]{1,0:T(8,128)(2,1)}, u32[]{:S(2)}, u32[]{:S(2)}) collective-permute-start(bf16[528,768]{1,0:T(8,128)(2,1)} %get-tuple-element.259), channel_id=1, source_target_pairs={{0,8},{1,9},{2,10},{3,11},{4,12},{5,13},{6,14},{7,15},{8,0},{9,1},... | collective-permute-start | bytes 2433032 | tf_op jit(solution)/shard_map/cond/branch_21_fun/ppermute | solution.py:20
  90.2 48.5 %collective-permute-start.64 = (s32[8,256]{1,0:T(8,128)S(1)}, s32[8,256]{1,0:T(8,128)}, u32[]{:S(2)}, u32[]{:S(2)}) collective-permute-start(s32[8,256]{1,0:T(8,128)S(1)} %get-tuple-element.260), channel_id=1, source_target_pairs={{0,16},{1,17},{2,18},{3,19},{4,20},{5,21},{6,22},{7,23},{8,24},{9,... | collective-permute-start | bytes 24584 | tf_op jit(solution)/shard_map/cond/branch_21_fun/ppermute | solution.py:20
  138.7 56.4 %collective-permute-start.111 = (bf16[512,768]{1,0:T(8,128)(2,1)}, bf16[512,768]{1,0:T(8,128)(2,1)S(1)}, u32[]{:S(2)}, u32[]{:S(2)}) collective-permute-start(bf16[512,768]{1,0:T(8,128)(2,1)} %copy-done.9), channel_id=1, source_target_pairs={{0,16},{1,17},{2,18},{3,19},{4,20},{5,21},{6,22},{7,23},{8,24},{9,... | collective-permute-start | bytes 2359304 | tf_op jit(solution)/shard_map/ppermute | solution.py:20
  164.4 1.9 collective-permute-start.107
  164.5 14.1 %collective-permute-start.112 = (bf16[128,768]{1,0:T(8,128)(2,1)S(1)}, bf16[128,768]{1,0:T(8,128)(2,1)S(1)}, u32[]{:S(2)}, u32[]{:S(2)}) collective-permute-start(bf16[128,768]{1,0:T(8,128)(2,1)S(1)} %get-tuple-element.407), channel_id=1, source_target_pairs={{0,2},{1,3},{2,0},{3,1},{4,6},{5,7},{6,4},{7,5},{8,10},{9,11},{10,... | collective-permute-start | bytes 589832 | tf_op jit(solution)/shard_map/ppermute | solution.py:20
  164.5 14.7 %collective-permute-start.113 = (bf16[128,768]{1,0:T(8,128)(2,1)S(1)}, bf16[128,768]{1,0:T(8,128)(2,1)S(1)}, u32[]{:S(2)}, u32[]{:S(2)}) collective-permute-start(bf16[128,768]{1,0:T(8,128)(2,1)S(1)} %get-tuple-element.408), channel_id=1, source_target_pairs={{0,3},{1,2},{2,1},{3,0},{4,7},{5,6},{6,5},{7,4},{8,11},{9,10},{10,... | collective-permute-start | bytes 589832 | tf_op jit(solution)/shard_map/ppermute | solution.py:20
  167.0 15.4 %copy-start.8 = (s32[2,4096]{1,0:T(2,128)S(1)}, s32[2,4096]{1,0:T(2,128)}, u32[]{:S(2)}) copy-start(s32[2,4096]{1,0:T(2,128)} %labels.5) | copy-start | bytes 98308
  167.9 1.2 collective-permute-start.108
  169.1 7.4 %collective-permute-start.109 = (f32[8,768]{1,0:T(8,128)S(1)}, f32[8,768]{1,0:T(8,128)S(1)}, u32[]{:S(2)}, u32[]{:S(2)}) collective-permute-start(f32[8,768]{1,0:T(8,128)S(1)} %add.76), channel_id=1, source_target_pairs={{0,2},{1,3},{2,0},{3,1},{4,6},{5,7},{6,4},{7,5},{8,10},{9,11},{10,... | collective-permute-start | bytes 73736 | tf_op jit(solution)/shard_map/ppermute | solution.py:20
  176.5 4.1 %collective-permute-start.110 = (f32[8,768]{1,0:T(8,128)S(1)}, f32[8,768]{1,0:T(8,128)S(1)}, u32[]{:S(2)}, u32[]{:S(2)}) collective-permute-start(f32[8,768]{1,0:T(8,128)S(1)} %add.77), channel_id=1, source_target_pairs={{0,4},{1,5},{2,6},{3,7},{4,0},{5,1},{6,2},{7,3},{8,12},{9,13},{10,... | collective-permute-start | bytes 73736 | tf_op jit(solution)/shard_map/ppermute | solution.py:20
  176.5 17.7 %collective-permute-start.114 = (bf16[128,768]{1,0:T(8,128)(2,1)}, bf16[128,768]{1,0:T(8,128)(2,1)S(1)}, u32[]{:S(2)}, u32[]{:S(2)}) collective-permute-start(bf16[128,768]{1,0:T(8,128)(2,1)} %get-tuple-element.409), channel_id=1, source_target_pairs={{0,4},{1,5},{2,6},{3,7},{4,0},{5,1},{6,2},{7,3},{8,12},{9,13},{10,... | collective-permute-start | bytes 589832 | tf_op jit(solution)/shard_map/ppermute | solution.py:20
  179.2 15.9 %collective-permute-start.115 = (bf16[128,768]{1,0:T(8,128)(2,1)}, bf16[128,768]{1,0:T(8,128)(2,1)S(1)}, u32[]{:S(2)}, u32[]{:S(2)}) collective-permute-start(bf16[128,768]{1,0:T(8,128)(2,1)} %get-tuple-element.410), channel_id=1, source_target_pairs={{0,5},{1,4},{2,7},{3,6},{4,1},{5,0},{6,3},{7,2},{8,13},{9,12},{10,... | collective-permute-start | bytes 589832 | tf_op jit(solution)/shard_map/ppermute | solution.py:20
  179.9 15.2 %collective-permute-start.116 = (bf16[128,768]{1,0:T(8,128)(2,1)}, bf16[128,768]{1,0:T(8,128)(2,1)S(1)}, u32[]{:S(2)}, u32[]{:S(2)}) collective-permute-start(bf16[128,768]{1,0:T(8,128)(2,1)} %get-tuple-element.411), channel_id=1, source_target_pairs={{0,6},{1,7},{2,4},{3,5},{4,2},{5,3},{6,0},{7,1},{8,14},{9,15},{10,... | collective-permute-start | bytes 589832 | tf_op jit(solution)/shard_map/ppermute | solution.py:20
  180.7 14.5 %collective-permute-start.117 = (bf16[128,768]{1,0:T(8,128)(2,1)}, bf16[128,768]{1,0:T(8,128)(2,1)S(1)}, u32[]{:S(2)}, u32[]{:S(2)}) collective-permute-start(bf16[128,768]{1,0:T(8,128)(2,1)} %get-tuple-element.412), channel_id=1, source_target_pairs={{0,7},{1,6},{2,5},{3,4},{4,3},{5,2},{6,1},{7,0},{8,15},{9,14},{10,... | collective-permute-start | bytes 589832 | tf_op jit(solution)/shard_map/ppermute | solution.py:20
  182.4 2.8 %copy-start = (bf16[4096,768]{1,0:T(8,128)(2,1)S(1)}, bf16[4096,768]{1,0:T(8,128)(2,1)}, u32[]{:S(2)}) copy-start(bf16[4096,768]{1,0:T(8,128)(2,1)} %x_ref.1) | copy-start | bytes 18874372
  189.8 5.4 %copy-start.2 = (bf16[128,768]{1,0:T(8,128)(2,1)S(1)}, bf16[128,768]{1,0:T(8,128)(2,1)}, u32[]{:S(2)}) copy-start(bf16[128,768]{1,0:T(8,128)(2,1)} %copy-done.1) | copy-start | bytes 589828
  189.8 5.4 %copy-start.4 = (bf16[128,768]{1,0:T(8,128)(2,1)S(1)}, bf16[128,768]{1,0:T(8,128)(2,1)}, u32[]{:S(2)}) copy-start(bf16[128,768]{1,0:T(8,128)(2,1)} %copy-done.3) | copy-start | bytes 589828
  189.8 5.4 %copy-start.6 = (bf16[128,768]{1,0:T(8,128)(2,1)S(1)}, bf16[128,768]{1,0:T(8,128)(2,1)}, u32[]{:S(2)}) copy-start(bf16[128,768]{1,0:T(8,128)(2,1)} %copy-done.5) | copy-start | bytes 589828
  (3 other events, 2.0 us)
